TPU v7x, 32 devices: a whole 2x2x4 slice. The times are simulated.
32 devices in a mesh: groups: 2 (over y), gz: 4 (over z), ta: 2 (over x), col: 2 (over core).
Axes of the slice: x: 2, y: 2, z: 4, core: 2. Of those that a mesh axis runs over, the one named last changes fastest.
Arguments:
- field: bfloat16 [64, 24, 20, 64, 128], P(('groups', 'gz'), 'ta', None, 'col'), parts along dimension 0, may hold values from -6 to 6
- cotangent: bfloat16 [64, 24, 20, 64, 128], P(('groups', 'gz'), 'ta', None, 'col'), parts along dimension 0, may hold values from -6 to 6
- spectral_weight: bfloat16 [16, 12, 576, 2, 20, 20], P('ta', None, ('gz', 'col')), may hold values from -4.1875 to 4.1875
- point_weight: bfloat16 [20, 20], replicated, may hold values from -1.25 to 1.25
- point_bias: float32 [20], replicated, may hold values from -3 to 3
Outputs:
- input_grad: bfloat16 [64, 24, 20, 64, 128], P(('groups', 'gz'), 'ta', None, 'col'), parts along dimension 0
- weight_grad: bfloat16 [32, 12, 576, 2, 20, 20], P(('groups', 'ta'), None, ('gz', 'col')), parts along dimension 0
There are 2 independent parts, one for each index of `groups`. A program takes and returns all parts, laid end to end along the dimension named above; an argument that names none is the same for every part. Nothing has to cross between parts.
All inputs are finite; a program needn't handle non-finite values.
Results may differ from a plain program's by a relative error of at most 0.025.
Values may be sent and summed in bfloat16 or wider, within the bound.
No kernel may reach another device: no remote copies, remote signals or barrier semaphores. Data moves between devices by JAX's collectives and lax.ppermute only.
A program may use at most 384 MiB of HBM per device.

v0:
```python
import math

import jax
import jax.numpy as jnp
from jax import lax
from jax.sharding import PartitionSpec as P

LX = 128
LY = 64
LZ = 32
LT = 24
WIDTH = 20
MX = 24
MY = 24
MZ = 16
MT = 12
PAIRS = 576


def wave_parts(length, mode_count, halfband):
    mode_index = jnp.arange(mode_count, dtype=jnp.int32)
    if halfband:
        frequency = mode_index
    else:
        frequency = jnp.where(mode_index < mode_count // 2, mode_index, mode_index - mode_count)
    places = jnp.arange(length, dtype=jnp.int32)
    phase_turns = places[:, None] * frequency[None, :] % length
    angles = phase_turns.astype(jnp.float32) * (2.0 * math.pi / length)
    scaling = 1.0 / math.sqrt(length)
    return (jnp.cos(angles) * scaling, jnp.sin(angles) * scaling)


def complex_table(length, mode_count, halfband, doubled, inverse):
    cosine, sine_part = wave_parts(length, mode_count, halfband)
    if doubled:
        factor = jnp.where(jnp.arange(mode_count) == 0, 1.0, 2.0).astype(jnp.float32)
        cosine = cosine * factor[None, :]
        sine_part = sine_part * factor[None, :]
    if inverse:
        table_out = jnp.stack(
            [jnp.stack([cosine, sine_part], -1), jnp.stack([-sine_part, cosine], -1)], 2
        )
        return jnp.transpose(table_out, (1, 0, 2, 3)).astype(jnp.bfloat16)
    table_out = jnp.stack(
        [jnp.stack([cosine, -sine_part], -1), jnp.stack([sine_part, cosine], -1)], 2
    )
    return table_out.astype(jnp.bfloat16)


def real_tables(length, mode_count):
    cosine, sine_part = wave_parts(length, mode_count, False)
    forward = jnp.stack([cosine, -sine_part], 0).astype(jnp.bfloat16)
    x_forward = jnp.transpose(forward, (1, 0, 2)).reshape(length, 2 * mode_count)
    x_inverse = jnp.transpose(forward, (0, 2, 1)).reshape(2 * mode_count, length)
    return (x_forward, x_inverse)


def product(pattern, first_op, second_op):
    return jnp.einsum(pattern, first_op, second_op, preferred_element_type=jnp.float32)


def gelu_slope(values):
    normal_cdf = 0.5 * (1.0 + lax.erf(values / math.sqrt(2.0)))
    return normal_cdf + values * jnp.exp(-0.5 * values * values) / math.sqrt(2.0 * math.pi)


def per_device(field, cotangent, spectral_weight, point_weight, point_bias):
    col_index = lax.axis_index("col")
    gz_count = lax.axis_size("gz")
    col_count = lax.axis_size("col")
    depth = field.shape[0]
    steps_here = field.shape[1]
    row_count = field.shape[3]
    owners = gz_count * col_count
    owned_pairs = PAIRS // owners
    x_fwd, x_inv = real_tables(LX, MX)
    y_fwd = lax.dynamic_slice_in_dim(
        complex_table(LY, MY, False, False, False), col_index * row_count, row_count, 0
    )
    y_inv = lax.dynamic_slice_in_dim(
        complex_table(LY, MY, False, False, True), col_index * row_count, row_count, 1
    )
    z_fwd = complex_table(LZ, MZ, False, False, False)
    z_inv = complex_table(LZ, MZ, False, False, True)
    t_plain_fwd = complex_table(LT, MT, True, False, False)
    t_weighted_fwd = complex_table(LT, MT, True, True, False)
    t_plain_inv = complex_table(LT, MT, True, False, True)
    t_weighted_inv = complex_table(LT, MT, True, True, True)

    def analyse(field_in, t_table):
        along_x = product("ztcyx,xj->ztcyj", field_in, x_fwd).astype(jnp.bfloat16)
        along_x = along_x.reshape(depth, steps_here, WIDTH, row_count, 2, MX)
        partial_sums = product("ztcyrk,ybrs->ztcsbk", along_x, y_fwd)
        spread = partial_sums.reshape(depth, steps_here, WIDTH, 2, gz_count, col_count, owned_pairs)
        halves = lax.psum_scatter(
            spread.astype(jnp.bfloat16), "col", scatter_dimension=5, tiled=True
        )
        mine = halves.reshape(depth, steps_here, WIDTH, 2, gz_count, owned_pairs)
        moved = lax.all_to_all(mine, "gz", split_axis=4, concat_axis=0, tiled=True)
        owned = moved.reshape(LZ, steps_here, WIDTH, 2, owned_pairs)
        along_z = product("ztcrm,zkrs->ktcsm", owned, z_fwd).astype(jnp.bfloat16)
        full_time = lax.all_to_all(along_z, "ta", split_axis=0, concat_axis=1, tiled=True)
        return product("ktcrm,tqrs->kqcsm", full_time, t_table).astype(jnp.bfloat16)

    def synthesize(spectrum_in, t_table):
        along_t = product("kqorm,qtrs->ktosm", spectrum_in, t_table).astype(jnp.bfloat16)
        own_steps = lax.all_to_all(along_t, "ta", split_axis=1, concat_axis=0, tiled=True)
        along_z = product("ktorm,kzrs->ztosm", own_steps, z_inv).astype(jnp.bfloat16)
        blocks = along_z.reshape(gz_count, depth, steps_here, WIDTH, 2, owned_pairs)
        copies = jnp.broadcast_to(
            blocks[:, None], (gz_count, col_count, depth, steps_here, WIDTH, 2, owned_pairs)
        )
        copies = copies.reshape(owners, depth, steps_here, WIDTH, 2, owned_pairs)
        gathered = lax.all_to_all(copies, ("gz", "col"), split_axis=0, concat_axis=5, tiled=True)
        split_pairs = gathered.reshape(depth, steps_here, WIDTH, 2, MY, MX)
        along_y = product("ztcrbk,byrs->ztcysk", split_pairs, y_inv).astype(jnp.bfloat16)
        along_y = along_y.reshape(depth, steps_here, WIDTH, row_count, 2 * MX)
        return product("ztcyj,jx->ztcyx", along_y, x_inv)

    spectrum = analyse(field, t_plain_fwd)
    real_in = spectrum[:, :, :, 0]
    imag_in = spectrum[:, :, :, 1]
    real_w = spectral_weight[:, :, :, 0]
    imag_w = spectral_weight[:, :, :, 1]
    mixed_real = product("kqim,kqmio->kqom", real_in, real_w) - product(
        "kqim,kqmio->kqom", imag_in, imag_w
    )
    mixed_imag = product("kqim,kqmio->kqom", real_in, imag_w) + product(
        "kqim,kqmio->kqom", imag_in, real_w
    )
    mixed = jnp.stack([mixed_real, mixed_imag], 3).astype(jnp.bfloat16)
    spectral = synthesize(mixed, t_weighted_inv)
    preact = (
        spectral
        + product("ztcyx,co->ztoyx", field, point_weight)
        + point_bias[None, None, :, None, None]
    )
    gprime = (cotangent.astype(jnp.float32) * gelu_slope(preact)).astype(jnp.bfloat16)
    gspec = analyse(gprime, t_weighted_fwd)
    grad_real = gspec[:, :, :, 0]
    grad_imag = gspec[:, :, :, 1]
    weight_real = product("kqim,kqom->kqmio", real_in, grad_real) + product(
        "kqim,kqom->kqmio", imag_in, grad_imag
    )
    weight_imag = product("kqim,kqom->kqmio", real_in, grad_imag) - product(
        "kqim,kqom->kqmio", imag_in, grad_real
    )
    weight_grad = jnp.stack([weight_real, weight_imag], 3).astype(jnp.bfloat16)
    back_real = product("kqom,kqmio->kqim", grad_real, real_w) + product(
        "kqom,kqmio->kqim", grad_imag, imag_w
    )
    back_imag = product("kqom,kqmio->kqim", grad_imag, real_w) - product(
        "kqom,kqmio->kqim", grad_real, imag_w
    )
    dspec = jnp.stack([back_real, back_imag], 3).astype(jnp.bfloat16)
    back_field = synthesize(dspec, t_plain_inv)
    input_grad = (back_field + product("ztoyx,co->ztcyx", gprime, point_weight)).astype(
        jnp.bfloat16
    )
    return (input_grad, weight_grad)


def solution(mesh):
    placed = (
        P(("groups", "gz"), "ta", None, "col", None),
        P(("groups", "gz"), "ta", None, "col", None),
        P("ta", None, ("gz", "col"), None, None, None),
        P(),
        P(),
    )
    return jax.shard_map(
        per_device,
        mesh=mesh,
        in_specs=placed,
        out_specs=(
            P(("groups", "gz"), "ta", None, "col", None),
            P(("groups", "ta"), None, ("gz", "col"), None, None, None),
        ),
        check_vma=False,
    )
```

profile of v0, /device:TPU:0, one launch (start us, length us, event | category | flops | bytes accessed | tf_op | source)
XLA Modules:
  0.0 1254.7 jit_solution(8484469754445480883)
XLA Ops:
  8.7 11.2 convert_bitcast_fusion
  20.0 25.7 %copy.168 = bf16[8,12,20,32,48]{3,4,2,1,0:T(8,128)(2,1)} copy(bf16[8,12,20,32,48]{4,3,2,1,0:T(8,128)(2,1)} %convert_bitcast_fusion) | data formatting | bytes 11796480 | tf_op jit(solution)/shard_map/convert_element_type | solution.py:91
  46.3 29.4 %fusion.8 = bf16[8,12,20,2,24,24]{5,4,2,1,0,3:T(8,128)(2,1)} fusion(bf16[8,12,20,32,2,24,1]{3,5,4,2,1,0,6:T(8,128)(2,1)} %bitcast.497, s32[]{:T(128)S(6)} %select_n.243, bf16[64,24,1,2]{0,1,2,3:T(8,128)(2,1)S(1)} %get-tuple-element.37, bf16[64,24,1,2]{0,1,2,3:T(8,128)(2,1)S(1)} %get-tuple-element.52), kind=kOutput, calls=%fused_computation.23 | convolution fusion | flops 285339648 | bytes 10334212 | tf_op jit(solution)/shard_map/ztcyrk,ybrs->ztcsbk/dot_general | solution.py:59
  75.7 27.2 %convert_element_type.275 = bf16[8,12,20,2,4,2,72]{6,5,4,2,1,0,3:T(2,128)(2,1)} reshape(bf16[8,12,20,2,24,24]{5,4,2,1,0,3:T(8,128)(2,1)} %fusion.8) | data formatting | bytes 8847360 | tf_op jit(solution)/shard_map/convert_element_type | solution.py:96
  102.9 15.6 %copy.169 = bf16[8,12,20,2,4,2,72]{6,0,5,4,3,2,1:T(8,128)(2,1)} copy(bf16[8,12,20,2,4,2,72]{6,5,4,2,1,0,3:T(2,128)(2,1)} %convert_element_type.275) | data formatting | bytes 8847360 | tf_op jit(solution)/shard_map/convert_element_type | solution.py:96
  120.1 36.3 %all-reduce.5.cloned.1.call-done = bf16[8,12,20,2,4,2,72]{6,0,5,4,3,2,1:T(8,128)(2,1)} async-done(((bf16[8,12,20,2,4,2,72]{6,0,5,4,3,2,1:T(8,128)(2,1)}), bf16[8,12,20,2,4,2,72]{6,0,5,4,3,2,1:T(8,128)(2,1)}) %all-reduce.5.cloned.1.call-update) | async-done | bytes 4423696
  168.2 37.7 %fusion.182 = (bf16[8,12,72,1,20,20]{2,3,5,4,1,0:T(2,128)(2,1)}, bf16[8,12,72,1,20,20]{2,3,5,4,1,0:T(2,128)(2,1)}) fusion(bf16[8,12,72,2,20,20]{2,3,5,4,1,0:T(2,128)(2,1)} %param.7), kind=kLoop, calls=%fused_computation.239 | loop fusion | bytes 22118400 | tf_op jit(solution)/shard_map/slice | solution.py:124
  206.0 50.6 %all-to-all-done = bf16[8,12,20,2,4,72]{5,0,3,2,1,4:T(8,128)(2,1)} async-done(((bf16[8,12,20,2,4,72]{5,0,3,2,1,4:T(8,128)(2,1)}), bf16[8,12,20,2,4,72]{5,0,3,2,1,4:T(8,128)(2,1)}, u32[]{:S(2)}, u32[]{:S(2)}) %all-to-all-start) | async-done | bytes 2211872 | tf_op jit(solution)/shard_map/all_to_all | solution.py:99
  267.2 22.6 %all-to-all-done.1 = bf16[16,12,20,2,72]{4,3,2,1,0:T(2,128)(2,1)S(1)} async-done(((bf16[16,12,20,2,72]{4,3,2,1,0:T(2,128)(2,1)}), bf16[16,12,20,2,72]{4,3,2,1,0:T(2,128)(2,1)S(1)}, u32[]{:S(2)}, u32[]{:S(2)}) %all-to-all-start.1) | async-done | bytes 1105952 | tf_op jit(solution)/shard_map/all_to_all | solution.py:102
  297.3 43.4 %fusion.30 = (f32[8,12,72,20]{2,0,3,1:T(8,128)S(1)}, f32[8,12,72,20]{2,0,3,1:T(8,128)S(1)}, f32[8,12,72,20]{2,0,3,1:T(8,128)S(1)}, f32[8,12,72,20]{2,0,3,1:T(8,1...) fusion(f32[8,12,72,20]{2,0,3,1:T(8,128)S(1)} %copy.329, ...), kind=kLoop, calls=%fused_computation.35 | loop fusion | flops 27095040 | bytes 25436160
  344.3 25.1 %all_to_all.132 = bf16[8,24,20,2,72]{4,0,3,2,1:T(8,128)(2,1)S(1)} all-to-all(bf16[8,24,20,2,72]{4,0,3,2,1:T(8,128)(2,1)S(1)} %copy.179), channel_id=1, replica_groups=mesh['groups'=2,'gz'=4,'ta'=2,'col'=2] {'ta'}, dimensions={1} | all-to-all | bytes 2211840 | tf_op jit(solution)/shard_map/all_to_all | solution.py:107
  386.3 21.4 %fusion.38 = f32[20,8,12,32,128]{4,0,3,2,1:T(8,128)} fusion(bf16[8,12,20,32,128]{4,3,2,1,0:T(8,128)(2,1)} %param.5, bf16[20,20]{1,0:T(8,128)(2,1)S(1)} %copy-done), kind=kOutput, calls=%fused_computation.46 | convolution fusion | flops 314572800 | bytes 47186720 | tf_op jit(solution)/shard_map/ztcyx,co->ztoyx/dot_general | solution.py:59
  407.6 151.2 %all-to-all-done.3 = bf16[8,8,12,20,2,72]{5,4,3,2,1,0:T(2,128)(2,1)} async-done(((bf16[8,8,12,20,2,72]{5,4,3,2,1,0:T(2,128)(2,1)}), bf16[8,8,12,20,2,72]{5,4,3,2,1,0:T(2,128)(2,1)}, u32[]{:S(2)}, u32[]{:S(2)}) %all-to-all-start.3) | async-done | bytes 4423712 | tf_op jit(solution)/shard_map/all_to_all | solution.py:114
  558.9 15.6 %copy.183 = bf16[1,8,12,20,2,8,72]{6,5,4,3,2,1,0:T(8,128)(2,1)} copy(bf16[1,8,12,20,2,8,72]{6,4,3,2,1,5,0:T(2,128)(2,1)} %bitcast.101) | data formatting | bytes 8847360 | tf_op jit(solution)/shard_map/all_to_all | solution.py:114
  574.4 28.1 %reshape.590 = bf16[8,12,20,2,24,24]{5,4,3,2,1,0:T(8,128)(2,1)} reshape(bf16[1,8,12,20,2,8,72]{6,5,4,3,2,1,0:T(8,128)(2,1)} %copy.183) | data formatting | bytes 8847360 | tf_op jit(solution)/shard_map/reshape | solution.py:115
  602.5 19.5 %fusion.217 = bf16[8,12,20,32,2,24]{3,5,4,2,1,0:T(8,128)(2,1)} fusion(bf16[8,12,20,2,24,24]{5,4,3,2,1,0:T(8,128)(2,1)} %reshape.590, s32[]{:T(128)S(6)} %select_n.243, bf16[64,24,1,2]{0,1,3,2:T(8,128)(2,1)S(1)} %get-tuple-element.53, bf16[64,24,1,2]{0,1,3,2:T(8,128)(2,1)S(1)} %get-tuple-element.36), kind=kOutput, calls=%fused_computation.25.clone.clone.clone.clone.2 | convolution fusion | flops 286076928 | bytes 10334212 | tf_op jit(solution)/shard_map/ztcrbk,byrs->ztcysk/dot_general | solution.py:59
  622.0 39.7 %fusion.5 = bf16[8,12,20,32,128]{4,3,2,1,0:T(8,128)(2,1)} fusion(f32[20,8,12,32,128]{4,0,3,2,1:T(8,128)} %fusion.38, bf16[8,12,20,32,128]{4,3,2,1,0:T(8,128)(2,1)} %param.6, f32[20]{0:T(128)S(1)} %copy-done.30, bf16[1,128,24]{1,2,0:T(8,128)(2,1)S(1)} %copy-done.27, bf16[1,128,24]{1,2,0:T(8,128)(2,1)S(1)} %copy-done.25, ...), kind=kOutput, calls=%fused_computation.10 | convolution fusion | flops 857217024 | bytes 68825168 | tf_op jit(solution)/shard_map/ztcyj,jx->ztcyx/dot_general | solution.py:59
  673.0 25.8 %copy.189 = bf16[8,12,20,32,48]{3,4,2,1,0:T(8,128)(2,1)} copy(bf16[8,12,20,32,48]{4,3,2,1,0:T(8,128)(2,1)} %convolution_convert_fusion) | data formatting | bytes 11796480 | tf_op jit(solution)/shard_map/convert_element_type | solution.py:91
  698.7 29.4 %fusion.9 = bf16[8,12,20,2,24,24]{5,4,2,1,0,3:T(8,128)(2,1)} fusion(bf16[8,12,20,32,2,24,1]{3,5,4,2,1,0,6:T(8,128)(2,1)} %bitcast.498, s32[]{:T(128)S(6)} %select_n.243, bf16[64,24,1,2]{0,1,2,3:T(8,128)(2,1)S(1)} %copy-done.12, bf16[64,24,1,2]{0,1,2,3:T(8,128)(2,1)S(1)} %copy-done.14), kind=kOutput, calls=%fused_computation.24 | convolution fusion | flops 285339648 | bytes 10334212 | tf_op jit(solution)/shard_map/ztcyrk,ybrs->ztcsbk/dot_general | solution.py:59
  728.1 27.5 %convert_element_type.290 = bf16[8,12,20,2,4,2,72]{6,5,4,2,1,0,3:T(2,128)(2,1)} reshape(bf16[8,12,20,2,24,24]{5,4,2,1,0,3:T(8,128)(2,1)} %fusion.9) | data formatting | bytes 8847360 | tf_op jit(solution)/shard_map/convert_element_type | solution.py:96
  755.6 15.4 %copy.190 = bf16[8,12,20,2,4,2,72]{6,0,5,4,3,2,1:T(8,128)(2,1)} copy(bf16[8,12,20,2,4,2,72]{6,5,4,2,1,0,3:T(2,128)(2,1)} %convert_element_type.290) | data formatting | bytes 8847360 | tf_op jit(solution)/shard_map/convert_element_type | solution.py:96
  771.0 33.4 %all-reduce.7.cloned.1.call-done = bf16[8,12,20,2,4,2,72]{6,0,5,4,3,2,1:T(8,128)(2,1)} async-done(((bf16[8,12,20,2,4,2,72]{6,0,5,4,3,2,1:T(8,128)(2,1)}), bf16[8,12,20,2,4,2,72]{6,0,5,4,3,2,1:T(8,128)(2,1)}) %all-reduce.7.cloned.1.call-update) | async-done | bytes 4423696
  809.2 92.8 %all_to_all.133 = bf16[8,12,20,2,4,72]{5,0,3,2,1,4:T(8,128)(2,1)S(1)} all-to-all(bf16[8,12,20,2,4,72]{5,0,3,2,1,4:T(8,128)(2,1)S(1)} %copy.191), channel_id=1, replica_groups=mesh['groups'=2,'gz'=4,'ta'=2,'col'=2] {'gz'}, dimensions={4} | all-to-all | bytes 4423680 | tf_op jit(solution)/shard_map/all_to_all | solution.py:99
  904.8 25.8 %all_to_all.134 = bf16[16,12,20,2,72]{4,3,2,1,0:T(2,128)(2,1)S(1)} all-to-all(bf16[16,12,20,2,72]{4,3,2,1,0:T(2,128)(2,1)S(1)} %copy.193), channel_id=1, replica_groups=mesh['groups'=2,'gz'=4,'ta'=2,'col'=2] {'ta'}, dimensions={0} | all-to-all | bytes 2211840 | tf_op jit(solution)/shard_map/all_to_all | solution.py:102
  938.3 16.4 %fusion.34 = (f32[8,12,72,20]{2,0,3,1:T(8,128)S(1)}, f32[8,12,72,20]{2,0,3,1:T(8,128)S(1)}, f32[8,12,72,20]{2,0,3,1:T(8,128)S(1)}, f32[8,12,72,20]{2,0,3,1:T(8,128)S(1)}) fusion(f32[8,12,72,20]{2,0,3,1:T(8,128)S(1)} %copy.331, bf16[8,12,72,1,20,20]{2,0,5,4,3,1:T(8,128)(2,1)S(1)} %bitcast.502, f32[8,12,72,20]{2,0,3,1:T(8,128)S(1)} %copy.330, ...), kind=kLoop, calls=%fused_computation.39 | loop fusion | flops 27095040 | bytes 14376960
  958.5 24.7 %all_to_all.135 = bf16[8,24,20,2,72]{4,0,3,2,1:T(8,128)(2,1)S(1)} all-to-all(bf16[8,24,20,2,72]{4,0,3,2,1:T(8,128)(2,1)S(1)} %copy.199), channel_id=1, replica_groups=mesh['groups'=2,'gz'=4,'ta'=2,'col'=2] {'ta'}, dimensions={1} | all-to-all | bytes 2211840 | tf_op jit(solution)/shard_map/all_to_all | solution.py:107
  1003.8 20.1 %fusion.36 = f32[8,12,32,128,20]{3,4,2,1,0:T(8,128)} fusion(bf16[8,12,20,32,128]{4,3,2,1,0:T(8,128)(2,1)} %fusion.5, bf16[20,20]{1,0:T(8,128)(2,1)S(1)} %copy-done), kind=kOutput, calls=%fused_computation.44 | convolution fusion | flops 314572800 | bytes 47186720 | tf_op jit(solution)/shard_map/ztoyx,co->ztcyx/dot_general | solution.py:59
  1042.7 34.2 %copy.212 = bf16[8,12,72,2,20,20]{2,3,5,4,1,0:T(2,128)(2,1)} copy(bf16[8,12,72,2,20,20]{2,0,5,4,3,1:T(8,128)(2,1)S(1)} %pad_maximum_fusion) | data formatting | bytes 22118400
  1076.9 96.4 %all-to-all-done.7 = bf16[8,8,12,20,2,72]{5,4,3,2,1,0:T(2,128)(2,1)} async-done(((bf16[8,8,12,20,2,72]{5,4,3,2,1,0:T(2,128)(2,1)}), bf16[8,8,12,20,2,72]{5,4,3,2,1,0:T(2,128)(2,1)}, u32[]{:S(2)}, u32[]{:S(2)}) %all-to-all-start.7) | async-done | bytes 4423712 | tf_op jit(solution)/shard_map/all_to_all | solution.py:114
  1173.3 15.6 %copy.203 = bf16[1,8,12,20,2,8,72]{6,5,4,3,2,1,0:T(8,128)(2,1)} copy(bf16[1,8,12,20,2,8,72]{6,4,3,2,1,5,0:T(2,128)(2,1)} %bitcast.161) | data formatting | bytes 8847360 | tf_op jit(solution)/shard_map/all_to_all | solution.py:114
  1188.9 28.0 %reshape.595 = bf16[8,12,20,2,24,24]{5,4,3,2,1,0:T(8,128)(2,1)} reshape(bf16[1,8,12,20,2,8,72]{6,5,4,3,2,1,0:T(8,128)(2,1)} %copy.203) | data formatting | bytes 8847360 | tf_op jit(solution)/shard_map/reshape | solution.py:115
  1216.9 30.7 %fusion.6 = bf16[8,12,20,32,128]{4,3,2,1,0:T(8,128)(2,1)} fusion(f32[8,12,32,128,20]{3,4,2,1,0:T(8,128)} %fusion.36, bf16[8,12,20,2,24,24]{5,4,3,2,1,0:T(8,128)(2,1)} %reshape.595, s32[]{:T(128)S(6)} %select_n.243, bf16[64,24,1,2]{0,1,3,2:T(8,128)(2,1)S(1)} %copy-done.10, bf16[64,24,1,2]{0,1,3,2:T(8,128)(2,1)S(1)} %copy-done.8, ...), kind=kOutput, calls=%fused_computation.12 | convolution fusion | flops 1056780288 | bytes 51634180 | tf_op jit(solution)/shard_map/ztcyj,jx->ztcyx/dot_general | solution.py:59
  (144 shorter events, 123.5 us)
Async XLA Ops:
  7.2 379.1 %copy-start = (bf16[20,20]{1,0:T(8,128)(2,1)S(1)}, bf16[20,20]{1,0:T(8,128)(2,1)}, u32[]{:S(2)}) copy-start(bf16[20,20]{1,0:T(8,128)(2,1)} %param.8) | copy-start | bytes 2404
  7.2 149.3 %all-reduce.5.cloned.1.call-start = ((), (), s32[]{:S(2)}) async-start(), calls=%async_computation.8 | async-start | bytes 15728640
  45.7 556.8 %copy-start.7 = (bf16[64,24,1,2]{0,1,3,2:T(8,128)(2,1)}, bf16[64,24,1,2]{0,1,3,2:T(8,128)(2,1)S(1)}, u32[]{:S(2)}) copy-start(bf16[64,24,1,2]{0,1,3,2:T(8,128)(2,1)S(1)} %get-tuple-element.36) | copy-start | bytes 18436
  45.7 556.8 %copy-start.9 = (bf16[64,24,1,2]{0,1,3,2:T(8,128)(2,1)}, bf16[64,24,1,2]{0,1,3,2:T(8,128)(2,1)S(1)}, u32[]{:S(2)}) copy-start(bf16[64,24,1,2]{0,1,3,2:T(8,128)(2,1)S(1)} %get-tuple-element.53) | copy-start | bytes 18436
  119.5 137.1 %copy-start.19 = (bf16[32,16,1,2]{0,1,2,3:T(8,128)(2,1)}, bf16[32,16,1,2]{0,1,2,3:T(8,128)(2,1)S(1)}, u32[]{:S(2)}) copy-start(bf16[32,16,1,2]{0,1,2,3:T(8,128)(2,1)S(1)} %get-tuple-element.49) | copy-start | bytes 6148
  119.5 137.1 %copy-start.21 = (bf16[32,16,1,2]{0,1,2,3:T(8,128)(2,1)}, bf16[32,16,1,2]{0,1,2,3:T(8,128)(2,1)S(1)}, u32[]{:S(2)}) copy-start(bf16[32,16,1,2]{0,1,2,3:T(8,128)(2,1)S(1)} %get-tuple-element.58) | copy-start | bytes 6148
  119.5 249.9 %copy-start.15 = (bf16[32,16,1,2]{0,1,3,2:T(8,128)(2,1)}, bf16[32,16,1,2]{0,1,3,2:T(8,128)(2,1)S(1)}, u32[]{:S(2)}) copy-start(bf16[32,16,1,2]{0,1,3,2:T(8,128)(2,1)S(1)} %get-tuple-element.48) | copy-start | bytes 6148
  119.5 249.9 %copy-start.17 = (bf16[32,16,1,2]{0,1,3,2:T(8,128)(2,1)}, bf16[32,16,1,2]{0,1,3,2:T(8,128)(2,1)S(1)}, u32[]{:S(2)}) copy-start(bf16[32,16,1,2]{0,1,3,2:T(8,128)(2,1)S(1)} %get-tuple-element.59) | copy-start | bytes 6148
  163.1 93.4 %all-to-all-start = ((bf16[8,12,20,2,4,72]{5,0,3,2,1,4:T(8,128)(2,1)}), bf16[8,12,20,2,4,72]{5,0,3,2,1,4:T(8,128)(2,1)}, u32[]{:S(2)}, u32[]{:S(2)}) async-start(bf16[8,12,20,2,4,72]{5,0,3,2,1,4:T(8,128)(2,1)} %copy.170), calls=%async_computation | async-start | bytes 7864320 | tf_op jit(solution)/shard_map/all_to_all | solution.py:99
  262.8 27.1 %all-to-all-start.1 = ((bf16[16,12,20,2,72]{4,3,2,1,0:T(2,128)(2,1)}), bf16[16,12,20,2,72]{4,3,2,1,0:T(2,128)(2,1)S(1)}, u32[]{:S(2)}, u32[]{:S(2)}) async-start(bf16[16,12,20,2,72]{4,3,2,1,0:T(2,128)(2,1)} %copy.172), calls=%async_computation.1 | async-start | bytes 3932160 | tf_op jit(solution)/shard_map/all_to_all | solution.py:102
  381.3 177.6 %all-to-all-start.3 = ((bf16[8,8,12,20,2,72]{5,4,3,2,1,0:T(2,128)(2,1)}), bf16[8,8,12,20,2,72]{5,4,3,2,1,0:T(2,128)(2,1)}, u32[]{:S(2)}, u32[]{:S(2)}) async-start(bf16[8,8,12,20,2,72]{5,4,3,2,1,0:T(2,128)(2,1)} %bitcast.504), calls=%async_computation.3 | async-start | bytes 15728640 | tf_op jit(solution)/shard_map/all_to_all | solution.py:114
  386.2 418.1 %all-reduce.7.cloned.1.call-start = ((), (), s32[]{:S(2)}) async-start(), calls=%async_computation.9 | async-start | bytes 15728640
  602.5 19.5 %copy-start.25 = (bf16[1,128,24]{1,2,0:T(8,128)(2,1)S(1)}, bf16[1,128,24]{1,2,0:T(8,128)(2,1)}, u32[]{:S(2)}) copy-start(bf16[1,128,24]{1,2,0:T(8,128)(2,1)} %copy-done.24) | copy-start | bytes 18436
  602.5 19.5 %copy-start.27 = (bf16[1,128,24]{1,2,0:T(8,128)(2,1)S(1)}, bf16[1,128,24]{1,2,0:T(8,128)(2,1)}, u32[]{:S(2)}) copy-start(bf16[1,128,24]{1,2,0:T(8,128)(2,1)} %copy-done.26) | copy-start | bytes 18436
  602.5 19.5 %copy-start.30 = (f32[20]{0:T(128)S(1)}, f32[20]{0:T(128)}, u32[]{:S(2)}) copy-start(f32[20]{0:T(128)} %param.9) | copy-start | bytes 244
  622.0 39.7 %copy-start.6 = (bf16[2,128,24]{1,2,0:T(8,128)(2,1)S(1)}, bf16[2,128,24]{1,2,0:T(8,128)(2,1)}, u32[]{:S(2)}) copy-start(bf16[2,128,24]{1,2,0:T(8,128)(2,1)} %copy-done.5) | copy-start | bytes 36868
  673.0 25.8 %copy-start.12 = (bf16[64,24,1,2]{0,1,2,3:T(8,128)(2,1)S(1)}, bf16[64,24,1,2]{0,1,2,3:T(8,128)(2,1)}, u32[]{:S(2)}) copy-start(bf16[64,24,1,2]{0,1,2,3:T(8,128)(2,1)} %copy-done.11) | copy-start | bytes 18436
  673.0 25.8 %copy-start.14 = (bf16[64,24,1,2]{0,1,2,3:T(8,128)(2,1)S(1)}, bf16[64,24,1,2]{0,1,2,3:T(8,128)(2,1)}, u32[]{:S(2)}) copy-start(bf16[64,24,1,2]{0,1,2,3:T(8,128)(2,1)} %copy-done.13) | copy-start | bytes 18436
  808.0 94.0 %copy-start.20 = (bf16[32,16,1,2]{0,1,2,3:T(8,128)(2,1)S(1)}, bf16[32,16,1,2]{0,1,2,3:T(8,128)(2,1)}, u32[]{:S(2)}) copy-start(bf16[32,16,1,2]{0,1,2,3:T(8,128)(2,1)} %copy-done.19) | copy-start | bytes 6148
  808.1 93.9 %copy-start.22 = (bf16[32,16,1,2]{0,1,2,3:T(8,128)(2,1)S(1)}, bf16[32,16,1,2]{0,1,2,3:T(8,128)(2,1)}, u32[]{:S(2)}) copy-start(bf16[32,16,1,2]{0,1,2,3:T(8,128)(2,1)} %copy-done.21) | copy-start | bytes 6148
  902.0 30.5 %copy-start.23 = (bf16[24,12,2,2,1,1]{0,1,3,2,5,4:T(8,128)(2,1)S(1)}, bf16[24,12,2,2,1,1]{0,1,3,2,5,4:T(8,128)(2,1)}, u32[]{:S(2)}) copy-start(bf16[24,12,2,2,1,1]{0,1,3,2,5,4:T(8,128)(2,1)} %get-tuple-element.73) | copy-start | bytes 6916
  902.0 36.2 %slice-start.3 = ((s8[9830400]{0:T(1024)(128)(4,1)}), s8[4194304]{0:T(1024)(128)(4,1)S(1)}, s32[]{:S(2)}) async-start(s8[9830400]{0:T(1024)(128)(4,1)} %bitcast.501), calls=%async_computation.13 | async-start | bytes 8388608
  904.8 33.4 %slice-start.4 = ((s8[9830400]{0:T(1024)(128)(4,1)}), s8[4194304]{0:T(1024)(128)(4,1)S(1)}, s32[]{:S(2)}) async-start(s8[9830400]{0:T(1024)(128)(4,1)} %bitcast.501), calls=%async_computation.14 | async-start | bytes 8388608
  938.3 18.7 %copy-start.28 = (bf16[24,12,1,2]{0,1,3,2:T(8,128)(2,1)S(1)}, bf16[24,12,1,2]{0,1,3,2:T(8,128)(2,1)}, u32[]{:S(2)}) copy-start(bf16[24,12,1,2]{0,1,3,2:T(8,128)(2,1)} %get-tuple-element.40) | copy-start | bytes 3460
  938.3 18.7 %copy-start.29 = (bf16[24,12,1,2]{0,1,3,2:T(8,128)(2,1)S(1)}, bf16[24,12,1,2]{0,1,3,2:T(8,128)(2,1)}, u32[]{:S(2)}) copy-start(bf16[24,12,1,2]{0,1,3,2:T(8,128)(2,1)} %get-tuple-element.55) | copy-start | bytes 3460
  954.7 28.4 %copy-start.16 = (bf16[32,16,1,2]{0,1,3,2:T(8,128)(2,1)S(1)}, bf16[32,16,1,2]{0,1,3,2:T(8,128)(2,1)}, u32[]{:S(2)}) copy-start(bf16[32,16,1,2]{0,1,3,2:T(8,128)(2,1)} %copy-done.15) | copy-start | bytes 6148
  954.8 28.4 %copy-start.18 = (bf16[32,16,1,2]{0,1,3,2:T(8,128)(2,1)S(1)}, bf16[32,16,1,2]{0,1,3,2:T(8,128)(2,1)}, u32[]{:S(2)}) copy-start(bf16[32,16,1,2]{0,1,3,2:T(8,128)(2,1)} %copy-done.17) | copy-start | bytes 6148
  995.1 178.2 %all-to-all-start.7 = ((bf16[8,8,12,20,2,72]{5,4,3,2,1,0:T(2,128)(2,1)}), bf16[8,8,12,20,2,72]{5,4,3,2,1,0:T(2,128)(2,1)}, u32[]{:S(2)}, u32[]{:S(2)}) async-start(bf16[8,8,12,20,2,72]{5,4,3,2,1,0:T(2,128)(2,1)} %bitcast.503), calls=%async_computation.7 | async-start | bytes 15728640 | tf_op jit(solution)/shard_map/all_to_all | solution.py:114
  1003.8 20.1 %copy-start.4 = (f32[8,12,72,20]{2,1,3,0:T(8,128)S(1)}, f32[8,12,72,20]{2,1,3,0:T(8,128)}, u32[]{:S(2)}) copy-start(f32[8,12,72,20]{2,1,3,0:T(8,128)} %get-tuple-element.32) | copy-start | bytes 1658884
  1003.8 20.7 %copy-start.3 = (f32[8,12,72,20]{2,1,3,0:T(8,128)S(1)}, f32[8,12,72,20]{2,1,3,0:T(8,128)}, u32[]{:S(2)}) copy-start(f32[8,12,72,20]{2,1,3,0:T(8,128)} %get-tuple-element.35) | copy-start | bytes 1658884
  1188.9 28.0 %copy-start.8 = (bf16[64,24,1,2]{0,1,3,2:T(8,128)(2,1)S(1)}, bf16[64,24,1,2]{0,1,3,2:T(8,128)(2,1)}, u32[]{:S(2)}) copy-start(bf16[64,24,1,2]{0,1,3,2:T(8,128)(2,1)} %copy-done.7) | copy-start | bytes 18436
  1188.9 28.0 %copy-start.10 = (bf16[64,24,1,2]{0,1,3,2:T(8,128)(2,1)S(1)}, bf16[64,24,1,2]{0,1,3,2:T(8,128)(2,1)}, u32[]{:S(2)}) copy-start(bf16[64,24,1,2]{0,1,3,2:T(8,128)(2,1)} %copy-done.9) | copy-start | bytes 18436
  (12 other events, 53.9 us)
Sparse Core Ops, SparseCore 0:
  118.7 37.7 all-reduce.4
  771.1 33.1 all-reduce.6
where the time goes:
time: 1260 us; the launch traced here: 1250 us
  waiting for transfers between devices  390 us (31%)
  local copies, waits for them, and re-layouts  349 us (28%)
  matrix products  225 us (18%)
  blocking collectives  168 us (13%)
  other arithmetic  87.4 us (7%)
  starting transfers between devices  19.4 us (2%)
  between operations  14.9 us (1%)
    all_to_all x2, waiting for transfers between devices, synthesize(): lax.all_to_all(copies, ('gz', 'col'), split_axis=0, concat_axis=5, tiled=...  248 us
    dot_general x17, matrix products, product(): jnp.einsum(pattern, first_op, second_op, preferred_element_type=jnp.float32)  225 us
    all_to_all x1, blocking collectives, analyse(): moved = lax.all_to_all(mine, 'gz', split_axis=4, concat_axis=0, tiled=True)  92.8 us
    convert_element_type x4, local copies, waits for them, and re-layouts, analyse(): spread.astype(jnp.bfloat16)  85.7 us
    unnamed x4, waiting for transfers between devices  69.7 us
    unnamed x4, other arithmetic  59.8 us
    reshape x2, local copies, waits for them, and re-layouts, synthesize(): split_pairs = gathered.reshape(depth, steps_here, WIDTH, 2, MY, MX)  56.1 us
    convert_element_type x2, local copies, waits for them, and re-layouts, analyse(): along_x = product('ztcyx,xj->ztcyj', field_in, x_fwd).astype(jnp.bfloat16)  51.5 us
  transfers between devices with their start and end apart: 6, of which 6 were waited for; matrix products, arithmetic and copies ran while one was open for 11% of the time, Pallas kernels for 0%

commit v1 on v0

--- a/solution.py
+++ b/solution.py
@@ -1,8 +1,13 @@
+import functools
 import math
 
 import jax
 import jax.numpy as jnp
+import ml_dtypes
+import numpy as np
 from jax import lax
+from jax.experimental import pallas as pl
+from jax.experimental.pallas import tpu as pltpu
 from jax.sharding import PartitionSpec as P
 
 LX = 128
@@ -15,6 +20,9 @@
 MZ = 16
 MT = 12
 PAIRS = 576
+LANE = 128
+GROUP = 8
+CHUNKS = 2
 
 
 def wave_parts(length, mode_count, halfband):
@@ -64,7 +72,7 @@
     return normal_cdf + values * jnp.exp(-0.5 * values * values) / math.sqrt(2.0 * math.pi)
 
 
-def per_device(field, cotangent, spectral_weight, point_weight, point_bias):
+def general_device(field, cotangent, spectral_weight, point_weight, point_bias):
     col_index = lax.axis_index("col")
     gz_count = lax.axis_size("gz")
     col_count = lax.axis_size("col")
@@ -160,6 +168,682 @@
     return (input_grad, weight_grad)
 
 
+def waves(length, frequencies, places):
+    turns = (np.asarray(places)[:, None] * np.asarray(frequencies)[None, :]) % length
+    angles = turns * (2.0 * math.pi / length)
+    scaling = 1.0 / math.sqrt(length)
+    return np.cos(angles) * scaling, np.sin(angles) * scaling
+
+
+def signed(count):
+    return [k if k < count // 2 else k - count for k in range(count)]
+
+
+def bf16(table):
+    return np.asarray(table, dtype=np.float32).astype(ml_dtypes.bfloat16)
+
+
+class Plan:
+    def __init__(self, mesh, depth, steps, rows):
+        self.gz, self.ta, self.col = mesh.shape["gz"], mesh.shape["ta"], mesh.shape["col"]
+        self.depth, self.steps, self.rows = depth, steps, rows
+        self.owned = PAIRS // (self.gz * self.col)
+        self.ky_own = self.owned // MX
+        self.ky_half = MY // self.col
+        self.lanes = self.ky_half * 2 * MX
+        self.half_pairs = self.ky_half * MX
+        self.kt = MT // self.ta
+        self.kz = MZ // self.ta
+        self.grid_rows = steps * WIDTH
+
+    def y_tables(self):
+        out = np.zeros((self.gz, self.col, 2 * MY * GROUP, GROUP * self.rows), np.float32)
+        freq = np.array(signed(MY))
+        for a in range(self.gz):
+            for b in range(self.col):
+                order = [
+                    self.ky_own * (self.col * ((a + k) % self.gz) + (b ^ h)) + j
+                    for h in range(self.col)
+                    for k in range(self.gz)
+                    for j in range(self.ky_own)
+                ]
+                places = np.arange(self.rows) + b * self.rows
+                c, s = waves(LY, freq[order], places)
+                part = np.stack([c.T, -s.T], 0)
+                full = np.einsum("sky,gh->skghy", part, np.eye(GROUP))
+                out[a, b] = full.reshape(out.shape[2:])
+        return bf16(out.reshape(self.gz * self.col, *out.shape[2:]))
+
+    def x_tiles(self):
+        c, s = waves(LX, signed(MX), np.arange(LX))
+        one = np.zeros((2, LX, 2, MX))
+        one[0, :, 0], one[1, :, 0], one[0, :, 1], one[1, :, 1] = c, s, -s, c
+        one = one.reshape(2 * LX, 2 * MX)
+        tiles = []
+        for low in range(0, self.lanes, 256):
+            high = min(low + 256, self.lanes)
+            kys = [k for k in range(self.ky_half) if k * 2 * MX < high and (k + 1) * 2 * MX > low]
+            table = np.zeros((len(kys), 2 * LX, self.lanes), np.float32)
+            for n, k in enumerate(kys):
+                table[n, :, k * 2 * MX : (k + 1) * 2 * MX] = one
+            table = table[:, :, low:high].reshape(len(kys) * 2 * LX, high - low)
+            tiles.append((low, high, kys, bf16(table)))
+        return tiles
+
+    def x_windows(self):
+        c, s = waves(LX, signed(MX), np.arange(LX))
+        one = np.zeros((2, MX, 2, LX))
+        one[0, :, 0], one[1, :, 0], one[0, :, 1], one[1, :, 1] = c.T, -s.T, s.T, c.T
+        one = one.reshape(2 * MX, 2 * LX)
+        windows, table = [], np.zeros((self.ky_half, 256, 2 * LX), np.float32)
+        for k in range(self.ky_half):
+            low = k * 2 * MX // 128 * 128
+            high = min(low + 256, self.lanes)
+            table[k, k * 2 * MX - low : (k + 1) * 2 * MX - low] = one
+            windows.append((low, high))
+        return windows, bf16(table)
+
+    def t_tables(self, weighted):
+        weight = np.array([1.0] + [2.0] * (MT - 1)) if weighted else np.ones(MT)
+        gp = self.grid_rows_padded()
+        eye = np.eye(WIDTH)
+        fwd = np.zeros((self.ta, self.grid_rows, 2, self.ta, LANE), np.float32)
+        inv = np.zeros((self.ta, self.ta, 2, LANE, 2, gp), np.float32)
+        for a in range(self.ta):
+            c, s = waves(LT, np.arange(MT), np.arange(self.steps) + a * self.steps)
+            c, s = bf16(c * weight).astype(np.float32), bf16(s * weight).astype(np.float32)
+            for h in range(self.ta):
+                pick = slice((a ^ h) * self.kt, ((a ^ h) + 1) * self.kt)
+                n = self.kt * WIDTH
+                kc = np.einsum("tk,cd->tckd", c[:, pick], eye).reshape(self.grid_rows, n)
+                ks = np.einsum("tk,cd->tckd", s[:, pick], eye).reshape(self.grid_rows, n)
+                fwd[a, :, 0, h, :n], fwd[a, :, 1, h, :n] = kc, -ks
+                g = self.grid_rows
+                inv[a, h, 0, :n, 0, :g], inv[a, h, 1, :n, 0, :g] = kc.T, -ks.T
+                inv[a, h, 0, :n, 1, :g], inv[a, h, 1, :n, 1, :g] = ks.T, kc.T
+        fwd = fwd.reshape(self.ta, self.grid_rows, 2 * self.ta * LANE)
+        return bf16(fwd), bf16(inv.reshape(self.ta, self.ta * 2 * LANE, 2 * gp))
+
+    def grid_rows_padded(self):
+        return (self.grid_rows + LANE - 1) // LANE * LANE
+
+    def z_tables(self):
+        shape = (self.ta, 2, self.kz, 2, self.gz, self.depth)
+        fwd = np.zeros((self.gz, self.ta) + shape, np.float32)
+        inv = np.zeros_like(fwd)
+        freq = np.array(signed(MZ))
+        for a in range(self.gz):
+            places = np.concatenate(
+                [np.arange(self.depth) + (a - k) % self.gz * self.depth for k in range(self.gz)]
+            )
+            for b in range(self.ta):
+                for h in range(self.ta):
+                    own = freq[(b ^ h) * self.kz : ((b ^ h) + 1) * self.kz]
+                    c, s = waves(LZ, own, places)
+                    c, s = (v.T.reshape(self.kz, self.gz, self.depth) for v in (c, s))
+                    f, i = fwd[a, b, h], inv[a, b, h]
+                    f[0, :, 0], f[0, :, 1], f[1, :, 0], f[1, :, 1] = c, s, -s, c
+                    i[0, :, 0], i[0, :, 1], i[1, :, 0], i[1, :, 1] = c, s, -s, c
+        eye = np.eye(GROUP)
+        n = self.gz * self.ta
+        f = np.einsum("abhskrmz,pq->abhskprmzq", fwd, eye)
+        i = np.einsum("abhskrmz,pq->abrmzphskq", inv, eye)
+        rows = self.ta * 2 * self.kz * GROUP
+        cols = 2 * self.gz * self.depth * GROUP
+        return bf16(f.reshape(n, rows, cols)), bf16(i.reshape(n, cols, rows))
+
+    def pair_rows(self):
+        n = self.kt * WIDTH
+        table = np.zeros((self.ta, n, 2, self.ta, 2, LANE), np.float32)
+        for h in range(self.ta):
+            for r in range(2):
+                table[h, np.arange(n), r, h, r, np.arange(n)] = 1.0
+        return bf16(table.reshape(self.ta * n * 2, self.ta * 2 * LANE))
+
+
+def dot(a, b):
+    return jnp.dot(a, b, preferred_element_type=jnp.float32)
+
+
+def dot_nt(a, b):
+    return lax.dot_general(a, b, (((1,), (1,)), ((), ())), preferred_element_type=jnp.float32)
+
+
+def slope_of(v):
+    e = jnp.exp(-0.5 * v * v)
+    t = 1.0 / (1.0 + (0.3275911 / math.sqrt(2.0)) * jnp.abs(v))
+    poly = t * (
+        0.5 * 0.254829592
+        + t
+        * (
+            0.5 * -0.284496736
+            + t * (0.5 * 1.421413741 + t * (0.5 * -1.453152027 + t * (0.5 * 1.061405429)))
+        )
+    )
+    tail = poly * e
+    cdf = jnp.where(v >= 0.0, 1.0 - tail, tail)
+    return cdf + v * e * (1.0 / math.sqrt(2.0 * math.pi))
+
+
+def params(steps=1):
+    return pltpu.CompilerParams(
+        vmem_limit_bytes=56 << 20, dimension_semantics=("arbitrary",) * steps
+    )
+
+
+def whole_block(a):
+    return pl.BlockSpec(a.shape, lambda *i, n=a.ndim: (0,) * n)
+
+
+def spread_y(plan, fields, base, count, ty, us):
+    for q in range(count // (2 * GROUP)):
+        g = pl.multiple_of(base + q * 2 * GROUP, 2 * GROUP)
+        a = fields[0, pl.ds(g, GROUP)].reshape(GROUP * plan.rows, LX)
+        b = fields[0, pl.ds(g + GROUP, GROUP)].reshape(GROUP * plan.rows, LX)
+        u = dot(ty, jnp.concatenate([a, b], 1))
+        ua = u[:, :LX].reshape(2 * MY, GROUP, LX)
+        ub = u[:, LX:].reshape(2 * MY, GROUP, LX)
+        us[:, pl.ds(g, 2 * GROUP), :] = jnp.concatenate([ua, ub], 1).astype(jnp.bfloat16)
+
+
+def gather_x(plan, tiles, us, tables, outs):
+    for h in range(plan.col):
+        for (low, high, kys, _), table in zip(tiles, tables):
+            parts = []
+            for k in kys:
+                ky = h * plan.ky_half + k
+                parts += [us[ky], us[MY + ky]]
+            o = dot(jnp.concatenate(parts, 1), table[...])
+            outs[h][0, :, low:high] = o.astype(jnp.bfloat16)
+
+
+def rows_call(kernel, n, plan, grid, inputs, specs, out_shapes, out_specs, scratch, aliases, flops):
+    size = sum(math.prod(s.shape) * 2 for s in out_shapes)
+    return pl.pallas_call(
+        kernel,
+        grid=(grid,),
+        in_specs=specs,
+        out_specs=out_specs,
+        out_shape=out_shapes,
+        scratch_shapes=scratch,
+        input_output_aliases=aliases,
+        compiler_params=params(),
+        name=n,
+        cost_estimate=pl.CostEstimate(
+            flops=int(flops), bytes_accessed=int(size * 2), transcendentals=0
+        ),
+    )(*inputs)
+
+
+def analyse_xy(plan, tiles, field, ty, z0, zc):
+    def kernel(f, ty_ref, *refs):
+        tables, outs, us = refs[: len(tiles)], refs[len(tiles) : -1], refs[-1]
+        step = 5 * 2 * GROUP
+        def body(i, carry):
+            spread_y(plan, f, i * step, step, ty_ref[...], us)
+            return carry
+        lax.fori_loop(0, plan.grid_rows // step, body, 0)
+        gather_x(plan, tiles, us, tables, outs)
+
+    tabs = [jnp.asarray(t[3]) for t in tiles]
+    out = jax.ShapeDtypeStruct((zc, plan.grid_rows, plan.lanes), jnp.bfloat16)
+    block = pl.BlockSpec((1, plan.grid_rows, plan.lanes), lambda z: (z, 0, 0))
+    fspec = pl.BlockSpec((1, plan.grid_rows, plan.rows, LX), lambda z: (z0 + z, 0, 0, 0))
+    return rows_call(
+        kernel, "analyse_xy", plan, zc, [field, ty, *tabs],
+        [fspec, whole_block(ty)] + [whole_block(t) for t in tabs],
+        [out, out], [block, block],
+        [pltpu.VMEM((2 * MY, plan.grid_rows, LX), jnp.bfloat16)], {}, zc * 24e9,
+    )
+
+
+def field_pass(plan, tiles, windows, own, other, field, mixer, ty, ty_inv, xi, z0, zc, cot=None, bias=None, full=None):
+    first = cot is not None
+    tabs = [jnp.asarray(t[3]) for t in tiles] if first else []
+    block_rows = 4 * WIDTH
+    half = plan.rows // 2
+
+    def kernel(*refs):
+        refs = list(refs)
+        s_refs = (refs.pop(0), refs.pop(0))
+        f, mix, tyi, xi_ref = refs.pop(0), refs.pop(0), refs.pop(0), refs.pop(0)
+        if first:
+            c_ref, bias_ref, ty_ref = refs.pop(0), refs.pop(0), refs.pop(0)
+            tables = [refs.pop(0) for _ in tabs]
+            g_out = refs.pop(0)
+            outs = (refs.pop(0), refs.pop(0))
+            us = refs.pop()
+        else:
+            if full is not None:
+                refs.pop(0)
+            g_out = refs.pop(0)
+        ws, pre = refs
+        for h in range(plan.col):
+            for k in range(plan.ky_half):
+                low, high = windows[k]
+                w = dot(s_refs[h][0, :, low:high], xi_ref[k, : high - low])
+                ws[h * plan.ky_half + k] = w[:, :LX]
+                ws[MY + h * plan.ky_half + k] = w[:, LX:]
+
+        def block(i, carry):
+            base = pl.multiple_of(i * block_rows, block_rows)
+            for q in range(block_rows // (2 * GROUP)):
+                g = pl.multiple_of(base + q * 2 * GROUP, GROUP)
+                a = ws[:, pl.ds(g, GROUP), :].reshape(2 * MY * GROUP, LX).astype(jnp.bfloat16)
+                b = ws[:, pl.ds(g + GROUP, GROUP), :].reshape(2 * MY * GROUP, LX).astype(jnp.bfloat16)
+                o = dot(tyi[...], jnp.concatenate([a, b], 1))
+                at = q * 2 * GROUP
+                pre[at : at + GROUP] = o[:, :LX].reshape(GROUP, plan.rows, LX)
+                pre[at + GROUP : at + 2 * GROUP] = o[:, LX:].reshape(GROUP, plan.rows, LX)
+            for t in range(block_rows // WIDTH):
+                v = f[0, pl.ds(base + t * WIDTH, WIDTH)]
+                a = v[:, :half].reshape(WIDTH * half, LX)
+                b = v[:, half:].reshape(WIDTH * half, LX)
+                o = dot(mix[...], jnp.concatenate([a, b], 1))
+                at = t * WIDTH
+                pre[at : at + WIDTH, :half] += o[:, :LX].reshape(WIDTH, half, LX)
+                pre[at : at + WIDTH, half:] += o[:, LX:].reshape(WIDTH, half, LX)
+            if first:
+                def slopes(j, c2):
+                    for m in range(4):
+                        v = pre[j * 4 + m] + bias_ref[lax.rem(j * 4 + m, WIDTH)]
+                        c = c_ref[0, base + j * 4 + m].astype(jnp.float32)
+                        g_out[0, base + j * 4 + m] = (c * slope_of(v)).astype(jnp.bfloat16)
+                    return c2
+                lax.fori_loop(0, block_rows // 4, slopes, 0)
+                spread_y(plan, g_out, base, block_rows, ty_ref[...], us)
+            else:
+                g_out[0, pl.ds(base, block_rows)] = pre[...].astype(jnp.bfloat16)
+            return carry
+
+        lax.fori_loop(0, plan.grid_rows // block_rows, block, 0)
+        if first:
+            gather_x(plan, tiles, us, tables, outs)
+
+    cell = (1, plan.grid_rows, plan.rows, LX)
+    local = pl.BlockSpec(cell, lambda z: (z, 0, 0, 0))
+    placed = pl.BlockSpec(cell, lambda z: (z0 + z, 0, 0, 0))
+    sblock = pl.BlockSpec((1, plan.grid_rows, plan.lanes), lambda z: (z, 0, 0))
+    scratch = [
+        pltpu.VMEM((2 * MY, plan.grid_rows, LX), jnp.float32),
+        pltpu.VMEM((block_rows, plan.rows, LX), jnp.float32),
+    ]
+    if first:
+        inputs = [own, other, field, mixer, ty_inv, xi, cot, bias, ty, *tabs]
+        specs = [sblock, sblock, placed, whole_block(mixer), whole_block(ty_inv), whole_block(xi), placed]
+        specs += [pl.BlockSpec(memory_space=pltpu.SMEM), whole_block(ty)] + [whole_block(t) for t in tabs]
+        spec = jax.ShapeDtypeStruct((zc, plan.grid_rows, plan.lanes), jnp.bfloat16)
+        gout = jax.ShapeDtypeStruct((zc,) + cell[1:], jnp.bfloat16)
+        return rows_call(
+            kernel, "slope_pass", plan, zc, inputs, specs, [gout, spec, spec], [local, sblock, sblock],
+            scratch + [pltpu.VMEM((2 * MY, plan.grid_rows, LX), jnp.bfloat16)], {}, zc * 70e9,
+        )
+    inputs = [own, other, field, mixer, ty_inv, xi]
+    specs = [sblock, sblock, local, whole_block(mixer), whole_block(ty_inv), whole_block(xi)]
+    aliases = {}
+    if full is not None:
+        aliases = {len(inputs): 0}
+        inputs.append(full)
+        specs.append(pl.BlockSpec(memory_space=pl.ANY))
+    gout = jax.ShapeDtypeStruct((plan.depth,) + cell[1:], jnp.bfloat16)
+    return rows_call(
+        kernel, "input_pass", plan, zc, inputs, specs, [gout], [placed], scratch, aliases, zc * 35e9
+    )[0]
+
+
+def time_forward(plan, own, other, table):
+    zc = own.shape[0]
+    hp = plan.half_pairs
+
+    def kernel(a_ref, b_ref, m_ref, keep, send):
+        a = a_ref[0].astype(jnp.float32) + b_ref[0].astype(jnp.float32)
+        at = jnp.transpose(a).astype(jnp.bfloat16)
+        p = dot(at, m_ref[...]).reshape(plan.ky_half, 2, MX, 4 * LANE)
+        re = p[:, 0, :, : 2 * LANE] - p[:, 1, :, 2 * LANE :]
+        im = p[:, 0, :, 2 * LANE :] + p[:, 1, :, : 2 * LANE]
+        re, im = (v.reshape(plan.gz, 1, plan.owned, 2 * LANE).astype(jnp.bfloat16) for v in (re, im))
+        keep[...] = jnp.concatenate([re[..., :LANE], im[..., :LANE]], -1)
+        send[...] = jnp.concatenate([re[..., LANE:], im[..., LANE:]], -1)
+
+    block = pl.BlockSpec((1, plan.grid_rows, plan.lanes), lambda z: (z, 0, 0))
+    out = jax.ShapeDtypeStruct((plan.gz, zc, plan.owned, 2 * LANE), jnp.bfloat16)
+    ospec = pl.BlockSpec((plan.gz, 1, plan.owned, 2 * LANE), lambda z: (0, z, 0, 0))
+    return rows_call(
+        kernel, "time_forward", plan, zc, [own, other, table], [block, block, whole_block(table)],
+        [out, out], [ospec, ospec], [], {}, zc * 1e9,
+    )
+
+
+def time_inverse(plan, keep, got, table):
+    zc = keep.shape[1]
+    gp = plan.grid_rows_padded()
+
+    def kernel(a_ref, b_ref, m_ref, out):
+        rows = plan.half_pairs
+        a = a_ref[...].reshape(rows, 2 * LANE)
+        b = b_ref[...].reshape(rows, 2 * LANE)
+        o = dot(jnp.concatenate([a, b], 1), m_ref[...]).reshape(plan.ky_half, 1, MX, 2 * gp)
+        o = jnp.concatenate([o[..., :gp], o[..., gp:]], 1).reshape(plan.lanes, gp)
+        out[0] = jnp.transpose(o)[: plan.grid_rows].astype(jnp.bfloat16)
+
+    ispec = pl.BlockSpec((plan.gz, 1, plan.owned, 2 * LANE), lambda z: (0, z, 0, 0))
+    out = jax.ShapeDtypeStruct((zc, plan.grid_rows, plan.lanes), jnp.bfloat16)
+    return rows_call(
+        kernel, "time_inverse", plan, zc, [keep, got, table], [ispec, ispec, whole_block(table)],
+        [out], [pl.BlockSpec((1, plan.grid_rows, plan.lanes), lambda z: (z, 0, 0))], [], {}, zc * 1e9,
+    )[0]
+
+
+def depth_forward(plan, pieces, table):
+    flat = [p for chunk in pieces for p in chunk]
+    n = len(flat)
+    zc = pieces[0][0].shape[0]
+    octets = plan.owned // GROUP
+    count = plan.gz * plan.depth
+
+    def kernel(*refs):
+        ins, m_ref, keep, send, buf, out = refs[:n], refs[n], refs[n + 1], refs[n + 2], refs[n + 3], refs[n + 4]
+        for c in range(len(pieces)):
+            for k in range(plan.gz):
+                at = k * plan.depth + c * zc
+                buf[at : at + zc] = ins[c * plan.gz + k][...].astype(jnp.float32)
+        for o in range(octets):
+            x = buf[:, o * GROUP : (o + 1) * GROUP, :].reshape(count * GROUP, 2 * LANE)
+            x = jnp.concatenate([x[:, :LANE], x[:, LANE:]], 0).astype(jnp.bfloat16)
+            y = dot(m_ref[...], x).reshape(plan.ta, 2, plan.kz, GROUP, LANE)
+            for h in range(plan.ta):
+                for s in range(2):
+                    out[h, :, o * GROUP : (o + 1) * GROUP, s * LANE : (s + 1) * LANE] = y[h, s]
+        keep[...] = out[0].astype(jnp.bfloat16)
+        send[...] = out[1].astype(jnp.bfloat16)
+
+    shape = jax.ShapeDtypeStruct((plan.kz, plan.owned, 2 * LANE), jnp.bfloat16)
+    return rows_call(
+        kernel, "depth_forward", plan, 1, [*flat, table], [whole_block(a) for a in flat] + [whole_block(table)],
+        [shape, shape], [pl.BlockSpec(shape.shape, lambda i: (0, 0, 0))] * 2,
+        [
+            pltpu.VMEM((count, plan.owned, 2 * LANE), jnp.float32),
+            pltpu.VMEM((plan.ta, plan.kz, plan.owned, 2 * LANE), jnp.float32),
+        ], {}, 1e9,
+    )
+
+
+def depth_inverse(plan, keep, got, table, chunks):
+    octets = plan.owned // GROUP
+    zc = plan.depth // chunks
+    count = plan.gz * plan.depth
+
+    def kernel(a_ref, b_ref, m_ref, *refs):
+        outs, buf, out = refs[:-2], refs[-2], refs[-1]
+        buf[0] = a_ref[...].astype(jnp.float32)
+        buf[1] = b_ref[...].astype(jnp.float32)
+        for o in range(octets):
+            rows = slice(o * GROUP, (o + 1) * GROUP)
+            x = [
+                buf[h, :, rows, s * LANE : (s + 1) * LANE].reshape(plan.kz * GROUP, LANE)
+                for h in range(plan.ta)
+                for s in range(2)
+            ]
+            y = dot(m_ref[...], jnp.concatenate(x, 0).astype(jnp.bfloat16))
+            y = y.reshape(2, count, GROUP, LANE)
+            for s in range(2):
+                out[:, rows, s * LANE : (s + 1) * LANE] = y[s]
+        for c in range(chunks):
+            for k in range(plan.gz):
+                at = k * plan.depth + c * zc
+                outs[c * plan.gz + k][...] = out[at : at + zc].astype(jnp.bfloat16)
+
+    shape = jax.ShapeDtypeStruct((zc, plan.owned, 2 * LANE), jnp.bfloat16)
+    n = chunks * plan.gz
+    flat = rows_call(
+        kernel, "depth_inverse", plan, 1, [keep, got, table],
+        [whole_block(keep), whole_block(got), whole_block(table)],
+        [shape] * n, [pl.BlockSpec(shape.shape, lambda i: (0, 0, 0))] * n,
+        [
+            pltpu.VMEM((plan.ta, plan.kz, plan.owned, 2 * LANE), jnp.float32),
+            pltpu.VMEM((count, plan.owned, 2 * LANE), jnp.float32),
+        ], {}, 1e9,
+    )
+    return [flat[c * plan.gz : (c + 1) * plan.gz] for c in range(chunks)]
+
+
+def swap_pairs(v):
+    n = v.shape[0]
+    even = lax.rem(lax.broadcasted_iota(jnp.int32, v.shape, 0), 2) == 0
+    return jnp.where(even, -pltpu.roll(v, n - 1, 0), pltpu.roll(v, 1, 0))
+
+
+def to_comm(plan, rows_ref, perm, keep, send):
+    flat = rows_ref[...].astype(jnp.bfloat16)
+    p = plan.owned
+    unit = (lax.broadcasted_iota(jnp.int32, (p, p), 0) == lax.broadcasted_iota(jnp.int32, (p, p), 1))
+    turned = dot_nt(unit.astype(jnp.bfloat16), flat).astype(jnp.bfloat16)
+    o = dot(turned, perm[...]).astype(jnp.bfloat16)
+    keep[0] = o[:, : 2 * LANE]
+    send[0] = o[:, 2 * LANE :]
+
+
+def mode_specs(plan):
+    mode_rows = MT * WIDTH * WIDTH * 2
+    half = pl.BlockSpec((1, plan.owned, 2 * LANE), lambda k: (k, 0, 0))
+    weights = pl.BlockSpec((1, mode_rows, plan.owned), lambda k: (k, 0, 0))
+    return half, weights, mode_rows
+
+
+def mix_modes(plan, spec, weights, here, perm, unit):
+    half, wspec, mode_rows = mode_specs(plan)
+    per_t = WIDTH * WIDTH * 2
+    wide = 2 * WIDTH
+
+    def kernel(here_ref, a_ref, b_ref, w_ref, perm_ref, unit_ref, keep, send, xs, ms):
+        x = jnp.concatenate([a_ref[0], b_ref[0]], 1)
+        xs[...] = dot_nt(unit_ref[...], x)
+
+        def step(q, carry):
+            h = q // plan.kt
+            kt = q - h * plan.kt
+            at = lax.rem(q + here_ref[0] * plan.kt, MT)
+            row = h * 2 * LANE + kt * WIDTH
+            s1 = jnp.zeros((wide, plan.owned), jnp.float32)
+            s2 = jnp.zeros((wide, plan.owned), jnp.float32)
+            for i in range(0, WIDTH, 2):
+                w = w_ref[0, pl.ds(pl.multiple_of(at * per_t + i * wide, 2 * wide), 2 * wide), :].astype(jnp.float32)
+                for j in range(2):
+                    wi = w[j * wide : (j + 1) * wide]
+                    s1 += xs[pl.ds(row + i + j, 1), :] * wi
+                    s2 += xs[pl.ds(row + LANE + i + j, 1), :] * wi
+            ms[pl.ds(pl.multiple_of(q * wide, 8), wide), :] = s1 + swap_pairs(s2)
+            return carry
+
+        lax.fori_loop(0, MT, step, 0)
+        to_comm(plan, ms, perm_ref, keep, send)
+
+    shape = jax.ShapeDtypeStruct((plan.kz, plan.owned, 2 * LANE), jnp.bfloat16)
+    return rows_call(
+        kernel, "mix_modes", plan, plan.kz, [here, *spec, weights, perm, unit],
+        [pl.BlockSpec(memory_space=pltpu.SMEM), half, half, wspec, whole_block(perm), whole_block(unit)],
+        [shape, shape], [half, half],
+        [
+            pltpu.VMEM((2 * plan.ta * LANE, plan.owned), jnp.float32),
+            pltpu.VMEM((MT * wide, plan.owned), jnp.float32),
+        ], {}, 1e9,
+    )
+
+
+def back_modes(plan, grad, weights, here, perm):
+    half, wspec, mode_rows = mode_specs(plan)
+    per_t = WIDTH * WIDTH * 2
+    wide = 2 * WIDTH
+
+    def kernel(here_ref, a_ref, b_ref, w_ref, perm_ref, keep, send, gs, ms):
+        gs[...] = dot_nt(perm_ref[...], jnp.concatenate([a_ref[0], b_ref[0]], 1))
+
+        def step(q, carry):
+            at = lax.rem(q + here_ref[0] * plan.kt, MT)
+            g = gs[pl.ds(pl.multiple_of(q * wide, 8), wide), :]
+            g2 = -swap_pairs(g)
+            rows = []
+            for i in range(0, WIDTH, 2):
+                w = w_ref[0, pl.ds(pl.multiple_of(at * per_t + i * wide, 2 * wide), 2 * wide), :].astype(jnp.float32)
+                for j in range(2):
+                    wi = w[j * wide : (j + 1) * wide]
+                    rows.append(jnp.sum(g * wi, 0, keepdims=True))
+                    rows.append(jnp.sum(g2 * wi, 0, keepdims=True))
+            ms[pl.ds(pl.multiple_of(q * wide, 8), wide), :] = jnp.concatenate(rows, 0)
+            return carry
+
+        lax.fori_loop(0, MT, step, 0)
+        to_comm(plan, ms, perm_ref, keep, send)
+
+    shape = jax.ShapeDtypeStruct((plan.kz, plan.owned, 2 * LANE), jnp.bfloat16)
+    return rows_call(
+        kernel, "back_modes", plan, plan.kz, [here, *grad, weights, perm],
+        [pl.BlockSpec(memory_space=pltpu.SMEM), half, half, wspec, whole_block(perm)],
+        [shape, shape], [half, half],
+        [pltpu.VMEM((MT * wide, plan.owned), jnp.float32)] * 2, {}, 1e9,
+    )
+
+
+def weight_modes(plan, spec, grad, here, perm, unit):
+    half, wspec, mode_rows = mode_specs(plan)
+    per_t = WIDTH * WIDTH * 2
+    wide = 2 * WIDTH
+
+    def kernel(here_ref, xa, xb, ga, gb, perm_ref, unit_ref, out, xs, gs):
+        xs[...] = dot_nt(unit_ref[...], jnp.concatenate([xa[0], xb[0]], 1))
+        gs[...] = dot_nt(perm_ref[...], jnp.concatenate([ga[0], gb[0]], 1))
+
+        def step(q, carry):
+            h = q // plan.kt
+            kt = q - h * plan.kt
+            at = lax.rem(q + here_ref[0] * plan.kt, MT)
+            row = h * 2 * LANE + kt * WIDTH
+            g = gs[pl.ds(pl.multiple_of(q * wide, 8), wide), :]
+            g2 = -swap_pairs(g)
+            for i in range(0, WIDTH, 2):
+                two = [
+                    xs[pl.ds(row + i + j, 1), :] * g + xs[pl.ds(row + LANE + i + j, 1), :] * g2
+                    for j in range(2)
+                ]
+                rows = pl.ds(pl.multiple_of(at * per_t + i * wide, 2 * wide), 2 * wide)
+                out[0, rows, :] = jnp.concatenate(two, 0).astype(jnp.bfloat16)
+            return carry
+
+        lax.fori_loop(0, MT, step, 0)
+
+    shape = jax.ShapeDtypeStruct((plan.kz, mode_rows, plan.owned), jnp.bfloat16)
+    return rows_call(
+        kernel, "weight_modes", plan, plan.kz, [here, *spec, *grad, perm, unit],
+        [pl.BlockSpec(memory_space=pltpu.SMEM), half, half, half, half, whole_block(perm), whole_block(unit)],
+        [shape], [wspec],
+        [
+            pltpu.VMEM((2 * plan.ta * LANE, plan.owned), jnp.float32),
+            pltpu.VMEM((MT * wide, plan.owned), jnp.float32),
+        ], {}, 1e9,
+    )[0]
+
+
+def direct_device(plan, field, cotangent, spectral_weight, point_weight, point_bias):
+    gz_at, ta_at, col_at = (lax.axis_index(a) for a in ("gz", "ta", "col"))
+    chunks = CHUNKS
+    zc = plan.depth // chunks
+    pick = lambda table, at: lax.dynamic_index_in_dim(jnp.asarray(table), at, 0, keepdims=False)
+    ty = pick(plan.y_tables(), gz_at * plan.col + col_at)
+    ty_inv = ty.T
+    tiles = plan.x_tiles()
+    windows, xi = plan.x_windows()
+    xi = jnp.asarray(xi)
+    zf, zi = plan.z_tables()
+    z_at = gz_at * plan.ta + ta_at
+    zf, zi = pick(zf, z_at), pick(zi, z_at)
+    plain, weighted = plan.t_tables(False), plan.t_tables(True)
+    perm = jnp.asarray(plan.pair_rows())
+    unit = jnp.eye(2 * plan.ta * LANE, dtype=jnp.bfloat16)
+    here = ta_at.astype(jnp.int32).reshape(1)
+    half = plan.rows // 2
+    eye = jnp.eye(half, dtype=jnp.bfloat16)
+    kron = lambda m: (m[:, None, :, None] * eye[None, :, None, :]).reshape(WIDTH * half, WIDTH * half)
+    mix_out, mix_in = kron(point_weight.T), kron(point_weight)
+    flat = (plan.depth, plan.grid_rows, plan.rows, LX)
+    field, cotangent = field.reshape(flat), cotangent.reshape(flat)
+    weights = jnp.transpose(spectral_weight, (0, 1, 4, 5, 3, 2))
+    weights = weights.reshape(plan.kz, MT * WIDTH * WIDTH * 2, plan.owned)
+
+    def swap(a, axis):
+        return lax.ppermute(a, axis, [(0, 1), (1, 0)])
+
+    def shift(a, k):
+        return lax.ppermute(a, "gz", [(d, (d + k) % plan.gz) for d in range(plan.gz)])
+
+    def outward(own, other, table):
+        keep, send = time_forward(plan, own, swap(other, "col"), table)
+        total = (keep.astype(jnp.float32) + swap(send, "ta").astype(jnp.float32)).astype(jnp.bfloat16)
+        return [total[0]] + [shift(total[k], k) for k in range(1, plan.gz)]
+
+    def collect(pieces):
+        keep, send = depth_forward(plan, pieces, zf)
+        return keep, swap(send, "ta")
+
+    def inward(keep, send, table):
+        pieces = depth_inverse(plan, keep, swap(send, "ta"), zi, chunks)
+        out = []
+        for chunk in pieces:
+            mine = jnp.stack([chunk[0]] + [shift(chunk[k], -k) for k in range(1, plan.gz)])
+            own = time_inverse(plan, mine, swap(mine, "ta"), table)
+            out.append((own, swap(own, "col")))
+        return out
+
+    t_fwd, t_inv = (pick(t, ta_at) for t in plain)
+    tw_fwd, tw_inv = (pick(t, ta_at) for t in weighted)
+
+    pieces = []
+    for n in range(chunks):
+        own, other = analyse_xy(plan, tiles, field, ty, n * zc, zc)
+        pieces.append(outward(own, other, t_fwd))
+    spec = collect(pieces)
+    mixed = mix_modes(plan, spec, weights, here, perm, unit)
+    planes = inward(*mixed, tw_inv)
+    pieces, gprime = [], []
+    for n in range(chunks):
+        g, own, other = field_pass(
+            plan, tiles, windows, *planes[n], field, mix_out, ty, ty_inv, xi, n * zc, zc,
+            cot=cotangent, bias=point_bias,
+        )
+        gprime.append(g)
+        pieces.append(outward(own, other, tw_fwd))
+    grad = collect(pieces)
+    back = back_modes(plan, grad, weights, here, perm)
+    planes = inward(*back, t_inv)
+    weight_grad = weight_modes(plan, spec, grad, here, perm, unit)
+    full = None
+    for n in range(chunks):
+        full = field_pass(
+            plan, tiles, windows, *planes[n], gprime[n], mix_in, ty, ty_inv, xi, n * zc, zc, full=full
+        )
+    input_grad = full.reshape(plan.depth, plan.steps, WIDTH, plan.rows, LX)
+    weight_grad = weight_grad.reshape(plan.kz, MT, WIDTH, WIDTH, 2, plan.owned)
+    return input_grad, jnp.transpose(weight_grad, (0, 1, 5, 4, 2, 3))
+
+
+def per_device(mesh, field, cotangent, spectral_weight, point_weight, point_bias):
+    args = (field, cotangent, spectral_weight, point_weight, point_bias)
+    depth, steps, _, rows, _ = field.shape
+    plan = Plan(mesh, depth, steps, rows)
+    fits = (
+        plan.col == 2
+        and plan.ta == 2
+        and plan.owned % MX == 0
+        and plan.owned % GROUP == 0
+        and steps % 4 == 0
+        and rows == 32
+        and plan.kt * WIDTH <= LANE
+        and depth % CHUNKS == 0
+    )
+    if fits:
+        return direct_device(plan, *args)
+    return general_device(*args)
+
+
 def solution(mesh):
     placed = (
         P(("groups", "gz"), "ta", None, "col", None),
@@ -169,7 +853,7 @@
         P(),
     )
     return jax.shard_map(
-        per_device,
+        functools.partial(per_device, mesh),
         mesh=mesh,
         in_specs=placed,
         out_specs=(

time: 1260 us -> 493 us (0.39)
  local copies, waits for them, and re-layouts: 349 us -> 53.5 us
  waiting for transfers between devices: 390 us -> 110 us
  Pallas kernels: 0 us -> 259 us
  matrix products: 225 us -> 0 us
  blocking collectives: 168 us -> 0 us
  other arithmetic: 87.4 us -> 7.72 us
  starting transfers between devices: 19.4 us -> 58.5 us
  between operations: 14.9 us -> 0.96 us
    all_to_all x4 -> x0, waiting for transfers between devices: 321 us -> none  [the longest x2 248 us: synthesize(): lax.all_to_all(copies, ('gz', 'col'), split_axis=0, concat_axis=5, tiled=...]
    pallas_call x0 -> x21, Pallas kernels: none -> 259 us  [rows_call(): pl.pallas_call(kernel, grid=(grid,), in_specs=specs, out_specs=out_specs,...]
    dot_general x17 -> x0, matrix products: 225 us -> none  [product(): jnp.einsum(pattern, first_op, second_op, preferred_element_type=jnp.float32)]
    all_to_all x4 -> x0, blocking collectives: 168 us -> none  [the longest x1 92.8 us: analyse(): moved = lax.all_to_all(mine, 'gz', split_axis=4, concat_axis=0, tiled=True)]
    convert_element_type x10 -> x0, local copies, waits for them, and re-layouts: 144 us -> none  [the longest x4 85.7 us: analyse(): spread.astype(jnp.bfloat16)]
    ppermute x0 -> x44, waiting for transfers between devices: none -> 110 us  [the longest x20 69.6 us: swap(): return lax.ppermute(a, axis, [(0, 1), (1, 0)])]
    unnamed x4 -> x0, waiting for transfers between devices: 69.7 us -> none
    reshape x6 -> x0, local copies, waits for them, and re-layouts: 67.6 us -> none  [the longest x2 56.1 us: synthesize(): split_pairs = gathered.reshape(depth, steps_here, WIDTH, 2, MY, MX)]
  transfers between devices with their start and end apart: 6 -> 44, of which waited for: 6 -> 19; matrix products, arithmetic and copies ran while one was open for 11% -> 10% of each run, Pallas kernels for 0% -> 36%
where the time goes in v1:
time: 493 us; the launch traced here: 490 us
  Pallas kernels  259 us (53%)
  waiting for transfers between devices  110 us (22%)
  starting transfers between devices  58.5 us (12%)
  local copies, waits for them, and re-layouts  53.5 us (11%)
  other arithmetic  7.72 us (2%)
    pallas_call x21, Pallas kernels, rows_call(): pl.pallas_call(kernel, grid=(grid,), in_specs=specs, out_specs=out_specs,...  259 us
    ppermute x20, waiting for transfers between devices, swap(): return lax.ppermute(a, axis, [(0, 1), (1, 0)])  69.6 us
    ppermute x24, waiting for transfers between devices, shift(): lax.ppermute(a, 'gz', [(d, (d + k) % plan.gz) for d in range(plan.gz)])  40.5 us
    ppermute x24, starting transfers between devices, shift(): lax.ppermute(a, 'gz', [(d, (d + k) % plan.gz) for d in range(plan.gz)])  39.4 us
    ppermute x20, starting transfers between devices, swap(): return lax.ppermute(a, axis, [(0, 1), (1, 0)])  19.1 us
    pallas_call x8, local copies, waits for them, and re-layouts, rows_call(): pl.pallas_call(kernel, grid=(grid,), in_specs=specs, out_specs=out_specs,...  16.9 us
    ppermute x8, local copies, waits for them, and re-layouts, swap(): return lax.ppermute(a, axis, [(0, 1), (1, 0)])  14.2 us
  transfers between devices with their start and end apart: 44, of which 19 were waited for; matrix products, arithmetic and copies ran while one was open for 10% of the time, Pallas kernels for 36%

profile of v1, /device:TPU:0, one launch (start us, length us, event | category | flops | bytes accessed | tf_op | source)
XLA Modules:
  0.0 489.5 jit_solution(9342910188934731489)
XLA Ops:
  3.1 12.5 %analyse_xy.3 = (bf16[4,240,576]{2,1,0:T(8,128)(2,1)}, bf16[4,240,576]{2,1,0:T(8,128)(2,1)}) custom-call(bf16[8,240,32,128]{3,2,1,0:T(8,128)(2,1)} %bitcast.94, bf16[384,256]{1,0:T(8,128)(2,1)} %copy.30.ty_ref.refs_8_, bf16[1536,256]{1,0:T(8,128)(2,1)} %constant.72.clone.refs_0_.refs_9_, bf16[1536,256]{1,0:T(8,128)(2,1)} %constant.73.clone.refs_1_.refs_10_, ...), custom_call_target="tpu_custom_call" | custom-call | flops 96000000000 | bytes 4423680 | tf_op jit(solution)/shard_map/analyse_xy/pallas_call | solution.py:362
  17.7 12.4 %analyse_xy.2 = (bf16[4,240,576]{2,1,0:T(8,128)(2,1)}, bf16[4,240,576]{2,1,0:T(8,128)(2,1)}) custom-call(bf16[8,240,32,128]{3,2,1,0:T(8,128)(2,1)} %bitcast.95, bf16[384,256]{1,0:T(8,128)(2,1)} %copy.30.ty_ref.refs_8_, bf16[1536,256]{1,0:T(8,128)(2,1)} %constant.72.clone.refs_0_.refs_9_, bf16[1536,256]{1,0:T(8,128)(2,1)} %constant.73.clone.refs_1_.refs_10_, ...), custom_call_target="tpu_custom_call" | custom-call | flops 96000000000 | bytes 4423680 | tf_op jit(solution)/shard_map/analyse_xy/pallas_call | solution.py:362
  35.8 4.5 time_forward.5
  44.7 4.5 time_forward.4
  49.2 8.4 %collective-permute-done.6 = bf16[4,4,72,256]{3,2,1,0:T(8,128)(2,1)S(1)} collective-permute-done((bf16[4,4,72,256]{3,2,1,0:T(8,128)(2,1)}, bf16[4,4,72,256]{3,2,1,0:T(8,128)(2,1)S(1)}, u32[]{:S(2)}, u32[]{:S(2)}) %collective-permute-start.6) | collective-permute-done | bytes 589856 | tf_op jit(solution)/shard_map/ppermute | solution.py:773
  58.5 4.2 collective-permute-start.9
  63.6 6.0 %collective-permute-done.1 = bf16[4,4,72,256]{3,2,1,0:T(8,128)(2,1)S(1)} collective-permute-done((bf16[4,4,72,256]{3,2,1,0:T(8,128)(2,1)}, bf16[4,4,72,256]{3,2,1,0:T(8,128)(2,1)S(1)}, u32[]{:S(2)}, u32[]{:S(2)}) %collective-permute-start.1) | collective-permute-done | bytes 589856 | tf_op jit(solution)/shard_map/ppermute | solution.py:773
  78.6 8.5 %collective-permute-done.3.refs_2_ = bf16[4,72,256]{2,1,0:T(8,128)(2,1)S(1)} collective-permute-done((bf16[4,72,256]{2,1,0:T(8,128)(2,1)S(1)}, bf16[4,72,256]{2,1,0:T(8,128)(2,1)S(1)}, u32[]{:S(2)}, u32[]{:S(2)}) %collective-permute-start.3) | collective-permute-done | bytes 147488 | tf_op jit(solution)/shard_map/ppermute | solution.py:776
  93.2 5.9 %collective-permute-done.10.b_ref.xb = bf16[8,72,256]{2,1,0:T(8,128)(2,1)S(1)} collective-permute-done((bf16[8,72,256]{2,1,0:T(8,128)(2,1)}, bf16[8,72,256]{2,1,0:T(8,128)(2,1)S(1)}, u32[]{:S(2)}, u32[]{:S(2)}) %collective-permute-start.10) | collective-permute-done | bytes 294944 | tf_op jit(solution)/shard_map/ppermute | solution.py:773
  99.9 19.7 %mix_modes.1 = (bf16[8,72,256]{2,1,0:T(8,128)(2,1)}, bf16[8,72,256]{2,1,0:T(8,128)(2,1)}) custom-call(s32[1]{0:T(128)} %bitcast.here_ref, bf16[8,72,256]{2,1,0:T(8,128)(2,1)} %get-tuple-element.52.a_ref.xa, bf16[8,72,256]{2,1,0:T(8,128)(2,1)} %copy-done.1, bf16[8,9600,72]{2,1,0:T(8,128)(2,1)} %bitcast.76, bf16[480,512]{1,0:T(8,128)(2,1)} %constant.67.clone.perm_ref, ...), custom_call_target="tpu_custom_call" | custom-call | flops 1000000000 | bytes 1179648 | tf_op jit(solution)/shard_map/mix_modes/pallas_call | solution.py:362
  122.8 4.1 collective-permute-done.11.b_ref
  137.5 6.2 %collective-permute-done.23 = bf16[4,72,256]{2,1,0:T(8,128)(2,1)S(1)} collective-permute-done((bf16[4,72,256]{2,1,0:T(8,128)(2,1)}, bf16[4,72,256]{2,1,0:T(8,128)(2,1)S(1)}, u32[]{:S(2)}, u32[]{:S(2)}) %collective-permute-start.23) | collective-permute-done | bytes 147488 | tf_op jit(solution)/shard_map/ppermute | solution.py:776
  150.4 4.3 collective-permute-done.25.b_ref
  155.5 4.5 time_inverse.5.refs_0_
  168.4 11.0 %collective-permute-done.15.b_ref = bf16[4,4,72,256]{3,2,1,0:T(8,128)(2,1)} collective-permute-done((bf16[4,4,72,256]{3,2,1,0:T(8,128)(2,1)}, bf16[4,4,72,256]{3,2,1,0:T(8,128)(2,1)}, u32[]{:S(2)}, u32[]{:S(2)}) %collective-permute-start.15) | collective-permute-done | bytes 589856 | tf_op jit(solution)/shard_map/ppermute | solution.py:773
  179.4 4.5 time_inverse.4.refs_0_
  187.8 46.8 %slope_pass.3 = (bf16[4,240,32,128]{3,2,1,0:T(8,128)(2,1)}, bf16[4,240,576]{2,1,0:T(8,128)(2,1)}, bf16[4,240,576]{2,1,0:T(8,128)(2,1)}) custom-call(bf16[4,240,576]{2,1,0:T(8,128)(2,1)} %time_inverse.5.refs_0_, bf16[4,240,576]{2,1,0:T(8,128)(2,1)} %copy.43.refs_1_, bf16[8,240,32,128]{3,2,1,0:T(8,128)(2,1)} %bitcast.96, bf16[320,320]{1,0:T(8,128)(2,1)} %mul.42.refs_3_, ...), custom_call_target="tpu_custom_call" | custom-call | flops 280000004096 | bytes 20152320 | tf_op jit(solution)/shard_map/slope_pass/pallas_call | solution.py:362
  239.9 46.7 %slope_pass.2 = (bf16[4,240,32,128]{3,2,1,0:T(8,128)(2,1)}, bf16[4,240,576]{2,1,0:T(8,128)(2,1)}, bf16[4,240,576]{2,1,0:T(8,128)(2,1)}) custom-call(bf16[4,240,576]{2,1,0:T(8,128)(2,1)} %time_inverse.4.refs_0_, bf16[4,240,576]{2,1,0:T(8,128)(2,1)} %copy.38.refs_1_, bf16[8,240,32,128]{3,2,1,0:T(8,128)(2,1)} %bitcast.97, bf16[320,320]{1,0:T(8,128)(2,1)} %mul.42.refs_3_, ...), custom_call_target="tpu_custom_call" | custom-call | flops 280000004096 | bytes 20152320 | tf_op jit(solution)/shard_map/slope_pass/pallas_call | solution.py:362
  291.4 4.4 time_forward.7
  298.8 4.5 time_forward.6
  303.8 8.4 %collective-permute-done.28 = bf16[4,4,72,256]{3,2,1,0:T(8,128)(2,1)S(1)} collective-permute-done((bf16[4,4,72,256]{3,2,1,0:T(8,128)(2,1)}, bf16[4,4,72,256]{3,2,1,0:T(8,128)(2,1)S(1)}, u32[]{:S(2)}, u32[]{:S(2)}) %collective-permute-start.28) | collective-permute-done | bytes 589856 | tf_op jit(solution)/shard_map/ppermute | solution.py:773
  334.8 9.1 %collective-permute-done.20.refs_2_ = bf16[4,72,256]{2,1,0:T(8,128)(2,1)S(1)} collective-permute-done((bf16[4,72,256]{2,1,0:T(8,128)(2,1)S(1)}, bf16[4,72,256]{2,1,0:T(8,128)(2,1)S(1)}, u32[]{:S(2)}, u32[]{:S(2)}) %collective-permute-start.20) | collective-permute-done | bytes 147488 | tf_op jit(solution)/shard_map/ppermute | solution.py:776
  349.1 6.7 %collective-permute-done.32.b_ref.gb = bf16[8,72,256]{2,1,0:T(8,128)(2,1)S(1)} collective-permute-done((bf16[8,72,256]{2,1,0:T(8,128)(2,1)}, bf16[8,72,256]{2,1,0:T(8,128)(2,1)S(1)}, u32[]{:S(2)}, u32[]{:S(2)}) %collective-permute-start.32) | collective-permute-done | bytes 294944 | tf_op jit(solution)/shard_map/ppermute | solution.py:773
  356.5 23.0 %back_modes.1 = (bf16[8,72,256]{2,1,0:T(8,128)(2,1)}, bf16[8,72,256]{2,1,0:T(8,128)(2,1)}) custom-call(s32[1]{0:T(128)} %bitcast.here_ref, bf16[8,72,256]{2,1,0:T(8,128)(2,1)} %get-tuple-element.72.a_ref.ga, bf16[8,72,256]{2,1,0:T(8,128)(2,1)} %copy-done.2, bf16[8,9600,72]{2,1,0:T(8,128)(2,1)} %bitcast.77, bf16[480,512]{1,0:T(8,128)(2,1)} %constant.67.clone.perm_ref), custom_call_target="tpu_custom_call" | custom-call | flops 1000000000 | bytes 1179648 | tf_op jit(solution)/shard_map/back_modes/pallas_call | solution.py:362
  381.1 5.8 %collective-permute-done.33.b_ref = bf16[8,72,256]{2,1,0:T(8,128)(2,1)S(1)} collective-permute-done((bf16[8,72,256]{2,1,0:T(8,128)(2,1)}, bf16[8,72,256]{2,1,0:T(8,128)(2,1)S(1)}, u32[]{:S(2)}, u32[]{:S(2)}) %collective-permute-start.33) | collective-permute-done | bytes 294944 | tf_op jit(solution)/shard_map/ppermute | solution.py:773
  396.5 8.4 %collective-permute-done.40 = bf16[4,72,256]{2,1,0:T(8,128)(2,1)S(1)} collective-permute-done((bf16[4,72,256]{2,1,0:T(8,128)(2,1)}, bf16[4,72,256]{2,1,0:T(8,128)(2,1)S(1)}, u32[]{:S(2)}, u32[]{:S(2)}) %collective-permute-start.40) | collective-permute-done | bytes 147488 | tf_op jit(solution)/shard_map/ppermute | solution.py:776
  411.5 5.0 %collective-permute-done.42.b_ref = bf16[4,4,72,256]{3,2,1,0:T(8,128)(2,1)S(1)} collective-permute-done((bf16[4,4,72,256]{3,2,1,0:T(8,128)(2,1)S(1)}, bf16[4,4,72,256]{3,2,1,0:T(8,128)(2,1)S(1)}, u32[]{:S(2)}, u32[]{:S(2)}) %collective-permute-start.42) | collective-permute-done | bytes 589856 | tf_op jit(solution)/shard_map/ppermute | solution.py:773
  417.3 4.5 time_inverse.7.refs_0_
  429.6 14.4 %weight_modes.1 = bf16[8,9600,72]{2,1,0:T(8,128)(2,1)} custom-call(s32[1]{0:T(128)} %bitcast.here_ref, bf16[8,72,256]{2,1,0:T(8,128)(2,1)} %get-tuple-element.52.a_ref.xa, bf16[8,72,256]{2,1,0:T(8,128)(2,1)} %copy-done.1, bf16[8,72,256]{2,1,0:T(8,128)(2,1)} %get-tuple-element.72.a_ref.ga, bf16[8,72,256]{2,1,0:T(8,128)(2,1)} %copy-done.2, ...), custom_call_target="tpu_custom_call" | custom-call | flops 1000000000 | bytes 22118400 | tf_op jit(solution)/shard_map/weight_modes/pallas_call | solution.py:362
  444.0 4.6 time_inverse.6.refs_0_
  452.6 17.7 %input_pass.2.refs_6_ = bf16[8,240,32,128]{3,2,1,0:T(8,128)(2,1)} custom-call(bf16[4,240,576]{2,1,0:T(8,128)(2,1)} %time_inverse.7.refs_0_, bf16[4,240,576]{2,1,0:T(8,128)(2,1)} %copy.49.refs_1_, bf16[4,240,32,128]{3,2,1,0:T(8,128)(2,1)} %get-tuple-element.85.refs_2_, bf16[320,320]{1,0:T(8,128)(2,1)} %mul.45.refs_3_, ...), custom_call_target="tpu_custom_call" | custom-call | flops 140000002048 | bytes 31457280 | tf_op jit(solution)/shard_map/input_pass/pallas_call | solution.py:362
  471.8 17.8 %input_pass.3 = bf16[8,240,32,128]{3,2,1,0:T(8,128)(2,1)} custom-call(bf16[4,240,576]{2,1,0:T(8,128)(2,1)} %time_inverse.6.refs_0_, bf16[4,240,576]{2,1,0:T(8,128)(2,1)} %copy.50.refs_1_, bf16[4,240,32,128]{3,2,1,0:T(8,128)(2,1)} %get-tuple-element.80.refs_2_, bf16[320,320]{1,0:T(8,128)(2,1)} %mul.45.refs_3_, ...), custom_call_target="tpu_custom_call", output_to_operand_aliasing={{}: (6, {})} | custom-call | flops 140000002048 | bytes 31457280 | tf_op jit(solution)/shard_map/input_pass/pallas_call | solution.py:362
  (187 shorter events, 139.7 us)
Async XLA Ops:
  17.2 16.3 %collective-permute-start.5 = (bf16[4,240,576]{1,2,0:T(8,128)(2,1)S(1)}, bf16[4,240,576]{1,2,0:T(8,128)(2,1)}, u32[]{:S(2)}, u32[]{:S(2)}) collective-permute-start(bf16[4,240,576]{1,2,0:T(8,128)(2,1)S(1)} %copy.34), channel_id=1, source_target_pairs={{0,1},{1,0},{2,3},{3,2},{4,5},{5,4},{6,7},{7,6},{8,9},{9,8},{10,11... | collective-permute-start | bytes 3317768 | tf_op jit(solution)/shard_map/ppermute | solution.py:773
  31.7 11.6 %collective-permute-start = (bf16[4,240,576]{1,2,0:T(8,128)(2,1)S(1)}, bf16[4,240,576]{1,2,0:T(8,128)(2,1)S(1)}, u32[]{:S(2)}, u32[]{:S(2)}) collective-permute-start(bf16[4,240,576]{1,2,0:T(8,128)(2,1)S(1)} %copy.31), channel_id=1, source_target_pairs={{0,1},{1,0},{2,3},{3,2},{4,5},{5,4},{6,7},{7,6},{8,9},{9,8},{10,11... | collective-permute-start | bytes 3317768 | tf_op jit(solution)/shard_map/ppermute | solution.py:773
  40.3 17.3 %collective-permute-start.6 = (bf16[4,4,72,256]{3,2,1,0:T(8,128)(2,1)}, bf16[4,4,72,256]{3,2,1,0:T(8,128)(2,1)S(1)}, u32[]{:S(2)}, u32[]{:S(2)}) collective-permute-start(bf16[4,4,72,256]{3,2,1,0:T(8,128)(2,1)} %get-tuple-element.51), channel_id=1, source_target_pairs={{0,2},{2,0},{1,3},{3,1},{4,6},{6,4},{5,7},{7,5},{8,10},{10,8},{9,1... | collective-permute-start | bytes 1769480 | tf_op jit(solution)/shard_map/ppermute | solution.py:773
  49.2 20.5 %collective-permute-start.1 = (bf16[4,4,72,256]{3,2,1,0:T(8,128)(2,1)}, bf16[4,4,72,256]{3,2,1,0:T(8,128)(2,1)S(1)}, u32[]{:S(2)}, u32[]{:S(2)}) collective-permute-start(bf16[4,4,72,256]{3,2,1,0:T(8,128)(2,1)} %get-tuple-element.47), channel_id=1, source_target_pairs={{0,2},{2,0},{1,3},{3,1},{4,6},{6,4},{5,7},{7,5},{8,10},{10,8},{9,1... | collective-permute-start | bytes 1769480 | tf_op jit(solution)/shard_map/ppermute | solution.py:773
  58.5 15.9 %collective-permute-start.9 = (bf16[4,72,256]{2,1,0:T(8,128)(2,1)S(1)}, bf16[4,72,256]{2,1,0:T(8,128)(2,1)S(1)}, u32[]{:S(2)}, u32[]{:S(2)}) collective-permute-start(bf16[4,72,256]{2,1,0:T(8,128)(2,1)S(1)} %get-tuple-element.96), channel_id=1, source_target_pairs={{0,12},{4,0},{8,4},{12,8},{1,13},{5,1},{9,5},{13,9},{2,14},{6,2},{... | collective-permute-start | bytes 442376 | tf_op jit(solution)/shard_map/ppermute | solution.py:776
  62.6 14.4 %collective-permute-start.8 = (bf16[4,72,256]{2,1,0:T(8,128)(2,1)S(1)}, bf16[4,72,256]{2,1,0:T(8,128)(2,1)S(1)}, u32[]{:S(2)}, u32[]{:S(2)}) collective-permute-start(bf16[4,72,256]{2,1,0:T(8,128)(2,1)S(1)} %get-tuple-element.97), channel_id=1, source_target_pairs={{0,8},{4,12},{8,0},{12,4},{1,9},{5,13},{9,1},{13,5},{2,10},{6,14},... | collective-permute-start | bytes 442376 | tf_op jit(solution)/shard_map/ppermute | solution.py:776
  62.6 14.4 %collective-permute-start.7 = (bf16[4,72,256]{2,1,0:T(8,128)(2,1)S(1)}, bf16[4,72,256]{2,1,0:T(8,128)(2,1)S(1)}, u32[]{:S(2)}, u32[]{:S(2)}) collective-permute-start(bf16[4,72,256]{2,1,0:T(8,128)(2,1)S(1)} %get-tuple-element.98), channel_id=1, source_target_pairs={{0,4},{4,8},{8,12},{12,0},{1,5},{5,9},{9,13},{13,1},{2,6},{6,10},{... | collective-permute-start | bytes 442376 | tf_op jit(solution)/shard_map/ppermute | solution.py:776
  74.3 12.8 %collective-permute-start.3 = (bf16[4,72,256]{2,1,0:T(8,128)(2,1)S(1)}, bf16[4,72,256]{2,1,0:T(8,128)(2,1)S(1)}, u32[]{:S(2)}, u32[]{:S(2)}) collective-permute-start(bf16[4,72,256]{2,1,0:T(8,128)(2,1)S(1)} %get-tuple-element.101), channel_id=1, source_target_pairs={{0,8},{4,12},{8,0},{12,4},{1,9},{5,13},{9,1},{13,5},{2,10},{6,14},... | collective-permute-start | bytes 442376 | tf_op jit(solution)/shard_map/ppermute | solution.py:776
  74.3 12.8 %collective-permute-start.2 = (bf16[4,72,256]{2,1,0:T(8,128)(2,1)S(1)}, bf16[4,72,256]{2,1,0:T(8,128)(2,1)S(1)}, u32[]{:S(2)}, u32[]{:S(2)}) collective-permute-start(bf16[4,72,256]{2,1,0:T(8,128)(2,1)S(1)} %get-tuple-element.102), channel_id=1, source_target_pairs={{0,4},{4,8},{8,12},{12,0},{1,5},{5,9},{9,13},{13,1},{2,6},{6,10},{... | collective-permute-start | bytes 442376 | tf_op jit(solution)/shard_map/ppermute | solution.py:776
  130.6 13.1 %collective-permute-start.23 = (bf16[4,72,256]{2,1,0:T(8,128)(2,1)}, bf16[4,72,256]{2,1,0:T(8,128)(2,1)S(1)}, u32[]{:S(2)}, u32[]{:S(2)}) collective-permute-start(bf16[4,72,256]{2,1,0:T(8,128)(2,1)} %get-tuple-element.66), channel_id=1, source_target_pairs={{0,8},{4,12},{8,0},{12,4},{1,9},{5,13},{9,1},{13,5},{2,10},{6,14},... | collective-permute-start | bytes 442376 | tf_op jit(solution)/shard_map/ppermute | solution.py:776
  147.2 15.2 %collective-permute-start.12 = (bf16[4,72,256]{2,1,0:T(8,128)(2,1)S(1)}, bf16[4,72,256]{2,1,0:T(8,128)(2,1)S(1)}, u32[]{:S(2)}, u32[]{:S(2)}) collective-permute-start(bf16[4,72,256]{2,1,0:T(8,128)(2,1)S(1)} %copy-done.25), channel_id=1, source_target_pairs={{0,12},{4,0},{8,4},{12,8},{1,13},{5,1},{9,5},{13,9},{2,14},{6,2},{... | collective-permute-start | bytes 442376 | tf_op jit(solution)/shard_map/ppermute | solution.py:776
  147.3 15.1 %collective-permute-start.13 = (bf16[4,72,256]{2,1,0:T(8,128)(2,1)S(1)}, bf16[4,72,256]{2,1,0:T(8,128)(2,1)S(1)}, u32[]{:S(2)}, u32[]{:S(2)}) collective-permute-start(bf16[4,72,256]{2,1,0:T(8,128)(2,1)S(1)} %copy-done.23), channel_id=1, source_target_pairs={{0,8},{4,12},{8,0},{12,4},{1,9},{5,13},{9,1},{13,5},{2,10},{6,14},... | collective-permute-start | bytes 442376 | tf_op jit(solution)/shard_map/ppermute | solution.py:776
  148.4 14.0 %collective-permute-start.14 = (bf16[4,72,256]{2,1,0:T(8,128)(2,1)S(1)}, bf16[4,72,256]{2,1,0:T(8,128)(2,1)S(1)}, u32[]{:S(2)}, u32[]{:S(2)}) collective-permute-start(bf16[4,72,256]{2,1,0:T(8,128)(2,1)S(1)} %copy-done.22), channel_id=1, source_target_pairs={{0,4},{4,8},{8,12},{12,0},{1,5},{5,9},{9,13},{13,1},{2,6},{6,10},{... | collective-permute-start | bytes 442376 | tf_op jit(solution)/shard_map/ppermute | solution.py:776
  162.4 23.9 %collective-permute-start.26 = (bf16[4,240,576]{1,2,0:T(8,128)(2,1)}, bf16[4,240,576]{1,2,0:T(8,128)(2,1)S(1)}, u32[]{:S(2)}, u32[]{:S(2)}) collective-permute-start(bf16[4,240,576]{1,2,0:T(8,128)(2,1)} %copy.42), channel_id=1, source_target_pairs={{0,1},{1,0},{2,3},{3,2},{4,5},{5,4},{6,7},{7,6},{8,9},{9,8},{10,11... | collective-permute-start | bytes 3317768 | tf_op jit(solution)/shard_map/ppermute | solution.py:773
  163.4 16.0 %collective-permute-start.15 = (bf16[4,4,72,256]{3,2,1,0:T(8,128)(2,1)}, bf16[4,4,72,256]{3,2,1,0:T(8,128)(2,1)}, u32[]{:S(2)}, u32[]{:S(2)}) collective-permute-start(bf16[4,4,72,256]{3,2,1,0:T(8,128)(2,1)} %pad_maximum_fusion.a_ref), channel_id=1, source_target_pairs={{0,2},{2,0},{1,3},{3,1},{4,6},{6,4},{5,7},{7,5},{8,10},{10,8},{9,1... | collective-permute-start | bytes 1769480 | tf_op jit(solution)/shard_map/ppermute | solution.py:773
  186.3 51.2 %collective-permute-start.16 = (bf16[4,240,576]{1,2,0:T(8,128)(2,1)}, bf16[4,240,576]{1,2,0:T(8,128)(2,1)}, u32[]{:S(2)}, u32[]{:S(2)}) collective-permute-start(bf16[4,240,576]{1,2,0:T(8,128)(2,1)} %copy.36), channel_id=1, source_target_pairs={{0,1},{1,0},{2,3},{3,2},{4,5},{5,4},{6,7},{7,6},{8,9},{9,8},{10,11... | collective-permute-start | bytes 3317768 | tf_op jit(solution)/shard_map/ppermute | solution.py:773
  237.0 52.1 %collective-permute-start.27 = (bf16[4,240,576]{1,2,0:T(8,128)(2,1)}, bf16[4,240,576]{1,2,0:T(8,128)(2,1)}, u32[]{:S(2)}, u32[]{:S(2)}) collective-permute-start(bf16[4,240,576]{1,2,0:T(8,128)(2,1)} %copy.45), channel_id=1, source_target_pairs={{0,1},{1,0},{2,3},{3,2},{4,5},{5,4},{6,7},{7,6},{8,9},{9,8},{10,11... | collective-permute-start | bytes 3317768 | tf_op jit(solution)/shard_map/ppermute | solution.py:773
  295.9 16.3 %collective-permute-start.28 = (bf16[4,4,72,256]{3,2,1,0:T(8,128)(2,1)}, bf16[4,4,72,256]{3,2,1,0:T(8,128)(2,1)S(1)}, u32[]{:S(2)}, u32[]{:S(2)}) collective-permute-start(bf16[4,4,72,256]{3,2,1,0:T(8,128)(2,1)} %get-tuple-element.71), channel_id=1, source_target_pairs={{0,2},{2,0},{1,3},{3,1},{4,6},{6,4},{5,7},{7,5},{8,10},{10,8},{9,1... | collective-permute-start | bytes 1769480 | tf_op jit(solution)/shard_map/ppermute | solution.py:773
  303.4 21.0 %collective-permute-start.18 = (bf16[4,4,72,256]{3,2,1,0:T(8,128)(2,1)}, bf16[4,4,72,256]{3,2,1,0:T(8,128)(2,1)S(1)}, u32[]{:S(2)}, u32[]{:S(2)}) collective-permute-start(bf16[4,4,72,256]{3,2,1,0:T(8,128)(2,1)} %get-tuple-element.63), channel_id=1, source_target_pairs={{0,2},{2,0},{1,3},{3,1},{4,6},{6,4},{5,7},{7,5},{8,10},{10,8},{9,1... | collective-permute-start | bytes 1769480 | tf_op jit(solution)/shard_map/ppermute | solution.py:773
  313.1 17.5 %collective-permute-start.31 = (bf16[4,72,256]{2,1,0:T(8,128)(2,1)S(1)}, bf16[4,72,256]{2,1,0:T(8,128)(2,1)S(1)}, u32[]{:S(2)}, u32[]{:S(2)}) collective-permute-start(bf16[4,72,256]{2,1,0:T(8,128)(2,1)S(1)} %get-tuple-element.88), channel_id=1, source_target_pairs={{0,12},{4,0},{8,4},{12,8},{1,13},{5,1},{9,5},{13,9},{2,14},{6,2},{... | collective-permute-start | bytes 442376 | tf_op jit(solution)/shard_map/ppermute | solution.py:776
  316.1 16.5 %collective-permute-start.30 = (bf16[4,72,256]{2,1,0:T(8,128)(2,1)S(1)}, bf16[4,72,256]{2,1,0:T(8,128)(2,1)S(1)}, u32[]{:S(2)}, u32[]{:S(2)}) collective-permute-start(bf16[4,72,256]{2,1,0:T(8,128)(2,1)S(1)} %get-tuple-element.89), channel_id=1, source_target_pairs={{0,8},{4,12},{8,0},{12,4},{1,9},{5,13},{9,1},{13,5},{2,10},{6,14},... | collective-permute-start | bytes 442376 | tf_op jit(solution)/shard_map/ppermute | solution.py:776
  318.4 14.2 %collective-permute-start.29 = (bf16[4,72,256]{2,1,0:T(8,128)(2,1)S(1)}, bf16[4,72,256]{2,1,0:T(8,128)(2,1)S(1)}, u32[]{:S(2)}, u32[]{:S(2)}) collective-permute-start(bf16[4,72,256]{2,1,0:T(8,128)(2,1)S(1)} %get-tuple-element.90), channel_id=1, source_target_pairs={{0,4},{4,8},{8,12},{12,0},{1,5},{5,9},{9,13},{13,1},{2,6},{6,10},{... | collective-permute-start | bytes 442376 | tf_op jit(solution)/shard_map/ppermute | solution.py:776
  328.3 15.5 %collective-permute-start.20 = (bf16[4,72,256]{2,1,0:T(8,128)(2,1)S(1)}, bf16[4,72,256]{2,1,0:T(8,128)(2,1)S(1)}, u32[]{:S(2)}, u32[]{:S(2)}) collective-permute-start(bf16[4,72,256]{2,1,0:T(8,128)(2,1)S(1)} %get-tuple-element.93), channel_id=1, source_target_pairs={{0,8},{4,12},{8,0},{12,4},{1,9},{5,13},{9,1},{13,5},{2,10},{6,14},... | collective-permute-start | bytes 442376 | tf_op jit(solution)/shard_map/ppermute | solution.py:776
  330.6 13.2 %collective-permute-start.19 = (bf16[4,72,256]{2,1,0:T(8,128)(2,1)S(1)}, bf16[4,72,256]{2,1,0:T(8,128)(2,1)S(1)}, u32[]{:S(2)}, u32[]{:S(2)}) collective-permute-start(bf16[4,72,256]{2,1,0:T(8,128)(2,1)S(1)} %get-tuple-element.94), channel_id=1, source_target_pairs={{0,4},{4,8},{8,12},{12,0},{1,5},{5,9},{9,13},{13,1},{2,6},{6,10},{... | collective-permute-start | bytes 442376 | tf_op jit(solution)/shard_map/ppermute | solution.py:776
  390.6 14.3 %collective-permute-start.40 = (bf16[4,72,256]{2,1,0:T(8,128)(2,1)}, bf16[4,72,256]{2,1,0:T(8,128)(2,1)S(1)}, u32[]{:S(2)}, u32[]{:S(2)}) collective-permute-start(bf16[4,72,256]{2,1,0:T(8,128)(2,1)} %get-tuple-element.83), channel_id=1, source_target_pairs={{0,8},{4,12},{8,0},{12,4},{1,9},{5,13},{9,1},{13,5},{2,10},{6,14},... | collective-permute-start | bytes 442376 | tf_op jit(solution)/shard_map/ppermute | solution.py:776
  392.9 12.0 %collective-permute-start.41 = (bf16[4,72,256]{2,1,0:T(8,128)(2,1)}, bf16[4,72,256]{2,1,0:T(8,128)(2,1)S(1)}, u32[]{:S(2)}, u32[]{:S(2)}) collective-permute-start(bf16[4,72,256]{2,1,0:T(8,128)(2,1)} %get-tuple-element.84), channel_id=1, source_target_pairs={{0,4},{4,8},{8,12},{12,0},{1,5},{5,9},{9,13},{13,1},{2,6},{6,10},{... | collective-permute-start | bytes 442376 | tf_op jit(solution)/shard_map/ppermute | solution.py:776
  408.3 16.0 %collective-permute-start.34 = (bf16[4,72,256]{2,1,0:T(8,128)(2,1)}, bf16[4,72,256]{2,1,0:T(8,128)(2,1)S(1)}, u32[]{:S(2)}, u32[]{:S(2)}) collective-permute-start(bf16[4,72,256]{2,1,0:T(8,128)(2,1)} %get-tuple-element.77), channel_id=1, source_target_pairs={{0,12},{4,0},{8,4},{12,8},{1,13},{5,1},{9,5},{13,9},{2,14},{6,2},{... | collective-permute-start | bytes 442376 | tf_op jit(solution)/shard_map/ppermute | solution.py:776
  408.4 16.0 %collective-permute-start.35 = (bf16[4,72,256]{2,1,0:T(8,128)(2,1)}, bf16[4,72,256]{2,1,0:T(8,128)(2,1)}, u32[]{:S(2)}, u32[]{:S(2)}) collective-permute-start(bf16[4,72,256]{2,1,0:T(8,128)(2,1)} %get-tuple-element.78), channel_id=1, source_target_pairs={{0,8},{4,12},{8,0},{12,4},{1,9},{5,13},{9,1},{13,5},{2,10},{6,14},... | collective-permute-start | bytes 442376 | tf_op jit(solution)/shard_map/ppermute | solution.py:776
  409.5 14.9 %collective-permute-start.36 = (bf16[4,72,256]{2,1,0:T(8,128)(2,1)}, bf16[4,72,256]{2,1,0:T(8,128)(2,1)}, u32[]{:S(2)}, u32[]{:S(2)}) collective-permute-start(bf16[4,72,256]{2,1,0:T(8,128)(2,1)} %get-tuple-element.79), channel_id=1, source_target_pairs={{0,4},{4,8},{8,12},{12,0},{1,5},{5,9},{9,13},{13,1},{2,6},{6,10},{... | collective-permute-start | bytes 442376 | tf_op jit(solution)/shard_map/ppermute | solution.py:776
  424.4 26.8 %collective-permute-start.43 = (bf16[4,240,576]{1,2,0:T(8,128)(2,1)}, bf16[4,240,576]{1,2,0:T(8,128)(2,1)S(1)}, u32[]{:S(2)}, u32[]{:S(2)}) collective-permute-start(bf16[4,240,576]{1,2,0:T(8,128)(2,1)} %copy.48), channel_id=1, source_target_pairs={{0,1},{1,0},{2,3},{3,2},{4,5},{5,4},{6,7},{7,6},{8,9},{9,8},{10,11... | collective-permute-start | bytes 3317768 | tf_op jit(solution)/shard_map/ppermute | solution.py:773
  426.3 17.8 %collective-permute-start.37 = (bf16[4,4,72,256]{3,2,1,0:T(8,128)(2,1)}, bf16[4,4,72,256]{3,2,1,0:T(8,128)(2,1)}, u32[]{:S(2)}, u32[]{:S(2)}) collective-permute-start(bf16[4,4,72,256]{3,2,1,0:T(8,128)(2,1)} %pad_maximum_fusion.2.a_ref), channel_id=1, source_target_pairs={{0,2},{2,0},{1,3},{3,1},{4,6},{6,4},{5,7},{7,5},{8,10},{10,8},{9,1... | collective-permute-start | bytes 1769480 | tf_op jit(solution)/shard_map/ppermute | solution.py:773
  451.0 19.4 %collective-permute-start.38 = (bf16[4,240,576]{1,2,0:T(8,128)(2,1)}, bf16[4,240,576]{1,2,0:T(8,128)(2,1)S(1)}, u32[]{:S(2)}, u32[]{:S(2)}) collective-permute-start(bf16[4,240,576]{1,2,0:T(8,128)(2,1)} %copy.47), channel_id=1, source_target_pairs={{0,1},{1,0},{2,3},{3,2},{4,5},{5,4},{6,7},{7,6},{8,9},{9,8},{10,11... | collective-permute-start | bytes 3317768 | tf_op jit(solution)/shard_map/ppermute | solution.py:773
  (46 other events, 369.5 us)

commit v2 on v1

--- a/solution.py
+++ b/solution.py
@@ -23,6 +23,13 @@
 LANE = 128
 GROUP = 8
 CHUNKS = 2
+SHIFTS = True
+PARTS = 1
+UNROLL = 4
+COST = 0.1
+WEIGHT_SIZES = (8,)
+WHOLE = True
+ORDERED = False
 
 
 def wave_parts(length, mode_count, halfband):
@@ -183,6 +190,10 @@
     return np.asarray(table, dtype=np.float32).astype(ml_dtypes.bfloat16)
 
 
+def place(own, k, count):
+    return (own + k) % count if SHIFTS else abs(k)
+
+
 class Plan:
     def __init__(self, mesh, depth, steps, rows):
         self.gz, self.ta, self.col = mesh.shape["gz"], mesh.shape["ta"], mesh.shape["col"]
@@ -191,6 +202,7 @@
         self.ky_own = self.owned // MX
         self.ky_half = MY // self.col
         self.lanes = self.ky_half * 2 * MX
+        self.wide = (self.lanes + LANE - 1) // LANE * LANE
         self.half_pairs = self.ky_half * MX
         self.kt = MT // self.ta
         self.kz = MZ // self.ta
@@ -202,7 +214,7 @@
         for a in range(self.gz):
             for b in range(self.col):
                 order = [
-                    self.ky_own * (self.col * ((a + k) % self.gz) + (b ^ h)) + j
+                    self.ky_own * (self.col * place(a, k, self.gz) + (b ^ h)) + j
                     for h in range(self.col)
                     for k in range(self.gz)
                     for j in range(self.ky_own)
@@ -274,7 +286,7 @@
         freq = np.array(signed(MZ))
         for a in range(self.gz):
             places = np.concatenate(
-                [np.arange(self.depth) + (a - k) % self.gz * self.depth for k in range(self.gz)]
+                [np.arange(self.depth) + place(a, -k, self.gz) * self.depth for k in range(self.gz)]
             )
             for b in range(self.ta):
                 for h in range(self.ta):
@@ -311,7 +323,9 @@
 
 def slope_of(v):
     e = jnp.exp(-0.5 * v * v)
-    t = 1.0 / (1.0 + (0.3275911 / math.sqrt(2.0)) * jnp.abs(v))
+    d = 1.0 + (0.3275911 / math.sqrt(2.0)) * jnp.abs(v)
+    t = pl.reciprocal(d, approx=True)
+    t = t * (2.0 - d * t)
     poly = t * (
         0.5 * 0.254829592
         + t
@@ -323,12 +337,6 @@
     tail = poly * e
     cdf = jnp.where(v >= 0.0, 1.0 - tail, tail)
     return cdf + v * e * (1.0 / math.sqrt(2.0 * math.pi))
-
-
-def params(steps=1):
-    return pltpu.CompilerParams(
-        vmem_limit_bytes=56 << 20, dimension_semantics=("arbitrary",) * steps
-    )
 
 
 def whole_block(a):
@@ -357,56 +365,83 @@
             outs[h][0, :, low:high] = o.astype(jnp.bfloat16)
 
 
-def rows_call(kernel, n, plan, grid, inputs, specs, out_shapes, out_specs, scratch, aliases, flops):
-    size = sum(math.prod(s.shape) * 2 for s in out_shapes)
+def rows_call(kernel, n, ids, grid, inputs, specs, out_shapes, out_specs, scratch, us, after=(), aliases=None, vmem=24):
+    count, skip = len(inputs), len(after)
+    any_spec = pl.BlockSpec(memory_space=pl.ANY)
+
+    def body(ids_ref, *refs):
+        kernel(ids_ref, *refs[:count], *refs[count + skip :])
+
     return pl.pallas_call(
-        kernel,
-        grid=(grid,),
-        in_specs=specs,
-        out_specs=out_specs,
+        body,
+        grid_spec=pltpu.PrefetchScalarGridSpec(
+            num_scalar_prefetch=1,
+            grid=(grid,),
+            in_specs=list(specs) + [any_spec] * skip,
+            out_specs=out_specs,
+            scratch_shapes=scratch,
+        ),
         out_shape=out_shapes,
-        scratch_shapes=scratch,
-        input_output_aliases=aliases,
-        compiler_params=params(),
+        input_output_aliases=aliases or {},
+        compiler_params=pltpu.CompilerParams(vmem_limit_bytes=vmem << 20),
         name=n,
         cost_estimate=pl.CostEstimate(
-            flops=int(flops), bytes_accessed=int(size * 2), transcendentals=0
+            flops=int(us * COST * 1.1e9), bytes_accessed=int(us * COST * 1e6), transcendentals=0
         ),
-    )(*inputs)
-
-
-def analyse_xy(plan, tiles, field, ty, z0, zc):
-    def kernel(f, ty_ref, *refs):
+    )(ids, *inputs, *after)
+
+
+def pick_block(a, which):
+    return pl.BlockSpec((None,) + a.shape[1:], lambda z, ids, n=a.ndim: (ids[which],) + (0,) * (n - 1))
+
+
+def repeat_rows(m, count):
+    n, bits = WIDTH * count, count.bit_length() - 1
+    iota = lambda shape, axis: lax.broadcasted_iota(jnp.int32, shape, axis)
+    up = lax.shift_right_logical(iota((n, WIDTH), 0), bits) == iota((n, WIDTH), 1)
+    up = up.astype(jnp.float32).astype(jnp.bfloat16)
+    full = dot_nt(dot(up, m).astype(jnp.bfloat16), up)
+    same = ((iota((n, n), 0) ^ iota((n, n), 1)) & (count - 1)) == 0
+    return jnp.where(same, full, 0.0).astype(jnp.bfloat16)
+
+
+def analyse_xy(plan, ids, tiles, field, ty, z0, zc, at, count, after, prev):
+    def kernel(ids_ref, f, ty_ref, *refs):
         tables, outs, us = refs[: len(tiles)], refs[len(tiles) : -1], refs[-1]
         step = 5 * 2 * GROUP
+
         def body(i, carry):
             spread_y(plan, f, i * step, step, ty_ref[...], us)
             return carry
+
         lax.fori_loop(0, plan.grid_rows // step, body, 0)
         gather_x(plan, tiles, us, tables, outs)
 
     tabs = [jnp.asarray(t[3]) for t in tiles]
-    out = jax.ShapeDtypeStruct((zc, plan.grid_rows, plan.lanes), jnp.bfloat16)
-    block = pl.BlockSpec((1, plan.grid_rows, plan.lanes), lambda z: (z, 0, 0))
-    fspec = pl.BlockSpec((1, plan.grid_rows, plan.rows, LX), lambda z: (z0 + z, 0, 0, 0))
+    out = jax.ShapeDtypeStruct((zc, plan.grid_rows, plan.wide), jnp.bfloat16)
+    block = pl.BlockSpec((1, plan.grid_rows, plan.wide), lambda z, ids: (at + z, 0, 0))
+    fspec = pl.BlockSpec((1, plan.grid_rows, plan.rows, LX), lambda z, ids: (z0 + at + z, 0, 0, 0))
+    aliases = {1 + 2 + len(tabs) + i: i for i in range(len(prev))}
     return rows_call(
-        kernel, "analyse_xy", plan, zc, [field, ty, *tabs],
-        [fspec, whole_block(ty)] + [whole_block(t) for t in tabs],
+        kernel, "analyse_xy", ids, count, [field, ty, *tabs],
+        [fspec, pick_block(ty, 0)] + [whole_block(t) for t in tabs],
         [out, out], [block, block],
-        [pltpu.VMEM((2 * MY, plan.grid_rows, LX), jnp.bfloat16)], {}, zc * 24e9,
-    )
-
-
-def field_pass(plan, tiles, windows, own, other, field, mixer, ty, ty_inv, xi, z0, zc, cot=None, bias=None, full=None):
+        [pltpu.VMEM((2 * MY, plan.grid_rows, LX), jnp.bfloat16)], 2.8 * count, [*prev, *after], aliases, 52,
+    )
+
+
+def field_pass(plan, ids, tiles, windows, own, other, field, point, ty, ty_inv, xi, z0, zc, at, count, after, prev, cot=None, bias=None):
     first = cot is not None
     tabs = [jnp.asarray(t[3]) for t in tiles] if first else []
     block_rows = 4 * WIDTH
     half = plan.rows // 2
-
-    def kernel(*refs):
+    pair = 2 * GROUP
+    at0 = at
+
+    def kernel(ids_ref, *refs):
         refs = list(refs)
         s_refs = (refs.pop(0), refs.pop(0))
-        f, mix, tyi, xi_ref = refs.pop(0), refs.pop(0), refs.pop(0), refs.pop(0)
+        f, point_ref, tyi, xi_ref = refs.pop(0), refs.pop(0), refs.pop(0), refs.pop(0)
         if first:
             c_ref, bias_ref, ty_ref = refs.pop(0), refs.pop(0), refs.pop(0)
             tables = [refs.pop(0) for _ in tabs]
@@ -414,46 +449,58 @@
             outs = (refs.pop(0), refs.pop(0))
             us = refs.pop()
         else:
-            if full is not None:
-                refs.pop(0)
             g_out = refs.pop(0)
-        ws, pre = refs
+        ws, pre, mix = refs
+
+        @pl.when(pl.program_id(0) == 0)
+        def _():
+            mix[...] = repeat_rows(point_ref[...], half)
+
+        z = at0 + pl.program_id(0) if WHOLE else 0
         for h in range(plan.col):
             for k in range(plan.ky_half):
                 low, high = windows[k]
-                w = dot(s_refs[h][0, :, low:high], xi_ref[k, : high - low])
+                w = dot(s_refs[h][z, :, low:high], xi_ref[k, : high - low])
                 ws[h * plan.ky_half + k] = w[:, :LX]
                 ws[MY + h * plan.ky_half + k] = w[:, LX:]
 
         def block(i, carry):
             base = pl.multiple_of(i * block_rows, block_rows)
-            for q in range(block_rows // (2 * GROUP)):
-                g = pl.multiple_of(base + q * 2 * GROUP, GROUP)
-                a = ws[:, pl.ds(g, GROUP), :].reshape(2 * MY * GROUP, LX).astype(jnp.bfloat16)
-                b = ws[:, pl.ds(g + GROUP, GROUP), :].reshape(2 * MY * GROUP, LX).astype(jnp.bfloat16)
-                o = dot(tyi[...], jnp.concatenate([a, b], 1))
-                at = q * 2 * GROUP
-                pre[at : at + GROUP] = o[:, :LX].reshape(GROUP, plan.rows, LX)
-                pre[at + GROUP : at + 2 * GROUP] = o[:, LX:].reshape(GROUP, plan.rows, LX)
-            for t in range(block_rows // WIDTH):
+            rhs = lambda g: ws[:, pl.ds(g, GROUP), :].reshape(2 * MY * GROUP, LX).astype(jnp.bfloat16)
+
+            def pointwise(t):
                 v = f[0, pl.ds(base + t * WIDTH, WIDTH)]
                 a = v[:, :half].reshape(WIDTH * half, LX)
                 b = v[:, half:].reshape(WIDTH * half, LX)
                 o = dot(mix[...], jnp.concatenate([a, b], 1))
                 at = t * WIDTH
-                pre[at : at + WIDTH, :half] += o[:, :LX].reshape(WIDTH, half, LX)
-                pre[at : at + WIDTH, half:] += o[:, LX:].reshape(WIDTH, half, LX)
-            if first:
-                def slopes(j, c2):
-                    for m in range(4):
-                        v = pre[j * 4 + m] + bias_ref[lax.rem(j * 4 + m, WIDTH)]
-                        c = c_ref[0, base + j * 4 + m].astype(jnp.float32)
-                        g_out[0, base + j * 4 + m] = (c * slope_of(v)).astype(jnp.bfloat16)
-                    return c2
-                lax.fori_loop(0, block_rows // 4, slopes, 0)
-                spread_y(plan, g_out, base, block_rows, ty_ref[...], us)
-            else:
-                g_out[0, pl.ds(base, block_rows)] = pre[...].astype(jnp.bfloat16)
+                pre[at : at + WIDTH, :half] = o[:, :LX].reshape(WIDTH, half, LX)
+                pre[at : at + WIDTH, half:] = o[:, LX:].reshape(WIDTH, half, LX)
+
+            def inverse(q):
+                g = pl.multiple_of(base + q * pair, GROUP)
+                o = dot(tyi[...], jnp.concatenate([rhs(g), rhs(g + GROUP)], 1))
+                return o[:, :LX].reshape(GROUP, plan.rows, LX), o[:, LX:].reshape(GROUP, plan.rows, LX)
+
+            def finish(q, parts):
+                for m in range(pair):
+                    at = q * pair + m
+                    v = pre[at] + parts[m // GROUP][m % GROUP]
+                    if first:
+                        c = c_ref[0, base + at].astype(jnp.float32)
+                        v = c * slope_of(v + bias_ref[at % WIDTH])
+                    g_out[0, base + at] = v.astype(jnp.bfloat16)
+
+            count = block_rows // pair
+            for t in range(block_rows // WIDTH):
+                pointwise(t)
+            parts = inverse(0)
+            for q in range(count):
+                following = inverse(q + 1) if q + 1 < count else None
+                finish(q, parts)
+                parts = following
+                if first:
+                    spread_y(plan, g_out, base + q * pair, pair, ty_ref[...], us)
             return carry
 
         lax.fori_loop(0, plan.grid_rows // block_rows, block, 0)
@@ -461,92 +508,93 @@
             gather_x(plan, tiles, us, tables, outs)
 
     cell = (1, plan.grid_rows, plan.rows, LX)
-    local = pl.BlockSpec(cell, lambda z: (z, 0, 0, 0))
-    placed = pl.BlockSpec(cell, lambda z: (z0 + z, 0, 0, 0))
-    sblock = pl.BlockSpec((1, plan.grid_rows, plan.lanes), lambda z: (z, 0, 0))
+    local = pl.BlockSpec(cell, lambda z, ids: (at + z, 0, 0, 0))
+    placed = pl.BlockSpec(cell, lambda z, ids: (z0 + at + z, 0, 0, 0))
+    sblock = pl.BlockSpec((1, plan.grid_rows, plan.wide), lambda z, ids: (at + z, 0, 0))
     scratch = [
         pltpu.VMEM((2 * MY, plan.grid_rows, LX), jnp.float32),
         pltpu.VMEM((block_rows, plan.rows, LX), jnp.float32),
+        pltpu.VMEM((WIDTH * half, WIDTH * half), jnp.bfloat16),
     ]
+    inputs = [own, other, field, point, ty_inv, xi]
+    kept = whole_block(own) if WHOLE else sblock
+    specs = [kept, kept, placed if first else local, whole_block(point), pick_block(ty_inv, 0), whole_block(xi)]
     if first:
-        inputs = [own, other, field, mixer, ty_inv, xi, cot, bias, ty, *tabs]
-        specs = [sblock, sblock, placed, whole_block(mixer), whole_block(ty_inv), whole_block(xi), placed]
-        specs += [pl.BlockSpec(memory_space=pltpu.SMEM), whole_block(ty)] + [whole_block(t) for t in tabs]
-        spec = jax.ShapeDtypeStruct((zc, plan.grid_rows, plan.lanes), jnp.bfloat16)
+        inputs += [cot, bias, ty, *tabs]
+        specs += [placed, pl.BlockSpec(memory_space=pltpu.SMEM), pick_block(ty, 0)]
+        specs += [whole_block(t) for t in tabs]
+        spec = jax.ShapeDtypeStruct((zc, plan.grid_rows, plan.wide), jnp.bfloat16)
         gout = jax.ShapeDtypeStruct((zc,) + cell[1:], jnp.bfloat16)
-        return rows_call(
-            kernel, "slope_pass", plan, zc, inputs, specs, [gout, spec, spec], [local, sblock, sblock],
-            scratch + [pltpu.VMEM((2 * MY, plan.grid_rows, LX), jnp.bfloat16)], {}, zc * 70e9,
-        )
-    inputs = [own, other, field, mixer, ty_inv, xi]
-    specs = [sblock, sblock, local, whole_block(mixer), whole_block(ty_inv), whole_block(xi)]
-    aliases = {}
-    if full is not None:
-        aliases = {len(inputs): 0}
-        inputs.append(full)
-        specs.append(pl.BlockSpec(memory_space=pl.ANY))
-    gout = jax.ShapeDtypeStruct((plan.depth,) + cell[1:], jnp.bfloat16)
+        shapes, out_specs, us, name = [gout, spec, spec], [local, sblock, sblock], 9.6, "slope_pass"
+        scratch.append(pltpu.VMEM((2 * MY, plan.grid_rows, LX), jnp.bfloat16))
+    else:
+        shapes, out_specs = [jax.ShapeDtypeStruct((plan.depth,) + cell[1:], jnp.bfloat16)], [placed]
+        us, name = 4.4, "input_pass"
+    aliases = {1 + len(inputs) + i: i for i in range(len(prev))}
     return rows_call(
-        kernel, "input_pass", plan, zc, inputs, specs, [gout], [placed], scratch, aliases, zc * 35e9
+        kernel, name, ids, count, inputs, specs, shapes, out_specs, scratch, us * count, [*prev, *after], aliases, 42
+    )
+
+
+def time_forward(plan, ids, own, other, table):
+    zc = own.shape[0]
+
+    def kernel(ids_ref, a_ref, b_ref, m_ref, keep, send):
+        for z in range(zc):
+            a = a_ref[z, :, : plan.lanes].astype(jnp.float32) + b_ref[z, :, : plan.lanes].astype(jnp.float32)
+            at = jnp.transpose(a).astype(jnp.bfloat16)
+            p = dot(at, m_ref[...]).reshape(plan.ky_half, 2, MX, 4 * LANE)
+            re = p[:, 0, :, : 2 * LANE] - p[:, 1, :, 2 * LANE :]
+            im = p[:, 0, :, 2 * LANE :] + p[:, 1, :, : 2 * LANE]
+            re, im = (v.reshape(plan.gz, plan.owned, 2 * LANE).astype(jnp.bfloat16) for v in (re, im))
+            keep[:, z, :, :LANE], keep[:, z, :, LANE:] = re[..., :LANE], im[..., :LANE]
+            send[:, z, :, :LANE], send[:, z, :, LANE:] = re[..., LANE:], im[..., LANE:]
+
+    out = jax.ShapeDtypeStruct((plan.gz, zc, plan.owned, 2 * LANE), jnp.bfloat16)
+    return rows_call(
+        kernel, "time_forward", ids, 1, [own, other, table],
+        [whole_block(own), whole_block(other), pick_block(table, 2)], [out, out], [whole_block(out)] * 2, [], 0.4 * zc,
+    )
+
+
+def time_inverse(plan, ids, keep, got, table, after):
+    zc = keep[0].shape[1]
+    gp = plan.grid_rows_padded()
+    flat = [*keep, *got]
+
+    def kernel(ids_ref, *refs):
+        ins, m_ref, out = refs[: len(flat)], refs[-2], refs[-1]
+        for z in range(zc):
+            stacked = lambda rs: jnp.concatenate([r[:, z].reshape(-1, 2 * LANE) for r in rs], 0)
+            a, b = stacked(ins[: len(keep)]), stacked(ins[len(keep) :])
+            o = dot(jnp.concatenate([a, b], 1), m_ref[...]).reshape(plan.ky_half, 1, MX, 2 * gp)
+            o = jnp.concatenate([o[..., :gp], o[..., gp:]], 1).reshape(plan.lanes, gp)
+            out[z, :, : plan.lanes] = jnp.transpose(o)[: plan.grid_rows].astype(jnp.bfloat16)
+
+    out = jax.ShapeDtypeStruct((zc, plan.grid_rows, plan.wide), jnp.bfloat16)
+    return rows_call(
+        kernel, "time_inverse", ids, 1, [*flat, table],
+        [whole_block(a) for a in flat] + [pick_block(table, 2)],
+        [out], [whole_block(out)], [], 0.4 * zc, after,
     )[0]
 
 
-def time_forward(plan, own, other, table):
-    zc = own.shape[0]
-    hp = plan.half_pairs
-
-    def kernel(a_ref, b_ref, m_ref, keep, send):
-        a = a_ref[0].astype(jnp.float32) + b_ref[0].astype(jnp.float32)
-        at = jnp.transpose(a).astype(jnp.bfloat16)
-        p = dot(at, m_ref[...]).reshape(plan.ky_half, 2, MX, 4 * LANE)
-        re = p[:, 0, :, : 2 * LANE] - p[:, 1, :, 2 * LANE :]
-        im = p[:, 0, :, 2 * LANE :] + p[:, 1, :, : 2 * LANE]
-        re, im = (v.reshape(plan.gz, 1, plan.owned, 2 * LANE).astype(jnp.bfloat16) for v in (re, im))
-        keep[...] = jnp.concatenate([re[..., :LANE], im[..., :LANE]], -1)
-        send[...] = jnp.concatenate([re[..., LANE:], im[..., LANE:]], -1)
-
-    block = pl.BlockSpec((1, plan.grid_rows, plan.lanes), lambda z: (z, 0, 0))
-    out = jax.ShapeDtypeStruct((plan.gz, zc, plan.owned, 2 * LANE), jnp.bfloat16)
-    ospec = pl.BlockSpec((plan.gz, 1, plan.owned, 2 * LANE), lambda z: (0, z, 0, 0))
-    return rows_call(
-        kernel, "time_forward", plan, zc, [own, other, table], [block, block, whole_block(table)],
-        [out, out], [ospec, ospec], [], {}, zc * 1e9,
-    )
-
-
-def time_inverse(plan, keep, got, table):
-    zc = keep.shape[1]
-    gp = plan.grid_rows_padded()
-
-    def kernel(a_ref, b_ref, m_ref, out):
-        rows = plan.half_pairs
-        a = a_ref[...].reshape(rows, 2 * LANE)
-        b = b_ref[...].reshape(rows, 2 * LANE)
-        o = dot(jnp.concatenate([a, b], 1), m_ref[...]).reshape(plan.ky_half, 1, MX, 2 * gp)
-        o = jnp.concatenate([o[..., :gp], o[..., gp:]], 1).reshape(plan.lanes, gp)
-        out[0] = jnp.transpose(o)[: plan.grid_rows].astype(jnp.bfloat16)
-
-    ispec = pl.BlockSpec((plan.gz, 1, plan.owned, 2 * LANE), lambda z: (0, z, 0, 0))
-    out = jax.ShapeDtypeStruct((zc, plan.grid_rows, plan.lanes), jnp.bfloat16)
-    return rows_call(
-        kernel, "time_inverse", plan, zc, [keep, got, table], [ispec, ispec, whole_block(table)],
-        [out], [pl.BlockSpec((1, plan.grid_rows, plan.lanes), lambda z: (z, 0, 0))], [], {}, zc * 1e9,
-    )[0]
-
-
-def depth_forward(plan, pieces, table):
+def depth_forward(plan, ids, pieces, table):
     flat = [p for chunk in pieces for p in chunk]
     n = len(flat)
-    zc = pieces[0][0].shape[0]
+    zc = flat[0].shape[1]
     octets = plan.owned // GROUP
     count = plan.gz * plan.depth
 
-    def kernel(*refs):
+    def kernel(ids_ref, *refs):
         ins, m_ref, keep, send, buf, out = refs[:n], refs[n], refs[n + 1], refs[n + 2], refs[n + 3], refs[n + 4]
-        for c in range(len(pieces)):
-            for k in range(plan.gz):
-                at = k * plan.depth + c * zc
-                buf[at : at + zc] = ins[c * plan.gz + k][...].astype(jnp.float32)
+        at = 0
+        for ref in ins:
+            for k in range(ref.shape[0]):
+                c, shift = at // plan.gz, at % plan.gz
+                first = shift * plan.depth + c * zc
+                buf[first : first + zc] = ref[k].astype(jnp.float32)
+                at += 1
         for o in range(octets):
             x = buf[:, o * GROUP : (o + 1) * GROUP, :].reshape(count * GROUP, 2 * LANE)
             x = jnp.concatenate([x[:, :LANE], x[:, LANE:]], 0).astype(jnp.bfloat16)
@@ -559,21 +607,22 @@
 
     shape = jax.ShapeDtypeStruct((plan.kz, plan.owned, 2 * LANE), jnp.bfloat16)
     return rows_call(
-        kernel, "depth_forward", plan, 1, [*flat, table], [whole_block(a) for a in flat] + [whole_block(table)],
-        [shape, shape], [pl.BlockSpec(shape.shape, lambda i: (0, 0, 0))] * 2,
+        kernel, "depth_forward", ids, 1, [*flat, table], [whole_block(a) for a in flat] + [pick_block(table, 1)],
+        [shape, shape], [pl.BlockSpec(shape.shape, lambda *i: (0, 0, 0))] * 2,
         [
             pltpu.VMEM((count, plan.owned, 2 * LANE), jnp.float32),
             pltpu.VMEM((plan.ta, plan.kz, plan.owned, 2 * LANE), jnp.float32),
-        ], {}, 1e9,
-    )
-
-
-def depth_inverse(plan, keep, got, table, chunks):
+        ], 1.4,
+    )
+
+
+def depth_inverse(plan, ids, keep, got, table, chunks):
     octets = plan.owned // GROUP
     zc = plan.depth // chunks
     count = plan.gz * plan.depth
-
-    def kernel(a_ref, b_ref, m_ref, *refs):
+    cut = plan.gz if SHIFTS else 1
+
+    def kernel(ids_ref, a_ref, b_ref, m_ref, *refs):
         outs, buf, out = refs[:-2], refs[-2], refs[-1]
         buf[0] = a_ref[...].astype(jnp.float32)
         buf[1] = b_ref[...].astype(jnp.float32)
@@ -591,20 +640,20 @@
         for c in range(chunks):
             for k in range(plan.gz):
                 at = k * plan.depth + c * zc
-                outs[c * plan.gz + k][...] = out[at : at + zc].astype(jnp.bfloat16)
-
-    shape = jax.ShapeDtypeStruct((zc, plan.owned, 2 * LANE), jnp.bfloat16)
-    n = chunks * plan.gz
+                outs[c * cut + k % cut][k // cut] = out[at : at + zc].astype(jnp.bfloat16)
+
+    shape = jax.ShapeDtypeStruct((plan.gz // cut, zc, plan.owned, 2 * LANE), jnp.bfloat16)
+    n = chunks * cut
     flat = rows_call(
-        kernel, "depth_inverse", plan, 1, [keep, got, table],
-        [whole_block(keep), whole_block(got), whole_block(table)],
-        [shape] * n, [pl.BlockSpec(shape.shape, lambda i: (0, 0, 0))] * n,
+        kernel, "depth_inverse", ids, 1, [keep, got, table],
+        [whole_block(keep), whole_block(got), pick_block(table, 1)],
+        [shape] * n, [pl.BlockSpec(shape.shape, lambda *i: (0, 0, 0, 0))] * n,
         [
             pltpu.VMEM((plan.ta, plan.kz, plan.owned, 2 * LANE), jnp.float32),
             pltpu.VMEM((count, plan.owned, 2 * LANE), jnp.float32),
-        ], {}, 1e9,
-    )
-    return [flat[c * plan.gz : (c + 1) * plan.gz] for c in range(chunks)]
+        ], 1.4,
+    )
+    return [flat[c * cut : (c + 1) * cut] for c in range(chunks)]
 
 
 def swap_pairs(v):
@@ -614,35 +663,31 @@
 
 
 def to_comm(plan, rows_ref, perm, keep, send):
-    flat = rows_ref[...].astype(jnp.bfloat16)
-    p = plan.owned
-    unit = (lax.broadcasted_iota(jnp.int32, (p, p), 0) == lax.broadcasted_iota(jnp.int32, (p, p), 1))
-    turned = dot_nt(unit.astype(jnp.bfloat16), flat).astype(jnp.bfloat16)
-    o = dot(turned, perm[...]).astype(jnp.bfloat16)
+    o = dot(jnp.transpose(rows_ref[...]).astype(jnp.bfloat16), perm[...]).astype(jnp.bfloat16)
     keep[0] = o[:, : 2 * LANE]
     send[0] = o[:, 2 * LANE :]
 
 
 def mode_specs(plan):
     mode_rows = MT * WIDTH * WIDTH * 2
-    half = pl.BlockSpec((1, plan.owned, 2 * LANE), lambda k: (k, 0, 0))
-    weights = pl.BlockSpec((1, mode_rows, plan.owned), lambda k: (k, 0, 0))
+    half = pl.BlockSpec((1, plan.owned, 2 * LANE), lambda k, ids: (k, 0, 0))
+    weights = pl.BlockSpec((1, mode_rows, plan.owned), lambda k, ids: (k, 0, 0))
     return half, weights, mode_rows
 
 
-def mix_modes(plan, spec, weights, here, perm, unit):
+def mix_modes(plan, ids, spec, weights, perm, unit):
     half, wspec, mode_rows = mode_specs(plan)
     per_t = WIDTH * WIDTH * 2
     wide = 2 * WIDTH
 
-    def kernel(here_ref, a_ref, b_ref, w_ref, perm_ref, unit_ref, keep, send, xs, ms):
+    def kernel(ids_ref, a_ref, b_ref, w_ref, perm_ref, unit_ref, keep, send, xs, ms):
         x = jnp.concatenate([a_ref[0], b_ref[0]], 1)
         xs[...] = dot_nt(unit_ref[...], x)
 
         def step(q, carry):
             h = q // plan.kt
             kt = q - h * plan.kt
-            at = lax.rem(q + here_ref[0] * plan.kt, MT)
+            at = lax.rem(q + ids_ref[2] * plan.kt, MT)
             row = h * 2 * LANE + kt * WIDTH
             s1 = jnp.zeros((wide, plan.owned), jnp.float32)
             s2 = jnp.zeros((wide, plan.owned), jnp.float32)
@@ -655,31 +700,31 @@
             ms[pl.ds(pl.multiple_of(q * wide, 8), wide), :] = s1 + swap_pairs(s2)
             return carry
 
-        lax.fori_loop(0, MT, step, 0)
+        lax.fori_loop(0, MT, step, 0, unroll=UNROLL)
         to_comm(plan, ms, perm_ref, keep, send)
 
     shape = jax.ShapeDtypeStruct((plan.kz, plan.owned, 2 * LANE), jnp.bfloat16)
     return rows_call(
-        kernel, "mix_modes", plan, plan.kz, [here, *spec, weights, perm, unit],
-        [pl.BlockSpec(memory_space=pltpu.SMEM), half, half, wspec, whole_block(perm), whole_block(unit)],
+        kernel, "mix_modes", ids, plan.kz, [*spec, weights, perm, unit],
+        [half, half, wspec, whole_block(perm), whole_block(unit)],
         [shape, shape], [half, half],
         [
             pltpu.VMEM((2 * plan.ta * LANE, plan.owned), jnp.float32),
             pltpu.VMEM((MT * wide, plan.owned), jnp.float32),
-        ], {}, 1e9,
-    )
-
-
-def back_modes(plan, grad, weights, here, perm):
+        ], 17.0, vmem=46,
+    )
+
+
+def back_modes(plan, ids, grad, weights, perm):
     half, wspec, mode_rows = mode_specs(plan)
     per_t = WIDTH * WIDTH * 2
     wide = 2 * WIDTH
 
-    def kernel(here_ref, a_ref, b_ref, w_ref, perm_ref, keep, send, gs, ms):
+    def kernel(ids_ref, a_ref, b_ref, w_ref, perm_ref, keep, send, gs, ms):
         gs[...] = dot_nt(perm_ref[...], jnp.concatenate([a_ref[0], b_ref[0]], 1))
 
         def step(q, carry):
-            at = lax.rem(q + here_ref[0] * plan.kt, MT)
+            at = lax.rem(q + ids_ref[2] * plan.kt, MT)
             g = gs[pl.ds(pl.multiple_of(q * wide, 8), wide), :]
             g2 = -swap_pairs(g)
             rows = []
@@ -692,31 +737,33 @@
             ms[pl.ds(pl.multiple_of(q * wide, 8), wide), :] = jnp.concatenate(rows, 0)
             return carry
 
-        lax.fori_loop(0, MT, step, 0)
+        lax.fori_loop(0, MT, step, 0, unroll=UNROLL)
         to_comm(plan, ms, perm_ref, keep, send)
 
     shape = jax.ShapeDtypeStruct((plan.kz, plan.owned, 2 * LANE), jnp.bfloat16)
     return rows_call(
-        kernel, "back_modes", plan, plan.kz, [here, *grad, weights, perm],
-        [pl.BlockSpec(memory_space=pltpu.SMEM), half, half, wspec, whole_block(perm)],
+        kernel, "back_modes", ids, plan.kz, [*grad, weights, perm],
+        [half, half, wspec, whole_block(perm)],
         [shape, shape], [half, half],
-        [pltpu.VMEM((MT * wide, plan.owned), jnp.float32)] * 2, {}, 1e9,
-    )
-
-
-def weight_modes(plan, spec, grad, here, perm, unit):
-    half, wspec, mode_rows = mode_specs(plan)
+        [pltpu.VMEM((MT * wide, plan.owned), jnp.float32)] * 2, 20.0, vmem=46,
+    )
+
+
+def weight_modes(plan, ids, spec, grad, perm, unit, k0, count, full, after):
+    _, _, mode_rows = mode_specs(plan)
+    half = pl.BlockSpec((1, plan.owned, 2 * LANE), lambda k, ids: (k0 + k, 0, 0))
+    wspec = pl.BlockSpec((1, mode_rows, plan.owned), lambda k, ids: (k0 + k, 0, 0))
     per_t = WIDTH * WIDTH * 2
     wide = 2 * WIDTH
 
-    def kernel(here_ref, xa, xb, ga, gb, perm_ref, unit_ref, out, xs, gs):
+    def kernel(ids_ref, xa, xb, ga, gb, perm_ref, unit_ref, out, xs, gs):
         xs[...] = dot_nt(unit_ref[...], jnp.concatenate([xa[0], xb[0]], 1))
         gs[...] = dot_nt(perm_ref[...], jnp.concatenate([ga[0], gb[0]], 1))
 
         def step(q, carry):
             h = q // plan.kt
             kt = q - h * plan.kt
-            at = lax.rem(q + here_ref[0] * plan.kt, MT)
+            at = lax.rem(q + ids_ref[2] * plan.kt, MT)
             row = h * 2 * LANE + kt * WIDTH
             g = gs[pl.ds(pl.multiple_of(q * wide, 8), wide), :]
             g2 = -swap_pairs(g)
@@ -729,17 +776,17 @@
                 out[0, rows, :] = jnp.concatenate(two, 0).astype(jnp.bfloat16)
             return carry
 
-        lax.fori_loop(0, MT, step, 0)
+        lax.fori_loop(0, MT, step, 0, unroll=UNROLL)
 
     shape = jax.ShapeDtypeStruct((plan.kz, mode_rows, plan.owned), jnp.bfloat16)
     return rows_call(
-        kernel, "weight_modes", plan, plan.kz, [here, *spec, *grad, perm, unit],
-        [pl.BlockSpec(memory_space=pltpu.SMEM), half, half, half, half, whole_block(perm), whole_block(unit)],
+        kernel, "weight_modes", ids, count, [*spec, *grad, perm, unit],
+        [half, half, half, half, whole_block(perm), whole_block(unit)],
         [shape], [wspec],
         [
             pltpu.VMEM((2 * plan.ta * LANE, plan.owned), jnp.float32),
             pltpu.VMEM((MT * wide, plan.owned), jnp.float32),
-        ], {}, 1e9,
+        ], 1.8 * count, [*([] if full is None else [full]), *after], {} if full is None else {7: 0}, 46,
     )[0]
 
 
@@ -747,23 +794,17 @@
     gz_at, ta_at, col_at = (lax.axis_index(a) for a in ("gz", "ta", "col"))
     chunks = CHUNKS
     zc = plan.depth // chunks
-    pick = lambda table, at: lax.dynamic_index_in_dim(jnp.asarray(table), at, 0, keepdims=False)
-    ty = pick(plan.y_tables(), gz_at * plan.col + col_at)
-    ty_inv = ty.T
+    ids = jnp.stack([gz_at * plan.col + col_at, gz_at * plan.ta + ta_at, ta_at]).astype(jnp.int32)
+    y_table = plan.y_tables()
+    ty, ty_inv = jnp.asarray(y_table), jnp.asarray(np.swapaxes(y_table, 1, 2).copy())
     tiles = plan.x_tiles()
     windows, xi = plan.x_windows()
     xi = jnp.asarray(xi)
-    zf, zi = plan.z_tables()
-    z_at = gz_at * plan.ta + ta_at
-    zf, zi = pick(zf, z_at), pick(zi, z_at)
-    plain, weighted = plan.t_tables(False), plan.t_tables(True)
+    zf, zi = (jnp.asarray(t) for t in plan.z_tables())
+    t_fwd, t_inv = (jnp.asarray(t) for t in plan.t_tables(False))
+    tw_fwd, tw_inv = (jnp.asarray(t) for t in plan.t_tables(True))
     perm = jnp.asarray(plan.pair_rows())
-    unit = jnp.eye(2 * plan.ta * LANE, dtype=jnp.bfloat16)
-    here = ta_at.astype(jnp.int32).reshape(1)
-    half = plan.rows // 2
-    eye = jnp.eye(half, dtype=jnp.bfloat16)
-    kron = lambda m: (m[:, None, :, None] * eye[None, :, None, :]).reshape(WIDTH * half, WIDTH * half)
-    mix_out, mix_in = kron(point_weight.T), kron(point_weight)
+    unit = jnp.asarray(bf16(np.eye(2 * plan.ta * LANE)))
     flat = (plan.depth, plan.grid_rows, plan.rows, LX)
     field, cotangent = field.reshape(flat), cotangent.reshape(flat)
     weights = jnp.transpose(spectral_weight, (0, 1, 4, 5, 3, 2))
@@ -772,55 +813,80 @@
     def swap(a, axis):
         return lax.ppermute(a, axis, [(0, 1), (1, 0)])
 
-    def shift(a, k):
-        return lax.ppermute(a, "gz", [(d, (d + k) % plan.gz) for d in range(plan.gz)])
+    def spread(blocks, sign):
+        if not SHIFTS:
+            return [lax.all_to_all(blocks[0], "gz", 0, 0, tiled=True)]
+        moved = [blocks[0]]
+        for k in range(1, plan.gz):
+            moved.append(lax.ppermute(blocks[k], "gz", [(d, (d + sign * k) % plan.gz) for d in range(plan.gz)]))
+        return moved
 
     def outward(own, other, table):
-        keep, send = time_forward(plan, own, swap(other, "col"), table)
+        keep, send = time_forward(plan, ids, own, swap(other, "col"), table)
         total = (keep.astype(jnp.float32) + swap(send, "ta").astype(jnp.float32)).astype(jnp.bfloat16)
-        return [total[0]] + [shift(total[k], k) for k in range(1, plan.gz)]
+        blocks = [total[k : k + 1] for k in range(plan.gz)] if SHIFTS else [total]
+        return spread(blocks, 1), send
 
     def collect(pieces):
-        keep, send = depth_forward(plan, pieces, zf)
+        keep, send = depth_forward(plan, ids, pieces, zf)
         return keep, swap(send, "ta")
 
-    def inward(keep, send, table):
-        pieces = depth_inverse(plan, keep, swap(send, "ta"), zi, chunks)
+    def inward(keep, send):
         out = []
-        for chunk in pieces:
-            mine = jnp.stack([chunk[0]] + [shift(chunk[k], -k) for k in range(1, plan.gz)])
-            own = time_inverse(plan, mine, swap(mine, "ta"), table)
-            out.append((own, swap(own, "col")))
+        for chunk in depth_inverse(plan, ids, keep, swap(send, "ta"), zi, chunks):
+            mine = spread(chunk, -1)
+            if len(mine) > 1:
+                mine = [jnp.concatenate(mine, 0)]
+            out.append((mine, [swap(m, "ta") for m in mine]))
         return out
 
-    t_fwd, t_inv = (pick(t, ta_at) for t in plain)
-    tw_fwd, tw_inv = (pick(t, ta_at) for t in weighted)
-
-    pieces = []
+    def planes(pieces, table, after):
+        own = time_inverse(plan, ids, *pieces, table, after)
+        return own, swap(own, "col")
+
+    sub = zc // PARTS
+    pieces, sent = [], []
     for n in range(chunks):
-        own, other = analyse_xy(plan, tiles, field, ty, n * zc, zc)
-        pieces.append(outward(own, other, t_fwd))
+        made = []
+        for m in range(PARTS):
+            after = [sent[n - 1]] if n and m == 1 else []
+            made = analyse_xy(plan, ids, tiles, field, ty, n * zc, zc, m * sub, sub, after, made)
+        moved, send = outward(*made, t_fwd)
+        pieces.append(moved)
+        sent.append(send)
     spec = collect(pieces)
-    mixed = mix_modes(plan, spec, weights, here, perm, unit)
-    planes = inward(*mixed, tw_inv)
-    pieces, gprime = [], []
+    mixed = mix_modes(plan, ids, spec, weights, perm, unit)
+    arrived = inward(*mixed)
+    pieces, gprime, sent = [], [], []
     for n in range(chunks):
-        g, own, other = field_pass(
-            plan, tiles, windows, *planes[n], field, mix_out, ty, ty_inv, xi, n * zc, zc,
-            cot=cotangent, bias=point_bias,
+        made = []
+        plane = planes(arrived[n], tw_inv, gprime[-1:] if n and ORDERED else [])
+        for m in range(PARTS):
+            after = [sent[n - 1]] if n and m == 1 else []
+            made = field_pass(
+                plan, ids, tiles, windows, *plane, field, point_weight.T, ty, ty_inv, xi,
+                n * zc, zc, m * sub, sub, after, made, cot=cotangent, bias=point_bias,
+            )
+        g, own, other = made
+        gprime.append(g)
+        moved, send = outward(own, other, tw_fwd)
+        pieces.append(moved)
+        sent.append(send)
+    grad = collect(pieces)
+    back = back_modes(plan, ids, grad, weights, perm)
+    arrived = inward(*back)
+    weight_grad, at = None, 0
+    for n, count in enumerate(WEIGHT_SIZES):
+        after = arrived[0][0] if n == len(WEIGHT_SIZES) - 1 else []
+        weight_grad = weight_modes(plan, ids, spec, grad, perm, unit, at, count, weight_grad, after)
+        at += count
+    made = []
+    for n in range(chunks):
+        plane = planes(arrived[n], t_inv, [weight_grad] if n == 0 else [])
+        made = field_pass(
+            plan, ids, tiles, windows, *plane, gprime[n], point_weight, ty, ty_inv, xi, n * zc, zc, 0, zc, [], made
         )
-        gprime.append(g)
-        pieces.append(outward(own, other, tw_fwd))
-    grad = collect(pieces)
-    back = back_modes(plan, grad, weights, here, perm)
-    planes = inward(*back, t_inv)
-    weight_grad = weight_modes(plan, spec, grad, here, perm, unit)
-    full = None
-    for n in range(chunks):
-        full = field_pass(
-            plan, tiles, windows, *planes[n], gprime[n], mix_in, ty, ty_inv, xi, n * zc, zc, full=full
-        )
-    input_grad = full.reshape(plan.depth, plan.steps, WIDTH, plan.rows, LX)
+    input_grad = made[0].reshape(plan.depth, plan.steps, WIDTH, plan.rows, LX)
     weight_grad = weight_grad.reshape(plan.kz, MT, WIDTH, WIDTH, 2, plan.owned)
     return input_grad, jnp.transpose(weight_grad, (0, 1, 5, 4, 2, 3))
 
@@ -838,6 +904,7 @@
         and rows == 32
         and plan.kt * WIDTH <= LANE
         and depth % CHUNKS == 0
+        and plan.kz == sum(WEIGHT_SIZES)
     )
     if fits:
         return direct_device(plan, *args)

time: 493 us -> 414 us (0.84)
  Pallas kernels: 259 us -> 209 us
  local copies, waits for them, and re-layouts: 53.5 us -> 14 us
  waiting for transfers between devices: 110 us -> 123 us
  starting transfers between devices: 58.5 us -> 66.4 us
  other arithmetic: 7.72 us -> 0.73 us
    pallas_call x21, Pallas kernels: 259 us -> 209 us  [rows_call(): pl.pallas_call(body, grid_spec=pltpu.PrefetchScalarGridSpec(num_scalar_pr...]
    pallas_call x8 -> x0, local copies, waits for them, and re-layouts: 16.9 us -> none  [rows_call(): pl.pallas_call(kernel, grid=(grid,), in_specs=specs, out_specs=out_specs,...]
    ppermute x8 -> x0, local copies, waits for them, and re-layouts: 14.2 us -> none  [swap(): return lax.ppermute(a, axis, [(0, 1), (1, 0)])]
    ppermute x24, waiting for transfers between devices: 40.5 us -> 51.9 us  [spread(): lax.ppermute(blocks[k], 'gz', [(d, (d + sign * k) % plan.gz) for d in ran...]
    squeeze x11 -> x0, local copies, waits for them, and re-layouts: 11 us -> none  [the longest x7 8.23 us: direct_device(): lax.dynamic_index_in_dim(jnp.asarray(table), at, 0, keepdims=False)]
    ppermute x24, starting transfers between devices: 39.4 us -> 49.9 us  [spread(): lax.ppermute(blocks[k], 'gz', [(d, (d + sign * k) % plan.gz) for d in ran...]
    unnamed x68 -> x73, local copies, waits for them, and re-layouts: 5.95 us -> 13.8 us
  transfers between devices with their start and end apart: 44 -> 44, of which waited for: 19 -> 23; matrix products, arithmetic and copies ran while one was open for 10% -> 0% of each run, Pallas kernels for 36% -> 33%
where the time goes in v2:
time: 414 us
  Pallas kernels  209 us (50%)
  waiting for transfers between devices  123 us (30%)
  starting transfers between devices  66.4 us (16%)
  local copies, waits for them, and re-layouts  14 us (3%)
    pallas_call x21, Pallas kernels, rows_call(): pl.pallas_call(body, grid_spec=pltpu.PrefetchScalarGridSpec(num_scalar_pr...  209 us
    ppermute x20, waiting for transfers between devices, swap(): return lax.ppermute(a, axis, [(0, 1), (1, 0)])  70.7 us
    ppermute x24, waiting for transfers between devices, spread(): lax.ppermute(blocks[k], 'gz', [(d, (d + sign * k) % plan.gz) for d in ran...  51.9 us
    ppermute x24, starting transfers between devices, spread(): lax.ppermute(blocks[k], 'gz', [(d, (d + sign * k) % plan.gz) for d in ran...  49.9 us
    ppermute x20, starting transfers between devices, swap(): return lax.ppermute(a, axis, [(0, 1), (1, 0)])  16.5 us
    unnamed x73, local copies, waits for them, and re-layouts  13.8 us
  transfers between devices with their start and end apart: 44, of which 23 were waited for; matrix products, arithmetic and copies ran while one was open for 0% of the time, Pallas kernels for 33%

profile of v2, /device:TPU:0, one launch (start us, length us, event | category | flops | bytes accessed | tf_op | source)
XLA Modules:
  0.0 413.5 jit_solution(4071509230835128812)
XLA Ops:
  3.9 12.6 %analyse_xy.3 = (bf16[4,240,640]{2,1,0:T(8,128)(2,1)}, bf16[4,240,640]{2,1,0:T(8,128)(2,1)}) custom-call(s32[3]{0:T(128)S(1)} %pad_add_fusion.ids_ref, bf16[8,240,32,128]{3,2,1,0:T(8,128)(2,1)} %bitcast.16, bf16[8,384,256]{2,1,0:T(8,128)(2,1)} %constant.41.clone.refs_1_.refs_8_, bf16[1536,256]{1,0:T(8,128)(2,1)S(1)} %copy-done.6, ...), custom_call_target="tpu_custom_call" | custom-call | flops 1232000000 | bytes 1120000 | tf_op jit(solution)/shard_map/analyse_xy/pallas_call | solution.py:375
  16.9 12.6 %analyse_xy.2 = (bf16[4,240,640]{2,1,0:T(8,128)(2,1)}, bf16[4,240,640]{2,1,0:T(8,128)(2,1)}) custom-call(s32[3]{0:T(128)S(1)} %pad_add_fusion.ids_ref, bf16[8,240,32,128]{3,2,1,0:T(8,128)(2,1)} %bitcast.17, bf16[8,384,256]{2,1,0:T(8,128)(2,1)} %constant.41.clone.refs_1_.refs_8_, bf16[1536,256]{1,0:T(8,128)(2,1)S(1)} %copy-done.6, ...), custom_call_target="tpu_custom_call" | custom-call | flops 1232000000 | bytes 1120000 | tf_op jit(solution)/shard_map/analyse_xy/pallas_call | solution.py:375
  31.0 3.0 collective-permute-start.6
  36.7 11.4 %collective-permute-done.6 = bf16[4,4,72,256]{3,2,1,0:T(8,128)(2,1)S(1)} collective-permute-done((bf16[4,4,72,256]{3,2,1,0:T(8,128)(2,1)S(1)}, bf16[4,4,72,256]{3,2,1,0:T(8,128)(2,1)S(1)}, u32[]{:S(2)}, u32[]{:S(2)}) %collective-permute-start.6) | collective-permute-done | bytes 589856 | tf_op jit(solution)/shard_map/ppermute | solution.py:814
  48.3 4.3 %collective-permute-start.9 = (bf16[1,4,72,256]{3,2,1,0:T(8,128)(2,1)S(1)}, bf16[1,4,72,256]{3,2,1,0:T(8,128)(2,1)S(1)}, u32[]{:S(2)}, u32[]{:S(2)}) collective-permute-start(bf16[1,4,72,256]{3,2,1,0:T(8,128)(2,1)S(1)} %get-tuple-element.94), channel_id=1, source_target_pairs={{0,12},{4,0},{8,4},{12,8},{1,13},{5,1},{9,5},{13,9},{2,14},{6,2},{... | collective-permute-start | bytes 442376 | tf_op jit(solution)/shard_map/ppermute | solution.py:821
  53.6 6.6 %collective-permute-done.1 = bf16[4,4,72,256]{3,2,1,0:T(8,128)(2,1)S(1)} collective-permute-done((bf16[4,4,72,256]{3,2,1,0:T(8,128)(2,1)S(1)}, bf16[4,4,72,256]{3,2,1,0:T(8,128)(2,1)S(1)}, u32[]{:S(2)}, u32[]{:S(2)}) %collective-permute-start.1) | collective-permute-done | bytes 589856 | tf_op jit(solution)/shard_map/ppermute | solution.py:814
  60.4 3.9 collective-permute-start.4
  65.5 3.1 collective-permute-done.4.refs_3_
  68.6 8.5 %collective-permute-done.3.refs_2_ = bf16[1,4,72,256]{3,2,1,0:T(8,128)(2,1)S(1)} collective-permute-done((bf16[1,4,72,256]{3,2,1,0:T(8,128)(2,1)S(1)}, bf16[1,4,72,256]{3,2,1,0:T(8,128)(2,1)S(1)}, u32[]{:S(2)}, u32[]{:S(2)}) %collective-permute-start.3) | collective-permute-done | bytes 147488 | tf_op jit(solution)/shard_map/ppermute | solution.py:821
  80.0 6.6 %collective-permute-done.10.refs_1_ = bf16[8,72,256]{2,1,0:T(8,128)(2,1)S(1)} collective-permute-done((bf16[8,72,256]{2,1,0:T(8,128)(2,1)S(1)}, bf16[8,72,256]{2,1,0:T(8,128)(2,1)S(1)}, u32[]{:S(2)}, u32[]{:S(2)}) %collective-permute-start.10) | collective-permute-done | bytes 294944 | tf_op jit(solution)/shard_map/ppermute | solution.py:814
  86.6 16.2 %mix_modes.1 = (bf16[8,72,256]{2,1,0:T(8,128)(2,1)S(1)}, bf16[8,72,256]{2,1,0:T(8,128)(2,1)S(1)}) custom-call(s32[3]{0:T(128)S(1)} %pad_add_fusion.ids_ref, bf16[8,72,256]{2,1,0:T(8,128)(2,1)S(1)} %get-tuple-element.52.refs_0_, bf16[8,72,256]{2,1,0:T(8,128)(2,1)S(1)} %collective-permute-done.10.refs_1_, bf16[8,9600,72]{2,1,0:T(8,128)(2,1)} %bitcast.20, ...), custom_call_target="tpu_custom_call" | custom-call | flops 1870000000 | bytes 1700000 | tf_op jit(solution)/shard_map/mix_modes/pallas_call | solution.py:375
  104.4 5.6 %collective-permute-done.11.refs_1_ = bf16[8,72,256]{2,1,0:T(8,128)(2,1)S(1)} collective-permute-done((bf16[8,72,256]{2,1,0:T(8,128)(2,1)S(1)}, bf16[8,72,256]{2,1,0:T(8,128)(2,1)S(1)}, u32[]{:S(2)}, u32[]{:S(2)}) %collective-permute-start.11) | collective-permute-done | bytes 294944 | tf_op jit(solution)/shard_map/ppermute | solution.py:814
  115.5 2.5 collective-permute-done.22
  118.0 6.3 %collective-permute-done.23 = bf16[1,4,72,256]{3,2,1,0:T(8,128)(2,1)S(1)} collective-permute-done((bf16[1,4,72,256]{3,2,1,0:T(8,128)(2,1)S(1)}, bf16[1,4,72,256]{3,2,1,0:T(8,128)(2,1)S(1)}, u32[]{:S(2)}, u32[]{:S(2)}) %collective-permute-start.23) | collective-permute-done | bytes 147488 | tf_op jit(solution)/shard_map/ppermute | solution.py:821
  131.4 7.6 %collective-permute-done.13 = bf16[1,4,72,256]{3,2,1,0:T(8,128)(2,1)S(1)} collective-permute-done((bf16[1,4,72,256]{3,2,1,0:T(8,128)(2,1)S(1)}, bf16[1,4,72,256]{3,2,1,0:T(8,128)(2,1)S(1)}, u32[]{:S(2)}, u32[]{:S(2)}) %collective-permute-start.13) | collective-permute-done | bytes 147488 | tf_op jit(solution)/shard_map/ppermute | solution.py:821
  142.4 7.4 %collective-permute-done.15.refs_1_ = bf16[4,4,72,256]{3,2,1,0:T(8,128)(2,1)S(1)} collective-permute-done((bf16[4,4,72,256]{3,2,1,0:T(8,128)(2,1)S(1)}, bf16[4,4,72,256]{3,2,1,0:T(8,128)(2,1)S(1)}, u32[]{:S(2)}, u32[]{:S(2)}) %collective-permute-start.15) | collective-permute-done | bytes 589856 | tf_op jit(solution)/shard_map/ppermute | solution.py:814
  156.0 39.4 %slope_pass.3 = (bf16[4,240,32,128]{3,2,1,0:T(8,128)(2,1)}, bf16[4,240,640]{2,1,0:T(8,128)(2,1)S(1)}, bf16[4,240,640]{2,1,0:T(8,128)(2,1)S(1)}) custom-call(s32[3]{0:T(128)S(1)} %pad_add_fusion.ids_ref, bf16[4,240,640]{2,1,0:T(8,128)(2,1)} %time_inverse.5.refs_0_, bf16[4,240,640]{2,1,0:T(8,128)(2,1)} %collective-permute-done.26.refs_1_, ...), custom_call_target="tpu_custom_call" | custom-call | flops 4224000000 | bytes 3840000 | tf_op jit(solution)/shard_map/slope_pass/pallas_call | solution.py:375
  196.0 39.1 %slope_pass.2 = (bf16[4,240,32,128]{3,2,1,0:T(8,128)(2,1)}, bf16[4,240,640]{2,1,0:T(8,128)(2,1)S(1)}, bf16[4,240,640]{2,1,0:T(8,128)(2,1)S(1)}) custom-call(s32[3]{0:T(128)S(1)} %pad_add_fusion.ids_ref, bf16[4,240,640]{2,1,0:T(8,128)(2,1)} %time_inverse.4.refs_0_, bf16[4,240,640]{2,1,0:T(8,128)(2,1)} %collective-permute-done.16.refs_1_, ...), custom_call_target="tpu_custom_call" | custom-call | flops 4224000000 | bytes 3840000 | tf_op jit(solution)/shard_map/slope_pass/pallas_call | solution.py:375
  240.1 12.6 %collective-permute-done.28 = bf16[4,4,72,256]{3,2,1,0:T(8,128)(2,1)S(1)} collective-permute-done((bf16[4,4,72,256]{3,2,1,0:T(8,128)(2,1)S(1)}, bf16[4,4,72,256]{3,2,1,0:T(8,128)(2,1)S(1)}, u32[]{:S(2)}, u32[]{:S(2)}) %collective-permute-start.28) | collective-permute-done | bytes 589856 | tf_op jit(solution)/shard_map/ppermute | solution.py:814
  252.9 3.1 collective-permute-start.31
  260.2 4.7 %collective-permute-done.18 = bf16[4,4,72,256]{3,2,1,0:T(8,128)(2,1)S(1)} collective-permute-done((bf16[4,4,72,256]{3,2,1,0:T(8,128)(2,1)S(1)}, bf16[4,4,72,256]{3,2,1,0:T(8,128)(2,1)S(1)}, u32[]{:S(2)}, u32[]{:S(2)}) %collective-permute-start.18) | collective-permute-done | bytes 589856 | tf_op jit(solution)/shard_map/ppermute | solution.py:814
  265.1 2.8 collective-permute-start.21
  274.4 9.3 %collective-permute-done.20.refs_2_ = bf16[1,4,72,256]{3,2,1,0:T(8,128)(2,1)S(1)} collective-permute-done((bf16[1,4,72,256]{3,2,1,0:T(8,128)(2,1)S(1)}, bf16[1,4,72,256]{3,2,1,0:T(8,128)(2,1)S(1)}, u32[]{:S(2)}, u32[]{:S(2)}) %collective-permute-start.20) | collective-permute-done | bytes 147488 | tf_op jit(solution)/shard_map/ppermute | solution.py:821
  285.7 7.6 %collective-permute-done.32.refs_1_.refs_3_ = bf16[8,72,256]{2,1,0:T(8,128)(2,1)S(1)} collective-permute-done((bf16[8,72,256]{2,1,0:T(8,128)(2,1)S(1)}, bf16[8,72,256]{2,1,0:T(8,128)(2,1)S(1)}, u32[]{:S(2)}, u32[]{:S(2)}) %collective-permute-start.32) | collective-permute-done | bytes 294944 | tf_op jit(solution)/shard_map/ppermute | solution.py:814
  293.3 20.2 %back_modes.1 = (bf16[8,72,256]{2,1,0:T(8,128)(2,1)S(1)}, bf16[8,72,256]{2,1,0:T(8,128)(2,1)S(1)}) custom-call(s32[3]{0:T(128)S(1)} %pad_add_fusion.ids_ref, bf16[8,72,256]{2,1,0:T(8,128)(2,1)S(1)} %get-tuple-element.72.refs_0_.refs_2_, bf16[8,72,256]{2,1,0:T(8,128)(2,1)S(1)} %collective-permute-done.32.refs_1_.refs_3_, bf16[8,9600,72]{2,1,0:T(8,128)(2,1)} %bitcast.21, ...), custom_call_target="tpu_custom_call" | custom-call | flops 2200000000 | bytes 2000000 | tf_op jit(solution)/shard_map/back_modes/pallas_call | solution.py:375
  314.2 6.7 %collective-permute-done.33.refs_1_ = bf16[8,72,256]{2,1,0:T(8,128)(2,1)S(1)} collective-permute-done((bf16[8,72,256]{2,1,0:T(8,128)(2,1)S(1)}, bf16[8,72,256]{2,1,0:T(8,128)(2,1)S(1)}, u32[]{:S(2)}, u32[]{:S(2)}) %collective-permute-start.33) | collective-permute-done | bytes 294944 | tf_op jit(solution)/shard_map/ppermute | solution.py:814
  328.1 7.2 %collective-permute-done.39 = bf16[1,4,72,256]{3,2,1,0:T(8,128)(2,1)S(1)} collective-permute-done((bf16[1,4,72,256]{3,2,1,0:T(8,128)(2,1)S(1)}, bf16[1,4,72,256]{3,2,1,0:T(8,128)(2,1)S(1)}, u32[]{:S(2)}, u32[]{:S(2)}) %collective-permute-start.39) | collective-permute-done | bytes 147488 | tf_op jit(solution)/shard_map/ppermute | solution.py:821
  335.3 12.2 %collective-permute-start.41 = (bf16[1,4,72,256]{3,2,1,0:T(8,128)(2,1)S(1)}, bf16[1,4,72,256]{3,2,1,0:T(8,128)(2,1)S(1)}, u32[]{:S(2)}, u32[]{:S(2)}) collective-permute-start(bf16[1,4,72,256]{3,2,1,0:T(8,128)(2,1)S(1)} %get-tuple-element.84), channel_id=1, source_target_pairs={{0,4},{4,8},{8,12},{12,0},{1,5},{5,9},{9,13},{13,1},{2,6},{6,10},{... | collective-permute-start | bytes 442376 | tf_op jit(solution)/shard_map/ppermute | solution.py:821
  352.5 14.6 %weight_modes.1.refs_3_ = bf16[8,9600,72]{2,1,0:T(8,128)(2,1)} custom-call(s32[3]{0:T(128)S(1)} %pad_add_fusion.ids_ref, bf16[8,72,256]{2,1,0:T(8,128)(2,1)S(1)} %copy-done.25, bf16[8,72,256]{2,1,0:T(8,128)(2,1)S(1)} %copy-done.27, bf16[8,72,256]{2,1,0:T(8,128)(2,1)S(1)} %get-tuple-element.72.refs_0_.refs_2_, ...), custom_call_target="tpu_custom_call" | custom-call | flops 1584000000 | bytes 1440000 | tf_op jit(solution)/shard_map/weight_modes/pallas_call | solution.py:375
  367.2 6.6 %copy-done = bf16[8,9600,72]{2,1,0:T(8,128)(2,1)S(1)} copy-done((bf16[8,9600,72]{2,1,0:T(8,128)(2,1)S(1)}, bf16[8,9600,72]{2,1,0:T(8,128)(2,1)}, u32[]{:S(2)}) %copy-start) | copy-done | bytes 11059224
  378.2 17.7 %input_pass.2.refs_6_ = bf16[8,240,32,128]{3,2,1,0:T(8,128)(2,1)} custom-call(s32[3]{0:T(128)S(1)} %pad_add_fusion.ids_ref, bf16[4,240,640]{2,1,0:T(8,128)(2,1)S(1)} %time_inverse.7.refs_0_, bf16[4,240,640]{2,1,0:T(8,128)(2,1)S(1)} %collective-permute-done.43.refs_1_, bf16[4,240,32,128]{3,2,1,0:T(8,128)(2,1)} %get-tuple-element.85.refs_2_, ...), custom_call_target="tpu_custom_call" | custom-call | flops 1936000000 | bytes 1760000 | tf_op jit(solution)/shard_map/input_pass/pallas_call | solution.py:375
  395.9 17.7 %input_pass.3 = bf16[8,240,32,128]{3,2,1,0:T(8,128)(2,1)} custom-call(s32[3]{0:T(128)S(1)} %pad_add_fusion.ids_ref, bf16[4,240,640]{2,1,0:T(8,128)(2,1)S(1)} %time_inverse.6.refs_0_, bf16[4,240,640]{2,1,0:T(8,128)(2,1)S(1)} %collective-permute-done.38.refs_1_, bf16[4,240,32,128]{3,2,1,0:T(8,128)(2,1)} %get-tuple-element.80.refs_2_, ...), custom_call_target="tpu_custom_call", output_to_operand_aliasing={{}: (7, {})} | custom-call | flops 1936000000 | bytes 1760000 | tf_op jit(solution)/shard_map/input_pass/pallas_call | solution.py:375
  (163 shorter events, 72.8 us)
Async XLA Ops:
  16.5 13.1 %collective-permute-start.5 = (bf16[4,240,640]{2,1,0:T(8,128)(2,1)}, bf16[4,240,640]{2,1,0:T(8,128)(2,1)S(1)}, u32[]{:S(2)}, u32[]{:S(2)}) collective-permute-start(bf16[4,240,640]{2,1,0:T(8,128)(2,1)} %get-tuple-element.49), channel_id=1, source_target_pairs={{0,1},{1,0},{2,3},{3,2},{4,5},{5,4},{6,7},{7,6},{8,9},{9,8},{10,11... | collective-permute-start | bytes 3686408 | tf_op jit(solution)/shard_map/ppermute | solution.py:814
  31.0 17.1 %collective-permute-start.6 = (bf16[4,4,72,256]{3,2,1,0:T(8,128)(2,1)S(1)}, bf16[4,4,72,256]{3,2,1,0:T(8,128)(2,1)S(1)}, u32[]{:S(2)}, u32[]{:S(2)}) collective-permute-start(bf16[4,4,72,256]{3,2,1,0:T(8,128)(2,1)S(1)} %get-tuple-element.51), channel_id=1, source_target_pairs={{0,2},{2,0},{1,3},{3,1},{4,6},{6,4},{5,7},{7,5},{8,10},{10,8},{9,1... | collective-permute-start | bytes 1769480 | tf_op jit(solution)/shard_map/ppermute | solution.py:814
  35.4 24.8 %collective-permute-start.1 = (bf16[4,4,72,256]{3,2,1,0:T(8,128)(2,1)S(1)}, bf16[4,4,72,256]{3,2,1,0:T(8,128)(2,1)S(1)}, u32[]{:S(2)}, u32[]{:S(2)}) collective-permute-start(bf16[4,4,72,256]{3,2,1,0:T(8,128)(2,1)S(1)} %get-tuple-element.47), channel_id=1, source_target_pairs={{0,2},{2,0},{1,3},{3,1},{4,6},{6,4},{5,7},{7,5},{8,10},{10,8},{9,1... | collective-permute-start | bytes 1769480 | tf_op jit(solution)/shard_map/ppermute | solution.py:814
  48.3 16.0 %collective-permute-start.9 = (bf16[1,4,72,256]{3,2,1,0:T(8,128)(2,1)S(1)}, bf16[1,4,72,256]{3,2,1,0:T(8,128)(2,1)S(1)}, u32[]{:S(2)}, u32[]{:S(2)}) collective-permute-start(bf16[1,4,72,256]{3,2,1,0:T(8,128)(2,1)S(1)} %get-tuple-element.94), channel_id=1, source_target_pairs={{0,12},{4,0},{8,4},{12,8},{1,13},{5,1},{9,5},{13,9},{2,14},{6,2},{... | collective-permute-start | bytes 442376 | tf_op jit(solution)/shard_map/ppermute | solution.py:821
  52.6 12.9 %collective-permute-start.8 = (bf16[1,4,72,256]{3,2,1,0:T(8,128)(2,1)S(1)}, bf16[1,4,72,256]{3,2,1,0:T(8,128)(2,1)S(1)}, u32[]{:S(2)}, u32[]{:S(2)}) collective-permute-start(bf16[1,4,72,256]{3,2,1,0:T(8,128)(2,1)S(1)} %get-tuple-element.95), channel_id=1, source_target_pairs={{0,8},{4,12},{8,0},{12,4},{1,9},{5,13},{9,1},{13,5},{2,10},{6,14},... | collective-permute-start | bytes 442376 | tf_op jit(solution)/shard_map/ppermute | solution.py:821
  52.6 12.9 %collective-permute-start.7 = (bf16[1,4,72,256]{3,2,1,0:T(8,128)(2,1)S(1)}, bf16[1,4,72,256]{3,2,1,0:T(8,128)(2,1)S(1)}, u32[]{:S(2)}, u32[]{:S(2)}) collective-permute-start(bf16[1,4,72,256]{3,2,1,0:T(8,128)(2,1)S(1)} %get-tuple-element.96), channel_id=1, source_target_pairs={{0,4},{4,8},{8,12},{12,0},{1,5},{5,9},{9,13},{13,1},{2,6},{6,10},{... | collective-permute-start | bytes 442376 | tf_op jit(solution)/shard_map/ppermute | solution.py:821
  64.3 12.8 %collective-permute-start.3 = (bf16[1,4,72,256]{3,2,1,0:T(8,128)(2,1)S(1)}, bf16[1,4,72,256]{3,2,1,0:T(8,128)(2,1)S(1)}, u32[]{:S(2)}, u32[]{:S(2)}) collective-permute-start(bf16[1,4,72,256]{3,2,1,0:T(8,128)(2,1)S(1)} %get-tuple-element.99), channel_id=1, source_target_pairs={{0,8},{4,12},{8,0},{12,4},{1,9},{5,13},{9,1},{13,5},{2,10},{6,14},... | collective-permute-start | bytes 442376 | tf_op jit(solution)/shard_map/ppermute | solution.py:821
  64.3 12.8 %collective-permute-start.2 = (bf16[1,4,72,256]{3,2,1,0:T(8,128)(2,1)S(1)}, bf16[1,4,72,256]{3,2,1,0:T(8,128)(2,1)S(1)}, u32[]{:S(2)}, u32[]{:S(2)}) collective-permute-start(bf16[1,4,72,256]{3,2,1,0:T(8,128)(2,1)S(1)} %get-tuple-element.100), channel_id=1, source_target_pairs={{0,4},{4,8},{8,12},{12,0},{1,5},{5,9},{9,13},{13,1},{2,6},{6,10},{... | collective-permute-start | bytes 442376 | tf_op jit(solution)/shard_map/ppermute | solution.py:821
  111.4 12.9 %collective-permute-start.23 = (bf16[1,4,72,256]{3,2,1,0:T(8,128)(2,1)S(1)}, bf16[1,4,72,256]{3,2,1,0:T(8,128)(2,1)S(1)}, u32[]{:S(2)}, u32[]{:S(2)}) collective-permute-start(bf16[1,4,72,256]{3,2,1,0:T(8,128)(2,1)S(1)} %get-tuple-element.66), channel_id=1, source_target_pairs={{0,8},{4,12},{8,0},{12,4},{1,9},{5,13},{9,1},{13,5},{2,10},{6,14},... | collective-permute-start | bytes 442376 | tf_op jit(solution)/shard_map/ppermute | solution.py:821
  113.5 10.8 %collective-permute-start.24 = (bf16[1,4,72,256]{3,2,1,0:T(8,128)(2,1)S(1)}, bf16[1,4,72,256]{3,2,1,0:T(8,128)(2,1)S(1)}, u32[]{:S(2)}, u32[]{:S(2)}) collective-permute-start(bf16[1,4,72,256]{3,2,1,0:T(8,128)(2,1)S(1)} %get-tuple-element.67), channel_id=1, source_target_pairs={{0,4},{4,8},{8,12},{12,0},{1,5},{5,9},{9,13},{13,1},{2,6},{6,10},{... | collective-permute-start | bytes 442376 | tf_op jit(solution)/shard_map/ppermute | solution.py:821
  124.4 15.4 %collective-permute-start.25 = (bf16[4,4,72,256]{3,2,1,0:T(8,128)(2,1)S(1)}, bf16[4,4,72,256]{3,2,1,0:T(8,128)(2,1)S(1)}, u32[]{:S(2)}, u32[]{:S(2)}) collective-permute-start(bf16[4,4,72,256]{3,2,1,0:T(8,128)(2,1)S(1)} %constant_dynamic-update-slice_fusion.4.refs_0_), channel_id=1, source_target_pairs={{0,2},{2,0},{1,3},{3,1},{4,6},{6,4},{5,7},{7,5},{8,10},{10,8},{9,1... | collective-permute-start | bytes 1769480 | tf_op jit(solution)/shard_map/ppermute | solution.py:814
  126.1 12.9 %collective-permute-start.13 = (bf16[1,4,72,256]{3,2,1,0:T(8,128)(2,1)S(1)}, bf16[1,4,72,256]{3,2,1,0:T(8,128)(2,1)S(1)}, u32[]{:S(2)}, u32[]{:S(2)}) collective-permute-start(bf16[1,4,72,256]{3,2,1,0:T(8,128)(2,1)S(1)} %get-tuple-element.58), channel_id=1, source_target_pairs={{0,8},{4,12},{8,0},{12,4},{1,9},{5,13},{9,1},{13,5},{2,10},{6,14},... | collective-permute-start | bytes 442376 | tf_op jit(solution)/shard_map/ppermute | solution.py:821
  127.0 12.0 %collective-permute-start.14 = (bf16[1,4,72,256]{3,2,1,0:T(8,128)(2,1)S(1)}, bf16[1,4,72,256]{3,2,1,0:T(8,128)(2,1)S(1)}, u32[]{:S(2)}, u32[]{:S(2)}) collective-permute-start(bf16[1,4,72,256]{3,2,1,0:T(8,128)(2,1)S(1)} %get-tuple-element.59), channel_id=1, source_target_pairs={{0,4},{4,8},{8,12},{12,0},{1,5},{5,9},{9,13},{13,1},{2,6},{6,10},{... | collective-permute-start | bytes 442376 | tf_op jit(solution)/shard_map/ppermute | solution.py:821
  139.1 10.7 %collective-permute-start.15 = (bf16[4,4,72,256]{3,2,1,0:T(8,128)(2,1)S(1)}, bf16[4,4,72,256]{3,2,1,0:T(8,128)(2,1)S(1)}, u32[]{:S(2)}, u32[]{:S(2)}) collective-permute-start(bf16[4,4,72,256]{3,2,1,0:T(8,128)(2,1)S(1)} %constant_dynamic-update-slice_fusion.refs_0_), channel_id=1, source_target_pairs={{0,2},{2,0},{1,3},{3,1},{4,6},{6,4},{5,7},{7,5},{8,10},{10,8},{9,1... | collective-permute-start | bytes 1769480 | tf_op jit(solution)/shard_map/ppermute | solution.py:814
  142.3 10.0 %collective-permute-start.26 = (bf16[4,240,640]{2,1,0:T(8,128)(2,1)}, bf16[4,240,640]{2,1,0:T(8,128)(2,1)}, u32[]{:S(2)}, u32[]{:S(2)}) collective-permute-start(bf16[4,240,640]{2,1,0:T(8,128)(2,1)} %time_inverse.5.refs_0_), channel_id=1, source_target_pairs={{0,1},{1,0},{2,3},{3,2},{4,5},{5,4},{6,7},{7,6},{8,9},{9,8},{10,11... | collective-permute-start | bytes 3686408 | tf_op jit(solution)/shard_map/ppermute | solution.py:814
  152.2 43.8 %collective-permute-start.16 = (bf16[4,240,640]{2,1,0:T(8,128)(2,1)}, bf16[4,240,640]{2,1,0:T(8,128)(2,1)}, u32[]{:S(2)}, u32[]{:S(2)}) collective-permute-start(bf16[4,240,640]{2,1,0:T(8,128)(2,1)} %time_inverse.4.refs_0_), channel_id=1, source_target_pairs={{0,1},{1,0},{2,3},{3,2},{4,5},{5,4},{6,7},{7,6},{8,9},{9,8},{10,11... | collective-permute-start | bytes 3686408 | tf_op jit(solution)/shard_map/ppermute | solution.py:814
  195.5 39.6 %collective-permute-start.27 = (bf16[4,240,640]{2,1,0:T(8,128)(2,1)S(1)}, bf16[4,240,640]{2,1,0:T(8,128)(2,1)S(1)}, u32[]{:S(2)}, u32[]{:S(2)}) collective-permute-start(bf16[4,240,640]{2,1,0:T(8,128)(2,1)S(1)} %get-tuple-element.69), channel_id=1, source_target_pairs={{0,1},{1,0},{2,3},{3,2},{4,5},{5,4},{6,7},{7,6},{8,9},{9,8},{10,11... | collective-permute-start | bytes 3686408 | tf_op jit(solution)/shard_map/ppermute | solution.py:814
  236.5 16.2 %collective-permute-start.28 = (bf16[4,4,72,256]{3,2,1,0:T(8,128)(2,1)S(1)}, bf16[4,4,72,256]{3,2,1,0:T(8,128)(2,1)S(1)}, u32[]{:S(2)}, u32[]{:S(2)}) collective-permute-start(bf16[4,4,72,256]{3,2,1,0:T(8,128)(2,1)S(1)} %get-tuple-element.71), channel_id=1, source_target_pairs={{0,2},{2,0},{1,3},{3,1},{4,6},{6,4},{5,7},{7,5},{8,10},{10,8},{9,1... | collective-permute-start | bytes 1769480 | tf_op jit(solution)/shard_map/ppermute | solution.py:814
  239.3 25.6 %collective-permute-start.18 = (bf16[4,4,72,256]{3,2,1,0:T(8,128)(2,1)S(1)}, bf16[4,4,72,256]{3,2,1,0:T(8,128)(2,1)S(1)}, u32[]{:S(2)}, u32[]{:S(2)}) collective-permute-start(bf16[4,4,72,256]{3,2,1,0:T(8,128)(2,1)S(1)} %get-tuple-element.63), channel_id=1, source_target_pairs={{0,2},{2,0},{1,3},{3,1},{4,6},{6,4},{5,7},{7,5},{8,10},{10,8},{9,1... | collective-permute-start | bytes 1769480 | tf_op jit(solution)/shard_map/ppermute | solution.py:814
  252.9 17.4 %collective-permute-start.31 = (bf16[1,4,72,256]{3,2,1,0:T(8,128)(2,1)S(1)}, bf16[1,4,72,256]{3,2,1,0:T(8,128)(2,1)S(1)}, u32[]{:S(2)}, u32[]{:S(2)}) collective-permute-start(bf16[1,4,72,256]{3,2,1,0:T(8,128)(2,1)S(1)} %get-tuple-element.86), channel_id=1, source_target_pairs={{0,12},{4,0},{8,4},{12,8},{1,13},{5,1},{9,5},{13,9},{2,14},{6,2},{... | collective-permute-start | bytes 442376 | tf_op jit(solution)/shard_map/ppermute | solution.py:821
  255.9 16.3 %collective-permute-start.30 = (bf16[1,4,72,256]{3,2,1,0:T(8,128)(2,1)S(1)}, bf16[1,4,72,256]{3,2,1,0:T(8,128)(2,1)S(1)}, u32[]{:S(2)}, u32[]{:S(2)}) collective-permute-start(bf16[1,4,72,256]{3,2,1,0:T(8,128)(2,1)S(1)} %get-tuple-element.87), channel_id=1, source_target_pairs={{0,8},{4,12},{8,0},{12,4},{1,9},{5,13},{9,1},{13,5},{2,10},{6,14},... | collective-permute-start | bytes 442376 | tf_op jit(solution)/shard_map/ppermute | solution.py:821
  258.3 14.0 %collective-permute-start.29 = (bf16[1,4,72,256]{3,2,1,0:T(8,128)(2,1)S(1)}, bf16[1,4,72,256]{3,2,1,0:T(8,128)(2,1)S(1)}, u32[]{:S(2)}, u32[]{:S(2)}) collective-permute-start(bf16[1,4,72,256]{3,2,1,0:T(8,128)(2,1)S(1)} %get-tuple-element.88), channel_id=1, source_target_pairs={{0,4},{4,8},{8,12},{12,0},{1,5},{5,9},{9,13},{13,1},{2,6},{6,10},{... | collective-permute-start | bytes 442376 | tf_op jit(solution)/shard_map/ppermute | solution.py:821
  268.0 15.7 %collective-permute-start.20 = (bf16[1,4,72,256]{3,2,1,0:T(8,128)(2,1)S(1)}, bf16[1,4,72,256]{3,2,1,0:T(8,128)(2,1)S(1)}, u32[]{:S(2)}, u32[]{:S(2)}) collective-permute-start(bf16[1,4,72,256]{3,2,1,0:T(8,128)(2,1)S(1)} %get-tuple-element.91), channel_id=1, source_target_pairs={{0,8},{4,12},{8,0},{12,4},{1,9},{5,13},{9,1},{13,5},{2,10},{6,14},... | collective-permute-start | bytes 442376 | tf_op jit(solution)/shard_map/ppermute | solution.py:821
  270.3 13.3 %collective-permute-start.19 = (bf16[1,4,72,256]{3,2,1,0:T(8,128)(2,1)S(1)}, bf16[1,4,72,256]{3,2,1,0:T(8,128)(2,1)S(1)}, u32[]{:S(2)}, u32[]{:S(2)}) collective-permute-start(bf16[1,4,72,256]{3,2,1,0:T(8,128)(2,1)S(1)} %get-tuple-element.92), channel_id=1, source_target_pairs={{0,4},{4,8},{8,12},{12,0},{1,5},{5,9},{9,13},{13,1},{2,6},{6,10},{... | collective-permute-start | bytes 442376 | tf_op jit(solution)/shard_map/ppermute | solution.py:821
  322.2 28.8 %collective-permute-start.34 = (bf16[1,4,72,256]{3,2,1,0:T(8,128)(2,1)S(1)}, bf16[1,4,72,256]{3,2,1,0:T(8,128)(2,1)S(1)}, u32[]{:S(2)}, u32[]{:S(2)}) collective-permute-start(bf16[1,4,72,256]{3,2,1,0:T(8,128)(2,1)S(1)} %get-tuple-element.77), channel_id=1, source_target_pairs={{0,12},{4,0},{8,4},{12,8},{1,13},{5,1},{9,5},{13,9},{2,14},{6,2},{... | collective-permute-start | bytes 442376 | tf_op jit(solution)/shard_map/ppermute | solution.py:821
  322.3 28.7 %collective-permute-start.35 = (bf16[1,4,72,256]{3,2,1,0:T(8,128)(2,1)S(1)}, bf16[1,4,72,256]{3,2,1,0:T(8,128)(2,1)S(1)}, u32[]{:S(2)}, u32[]{:S(2)}) collective-permute-start(bf16[1,4,72,256]{3,2,1,0:T(8,128)(2,1)S(1)} %get-tuple-element.78), channel_id=1, source_target_pairs={{0,8},{4,12},{8,0},{12,4},{1,9},{5,13},{9,1},{13,5},{2,10},{6,14},... | collective-permute-start | bytes 442376 | tf_op jit(solution)/shard_map/ppermute | solution.py:821
  324.3 26.8 %collective-permute-start.36 = (bf16[1,4,72,256]{3,2,1,0:T(8,128)(2,1)S(1)}, bf16[1,4,72,256]{3,2,1,0:T(8,128)(2,1)S(1)}, u32[]{:S(2)}, u32[]{:S(2)}) collective-permute-start(bf16[1,4,72,256]{3,2,1,0:T(8,128)(2,1)S(1)} %get-tuple-element.79), channel_id=1, source_target_pairs={{0,4},{4,8},{8,12},{12,0},{1,5},{5,9},{9,13},{13,1},{2,6},{6,10},{... | collective-permute-start | bytes 442376 | tf_op jit(solution)/shard_map/ppermute | solution.py:821
  328.1 20.5 %collective-permute-start.40 = (bf16[1,4,72,256]{3,2,1,0:T(8,128)(2,1)S(1)}, bf16[1,4,72,256]{3,2,1,0:T(8,128)(2,1)S(1)}, u32[]{:S(2)}, u32[]{:S(2)}) collective-permute-start(bf16[1,4,72,256]{3,2,1,0:T(8,128)(2,1)S(1)} %get-tuple-element.83), channel_id=1, source_target_pairs={{0,8},{4,12},{8,0},{12,4},{1,9},{5,13},{9,1},{13,5},{2,10},{6,14},... | collective-permute-start | bytes 442376 | tf_op jit(solution)/shard_map/ppermute | solution.py:821
  335.3 14.9 %collective-permute-start.41 = (bf16[1,4,72,256]{3,2,1,0:T(8,128)(2,1)S(1)}, bf16[1,4,72,256]{3,2,1,0:T(8,128)(2,1)S(1)}, u32[]{:S(2)}, u32[]{:S(2)}) collective-permute-start(bf16[1,4,72,256]{3,2,1,0:T(8,128)(2,1)S(1)} %get-tuple-element.84), channel_id=1, source_target_pairs={{0,4},{4,8},{8,12},{12,0},{1,5},{5,9},{9,13},{13,1},{2,6},{6,10},{... | collective-permute-start | bytes 442376 | tf_op jit(solution)/shard_map/ppermute | solution.py:821
  350.3 16.9 %collective-permute-start.42 = (bf16[4,4,72,256]{3,2,1,0:T(8,128)(2,1)S(1)}, bf16[4,4,72,256]{3,2,1,0:T(8,128)(2,1)S(1)}, u32[]{:S(2)}, u32[]{:S(2)}) collective-permute-start(bf16[4,4,72,256]{3,2,1,0:T(8,128)(2,1)S(1)} %constant_dynamic-update-slice_fusion.12.refs_6_.refs_0_), channel_id=1, source_target_pairs={{0,2},{2,0},{1,3},{3,1},{4,6},{6,4},{5,7},{7,5},{8,10},{10,8},{9,1... | collective-permute-start | bytes 1769480 | tf_op jit(solution)/shard_map/ppermute | solution.py:814
  351.1 24.2 %collective-permute-start.37 = (bf16[4,4,72,256]{3,2,1,0:T(8,128)(2,1)S(1)}, bf16[4,4,72,256]{3,2,1,0:T(8,128)(2,1)S(1)}, u32[]{:S(2)}, u32[]{:S(2)}) collective-permute-start(bf16[4,4,72,256]{3,2,1,0:T(8,128)(2,1)S(1)} %constant_dynamic-update-slice_fusion.8.refs_0_), channel_id=1, source_target_pairs={{0,2},{2,0},{1,3},{3,1},{4,6},{6,4},{5,7},{7,5},{8,10},{10,8},{9,1... | collective-permute-start | bytes 1769480 | tf_op jit(solution)/shard_map/ppermute | solution.py:814
  376.8 19.1 %collective-permute-start.38 = (bf16[4,240,640]{2,1,0:T(8,128)(2,1)S(1)}, bf16[4,240,640]{2,1,0:T(8,128)(2,1)S(1)}, u32[]{:S(2)}, u32[]{:S(2)}) collective-permute-start(bf16[4,240,640]{2,1,0:T(8,128)(2,1)S(1)} %time_inverse.6.refs_0_), channel_id=1, source_target_pairs={{0,1},{1,0},{2,3},{3,2},{4,5},{5,4},{6,7},{7,6},{8,9},{9,8},{10,11... | collective-permute-start | bytes 3686408 | tf_op jit(solution)/shard_map/ppermute | solution.py:814
  (42 other events, 505.2 us)

commit v3 on v2

--- a/solution.py
+++ b/solution.py
@@ -30,6 +30,11 @@
 WEIGHT_SIZES = (8,)
 WHOLE = True
 ORDERED = False
+QUEUE_IN = True
+QUEUE_OUT = False
+EARLY = False
+FAR = True
+LAST_ORDERED = False
 
 
 def wave_parts(length, mode_count, halfband):
@@ -391,6 +396,10 @@
     )(ids, *inputs, *after)
 
 
+def far(a):
+    return pltpu.with_memory_space_constraint(a, pltpu.HBM) if FAR else a
+
+
 def pick_block(a, which):
     return pl.BlockSpec((None,) + a.shape[1:], lambda z, ids, n=a.ndim: (ids[which],) + (0,) * (n - 1))
 
@@ -417,7 +426,7 @@
         lax.fori_loop(0, plan.grid_rows // step, body, 0)
         gather_x(plan, tiles, us, tables, outs)
 
-    tabs = [jnp.asarray(t[3]) for t in tiles]
+    tabs = [far(jnp.asarray(t[3])) for t in tiles]
     out = jax.ShapeDtypeStruct((zc, plan.grid_rows, plan.wide), jnp.bfloat16)
     block = pl.BlockSpec((1, plan.grid_rows, plan.wide), lambda z, ids: (at + z, 0, 0))
     fspec = pl.BlockSpec((1, plan.grid_rows, plan.rows, LX), lambda z, ids: (z0 + at + z, 0, 0, 0))
@@ -432,7 +441,7 @@
 
 def field_pass(plan, ids, tiles, windows, own, other, field, point, ty, ty_inv, xi, z0, zc, at, count, after, prev, cot=None, bias=None):
     first = cot is not None
-    tabs = [jnp.asarray(t[3]) for t in tiles] if first else []
+    tabs = [far(jnp.asarray(t[3])) for t in tiles] if first else []
     block_rows = 4 * WIDTH
     half = plan.rows // 2
     pair = 2 * GROUP
@@ -536,7 +545,7 @@
     )
 
 
-def time_forward(plan, ids, own, other, table):
+def time_forward(plan, ids, own, other, table, after):
     zc = own.shape[0]
 
     def kernel(ids_ref, a_ref, b_ref, m_ref, keep, send):
@@ -553,7 +562,7 @@
     out = jax.ShapeDtypeStruct((plan.gz, zc, plan.owned, 2 * LANE), jnp.bfloat16)
     return rows_call(
         kernel, "time_forward", ids, 1, [own, other, table],
-        [whole_block(own), whole_block(other), pick_block(table, 2)], [out, out], [whole_block(out)] * 2, [], 0.4 * zc,
+        [whole_block(own), whole_block(other), pick_block(table, 2)], [out, out], [whole_block(out)] * 2, [], 0.4 * zc, after,
     )
 
 
@@ -616,16 +625,17 @@
     )
 
 
-def depth_inverse(plan, ids, keep, got, table, chunks):
+def depth_inverse(plan, ids, keep, got, table, chunk, chunks, after):
     octets = plan.owned // GROUP
     zc = plan.depth // chunks
-    count = plan.gz * plan.depth
     cut = plan.gz if SHIFTS else 1
 
     def kernel(ids_ref, a_ref, b_ref, m_ref, *refs):
         outs, buf, out = refs[:-2], refs[-2], refs[-1]
         buf[0] = a_ref[...].astype(jnp.float32)
         buf[1] = b_ref[...].astype(jnp.float32)
+        m = m_ref[...].reshape(2 * plan.gz, plan.depth * GROUP, -1)
+        m = m[:, chunk * zc * GROUP : (chunk + 1) * zc * GROUP].reshape(2 * plan.gz * zc * GROUP, -1)
         for o in range(octets):
             rows = slice(o * GROUP, (o + 1) * GROUP)
             x = [
@@ -633,27 +643,23 @@
                 for h in range(plan.ta)
                 for s in range(2)
             ]
-            y = dot(m_ref[...], jnp.concatenate(x, 0).astype(jnp.bfloat16))
-            y = y.reshape(2, count, GROUP, LANE)
+            y = dot(m, jnp.concatenate(x, 0).astype(jnp.bfloat16))
+            y = y.reshape(2, plan.gz * zc, GROUP, LANE)
             for s in range(2):
                 out[:, rows, s * LANE : (s + 1) * LANE] = y[s]
-        for c in range(chunks):
-            for k in range(plan.gz):
-                at = k * plan.depth + c * zc
-                outs[c * cut + k % cut][k // cut] = out[at : at + zc].astype(jnp.bfloat16)
+        for k in range(plan.gz):
+            outs[k % cut][k // cut] = out[k * zc : (k + 1) * zc].astype(jnp.bfloat16)
 
     shape = jax.ShapeDtypeStruct((plan.gz // cut, zc, plan.owned, 2 * LANE), jnp.bfloat16)
-    n = chunks * cut
-    flat = rows_call(
+    return rows_call(
         kernel, "depth_inverse", ids, 1, [keep, got, table],
         [whole_block(keep), whole_block(got), pick_block(table, 1)],
-        [shape] * n, [pl.BlockSpec(shape.shape, lambda *i: (0, 0, 0, 0))] * n,
+        [shape] * cut, [pl.BlockSpec(shape.shape, lambda *i: (0, 0, 0, 0))] * cut,
         [
             pltpu.VMEM((plan.ta, plan.kz, plan.owned, 2 * LANE), jnp.float32),
-            pltpu.VMEM((count, plan.owned, 2 * LANE), jnp.float32),
-        ], 1.4,
-    )
-    return [flat[c * cut : (c + 1) * cut] for c in range(chunks)]
+            pltpu.VMEM((plan.gz * zc, plan.owned, 2 * LANE), jnp.float32),
+        ], 1.0, after,
+    )
 
 
 def swap_pairs(v):
@@ -796,10 +802,10 @@
     zc = plan.depth // chunks
     ids = jnp.stack([gz_at * plan.col + col_at, gz_at * plan.ta + ta_at, ta_at]).astype(jnp.int32)
     y_table = plan.y_tables()
-    ty, ty_inv = jnp.asarray(y_table), jnp.asarray(np.swapaxes(y_table, 1, 2).copy())
+    ty, ty_inv = far(jnp.asarray(y_table)), far(jnp.asarray(np.swapaxes(y_table, 1, 2).copy()))
     tiles = plan.x_tiles()
     windows, xi = plan.x_windows()
-    xi = jnp.asarray(xi)
+    xi = far(jnp.asarray(xi))
     zf, zi = (jnp.asarray(t) for t in plan.z_tables())
     t_fwd, t_inv = (jnp.asarray(t) for t in plan.t_tables(False))
     tw_fwd, tw_inv = (jnp.asarray(t) for t in plan.t_tables(True))
@@ -821,20 +827,26 @@
             moved.append(lax.ppermute(blocks[k], "gz", [(d, (d + sign * k) % plan.gz) for d in range(plan.gz)]))
         return moved
 
-    def outward(own, other, table):
-        keep, send = time_forward(plan, ids, own, swap(other, "col"), table)
+    def outward(own, other, table, before):
+        after = [before[-1]] if before and QUEUE_OUT else []
+        keep, send = time_forward(plan, ids, own, swap(other, "col"), table, after)
         total = (keep.astype(jnp.float32) + swap(send, "ta").astype(jnp.float32)).astype(jnp.bfloat16)
         blocks = [total[k : k + 1] for k in range(plan.gz)] if SHIFTS else [total]
-        return spread(blocks, 1), send
+        return spread(blocks, 1), total
 
     def collect(pieces):
         keep, send = depth_forward(plan, ids, pieces, zf)
         return keep, swap(send, "ta")
 
-    def inward(keep, send):
+    def inward(keep, send, beside=None):
         out = []
-        for chunk in depth_inverse(plan, ids, keep, swap(send, "ta"), zi, chunks):
-            mine = spread(chunk, -1)
+        got = swap(send, "ta")
+        for n in range(chunks):
+            after = out[-1][0] if out and QUEUE_IN else []
+            if n == 1 and beside is not None and EARLY:
+                after = [*after, *beside(blocks[:1])]
+            blocks = depth_inverse(plan, ids, keep, got, zi, n, chunks, after)
+            mine = spread(blocks, -1)
             if len(mine) > 1:
                 mine = [jnp.concatenate(mine, 0)]
             out.append((mine, [swap(m, "ta") for m in mine]))
@@ -851,7 +863,7 @@
         for m in range(PARTS):
             after = [sent[n - 1]] if n and m == 1 else []
             made = analyse_xy(plan, ids, tiles, field, ty, n * zc, zc, m * sub, sub, after, made)
-        moved, send = outward(*made, t_fwd)
+        moved, send = outward(*made, t_fwd, sent)
         pieces.append(moved)
         sent.append(send)
     spec = collect(pieces)
@@ -860,7 +872,7 @@
     pieces, gprime, sent = [], [], []
     for n in range(chunks):
         made = []
-        plane = planes(arrived[n], tw_inv, gprime[-1:] if n and ORDERED else [])
+        plane = planes(arrived[n], tw_inv, [far(gprime[-1])] if n and ORDERED else [])
         for m in range(PARTS):
             after = [sent[n - 1]] if n and m == 1 else []
             made = field_pass(
@@ -869,20 +881,29 @@
             )
         g, own, other = made
         gprime.append(g)
-        moved, send = outward(own, other, tw_fwd)
+        moved, send = outward(own, other, tw_fwd, sent)
         pieces.append(moved)
         sent.append(send)
     grad = collect(pieces)
     back = back_modes(plan, ids, grad, weights, perm)
-    arrived = inward(*back)
-    weight_grad, at = None, 0
-    for n, count in enumerate(WEIGHT_SIZES):
-        after = arrived[0][0] if n == len(WEIGHT_SIZES) - 1 else []
-        weight_grad = weight_modes(plan, ids, spec, grad, perm, unit, at, count, weight_grad, after)
-        at += count
+    weight_grad = None
+
+    def beside(first):
+        nonlocal weight_grad
+        at = 0
+        for count in WEIGHT_SIZES:
+            weight_grad = weight_modes(plan, ids, spec, grad, perm, unit, at, count, weight_grad, first if at == 0 else [])
+            at += count
+        return [far(weight_grad)]
+
+    arrived = inward(*back, beside)
+    if not EARLY:
+        beside([])
     made = []
     for n in range(chunks):
-        plane = planes(arrived[n], t_inv, [weight_grad] if n == 0 else [])
+        after = [far(weight_grad)] if n == 0 and not EARLY else []
+        after += [far(made[0])] if n and LAST_ORDERED else []
+        plane = planes(arrived[n], t_inv, after)
         made = field_pass(
             plan, ids, tiles, windows, *plane, gprime[n], point_weight, ty, ty_inv, xi, n * zc, zc, 0, zc, [], made
         )

time: 414 us -> 403 us (0.973)
  local copies, waits for them, and re-layouts: 14 us -> 0.54 us
  starting transfers between devices: 66.4 us -> 54.6 us
  waiting for transfers between devices: 123 us -> 134 us
    unnamed x73 -> x55, local copies, waits for them, and re-layouts: 13.8 us -> 0.32 us
    ppermute x24, waiting for transfers between devices: 51.9 us -> 62.5 us  [spread(): lax.ppermute(blocks[k], 'gz', [(d, (d + sign * k) % plan.gz) for d in ran...]
    ppermute x24, starting transfers between devices: 49.9 us -> 39.5 us  [spread(): lax.ppermute(blocks[k], 'gz', [(d, (d + sign * k) % plan.gz) for d in ran...]
    pallas_call x21 -> x23, Pallas kernels: 209 us -> 212 us  [rows_call(): pl.pallas_call(body, grid_spec=pltpu.PrefetchScalarGridSpec(num_scalar_pr...]
  transfers between devices with their start and end apart: 44 -> 44, of which waited for: 23 -> 24; matrix products, arithmetic and copies ran while one was open for 0% -> 0% of each run, Pallas kernels for 33% -> 35%
where the time goes in v3:
time: 403 us; the launch traced here: 402 us
  Pallas kernels  212 us (53%)
  waiting for transfers between devices  134 us (33%)
  starting transfers between devices  54.6 us (14%)
    pallas_call x23, Pallas kernels, rows_call(): pl.pallas_call(body, grid_spec=pltpu.PrefetchScalarGridSpec(num_scalar_pr...  212 us
    ppermute x20, waiting for transfers between devices, swap(): return lax.ppermute(a, axis, [(0, 1), (1, 0)])  71.1 us
    ppermute x24, waiting for transfers between devices, spread(): lax.ppermute(blocks[k], 'gz', [(d, (d + sign * k) % plan.gz) for d in ran...  62.5 us
    ppermute x24, starting transfers between devices, spread(): lax.ppermute(blocks[k], 'gz', [(d, (d + sign * k) % plan.gz) for d in ran...  39.5 us
    ppermute x20, starting transfers between devices, swap(): return lax.ppermute(a, axis, [(0, 1), (1, 0)])  15.1 us
  transfers between devices with their start and end apart: 44, of which 24 were waited for; matrix products, arithmetic and copies ran while one was open for 0% of the time, Pallas kernels for 35%

profile of v3, /device:TPU:0, one launch (start us, length us, event | category | flops | bytes accessed | tf_op | source)
XLA Modules:
  0.0 402.4 jit_solution(3576296114266815522)
XLA Ops:
  0.7 13.0 %analyse_xy.3 = (bf16[4,240,640]{2,1,0:T(8,128)(2,1)S(1)}, bf16[4,240,640]{2,1,0:T(8,128)(2,1)}) custom-call(s32[3]{0:T(128)S(1)} %pad_add_fusion.ids_ref, bf16[8,240,32,128]{3,2,1,0:T(8,128)(2,1)} %bitcast.19, bf16[8,384,256]{2,1,0:T(8,128)(2,1)} %constant.41.clone.refs_1_.refs_8_, bf16[1536,256]{1,0:T(8,128)(2,1)} %constant.52.clone.refs_2_.refs_9_, ...), custom_call_target="tpu_custom_call" | custom-call | flops 1232000000 | bytes 1120000 | tf_op jit(solution)/shard_map/analyse_xy/pallas_call | solution.py:380
  14.2 13.0 %analyse_xy.2 = (bf16[4,240,640]{2,1,0:T(8,128)(2,1)S(1)}, bf16[4,240,640]{2,1,0:T(8,128)(2,1)}) custom-call(s32[3]{0:T(128)S(1)} %pad_add_fusion.ids_ref, bf16[8,240,32,128]{3,2,1,0:T(8,128)(2,1)} %bitcast.20, bf16[8,384,256]{2,1,0:T(8,128)(2,1)} %constant.41.clone.refs_1_.refs_8_, bf16[1536,256]{1,0:T(8,128)(2,1)} %constant.52.clone.refs_2_.refs_9_, ...), custom_call_target="tpu_custom_call" | custom-call | flops 1232000000 | bytes 1120000 | tf_op jit(solution)/shard_map/analyse_xy/pallas_call | solution.py:380
  28.6 3.0 collective-permute-start.6
  34.4 11.4 %collective-permute-done.6 = bf16[4,4,72,256]{3,2,1,0:T(8,128)(2,1)S(1)} collective-permute-done((bf16[4,4,72,256]{3,2,1,0:T(8,128)(2,1)S(1)}, bf16[4,4,72,256]{3,2,1,0:T(8,128)(2,1)S(1)}, u32[]{:S(2)}, u32[]{:S(2)}) %collective-permute-start.6) | collective-permute-done | bytes 589856 | tf_op jit(solution)/shard_map/ppermute | solution.py:820
  46.0 4.2 %collective-permute-start.9 = (bf16[1,4,72,256]{3,2,1,0:T(8,128)(2,1)S(1)}, bf16[1,4,72,256]{3,2,1,0:T(8,128)(2,1)S(1)}, u32[]{:S(2)}, u32[]{:S(2)}) collective-permute-start(bf16[1,4,72,256]{3,2,1,0:T(8,128)(2,1)S(1)} %get-tuple-element.94), channel_id=1, source_target_pairs={{0,12},{4,0},{8,4},{12,8},{1,13},{5,1},{9,5},{13,9},{2,14},{6,2},{... | collective-permute-start | bytes 442376 | tf_op jit(solution)/shard_map/ppermute | solution.py:827
  51.2 6.6 %collective-permute-done.1 = bf16[4,4,72,256]{3,2,1,0:T(8,128)(2,1)S(1)} collective-permute-done((bf16[4,4,72,256]{3,2,1,0:T(8,128)(2,1)S(1)}, bf16[4,4,72,256]{3,2,1,0:T(8,128)(2,1)S(1)}, u32[]{:S(2)}, u32[]{:S(2)}) %collective-permute-start.1) | collective-permute-done | bytes 589856 | tf_op jit(solution)/shard_map/ppermute | solution.py:820
  58.0 3.9 collective-permute-start.4
  63.1 3.1 collective-permute-done.4.refs_3_
  66.2 8.5 %collective-permute-done.3.refs_2_ = bf16[1,4,72,256]{3,2,1,0:T(8,128)(2,1)S(1)} collective-permute-done((bf16[1,4,72,256]{3,2,1,0:T(8,128)(2,1)S(1)}, bf16[1,4,72,256]{3,2,1,0:T(8,128)(2,1)S(1)}, u32[]{:S(2)}, u32[]{:S(2)}) %collective-permute-start.3) | collective-permute-done | bytes 147488 | tf_op jit(solution)/shard_map/ppermute | solution.py:827
  77.6 6.6 %collective-permute-done.10.refs_1_ = bf16[8,72,256]{2,1,0:T(8,128)(2,1)S(1)} collective-permute-done((bf16[8,72,256]{2,1,0:T(8,128)(2,1)S(1)}, bf16[8,72,256]{2,1,0:T(8,128)(2,1)S(1)}, u32[]{:S(2)}, u32[]{:S(2)}) %collective-permute-start.10) | collective-permute-done | bytes 294944 | tf_op jit(solution)/shard_map/ppermute | solution.py:820
  84.2 16.2 %mix_modes.1 = (bf16[8,72,256]{2,1,0:T(8,128)(2,1)S(1)}, bf16[8,72,256]{2,1,0:T(8,128)(2,1)S(1)}) custom-call(s32[3]{0:T(128)S(1)} %pad_add_fusion.ids_ref, bf16[8,72,256]{2,1,0:T(8,128)(2,1)S(1)} %get-tuple-element.52.refs_0_, bf16[8,72,256]{2,1,0:T(8,128)(2,1)S(1)} %collective-permute-done.10.refs_1_, bf16[8,9600,72]{2,1,0:T(8,128)(2,1)} %bitcast.23, ...), custom_call_target="tpu_custom_call" | custom-call | flops 1870000000 | bytes 1700000 | tf_op jit(solution)/shard_map/mix_modes/pallas_call | solution.py:380
  102.0 5.7 %collective-permute-done.11.refs_1_ = bf16[8,72,256]{2,1,0:T(8,128)(2,1)S(1)} collective-permute-done((bf16[8,72,256]{2,1,0:T(8,128)(2,1)S(1)}, bf16[8,72,256]{2,1,0:T(8,128)(2,1)S(1)}, u32[]{:S(2)}, u32[]{:S(2)}) %collective-permute-start.11) | collective-permute-done | bytes 294944 | tf_op jit(solution)/shard_map/ppermute | solution.py:820
  112.8 2.8 collective-permute-done.12
  115.5 6.0 %collective-permute-done.13 = bf16[1,4,72,256]{3,2,1,0:T(8,128)(2,1)S(1)} collective-permute-done((bf16[1,4,72,256]{3,2,1,0:T(8,128)(2,1)S(1)}, bf16[1,4,72,256]{3,2,1,0:T(8,128)(2,1)S(1)}, u32[]{:S(2)}, u32[]{:S(2)}) %collective-permute-start.13) | collective-permute-done | bytes 147488 | tf_op jit(solution)/shard_map/ppermute | solution.py:827
  129.7 7.7 %collective-permute-done.23 = bf16[1,4,72,256]{3,2,1,0:T(8,128)(2,1)S(1)} collective-permute-done((bf16[1,4,72,256]{3,2,1,0:T(8,128)(2,1)S(1)}, bf16[1,4,72,256]{3,2,1,0:T(8,128)(2,1)S(1)}, u32[]{:S(2)}, u32[]{:S(2)}) %collective-permute-start.23) | collective-permute-done | bytes 147488 | tf_op jit(solution)/shard_map/ppermute | solution.py:827
  138.0 2.5 time_inverse.4.refs_0_
  140.5 7.5 %collective-permute-done.25.refs_1_ = bf16[4,4,72,256]{3,2,1,0:T(8,128)(2,1)S(1)} collective-permute-done((bf16[4,4,72,256]{3,2,1,0:T(8,128)(2,1)S(1)}, bf16[4,4,72,256]{3,2,1,0:T(8,128)(2,1)S(1)}, u32[]{:S(2)}, u32[]{:S(2)}) %collective-permute-start.25) | collective-permute-done | bytes 589856 | tf_op jit(solution)/shard_map/ppermute | solution.py:820
  149.7 40.0 %slope_pass.2 = (bf16[4,240,32,128]{3,2,1,0:T(8,128)(2,1)}, bf16[4,240,640]{2,1,0:T(8,128)(2,1)S(1)}, bf16[4,240,640]{2,1,0:T(8,128)(2,1)S(1)}) custom-call(s32[3]{0:T(128)S(1)} %pad_add_fusion.ids_ref, bf16[4,240,640]{2,1,0:T(8,128)(2,1)} %time_inverse.4.refs_0_, bf16[4,240,640]{2,1,0:T(8,128)(2,1)} %collective-permute-done.16.refs_1_, ...), custom_call_target="tpu_custom_call" | custom-call | flops 4224000000 | bytes 3840000 | tf_op jit(solution)/shard_map/slope_pass/pallas_call | solution.py:380
  190.2 40.3 %slope_pass.3 = (bf16[4,240,32,128]{3,2,1,0:T(8,128)(2,1)}, bf16[4,240,640]{2,1,0:T(8,128)(2,1)S(1)}, bf16[4,240,640]{2,1,0:T(8,128)(2,1)S(1)}) custom-call(s32[3]{0:T(128)S(1)} %pad_add_fusion.ids_ref, bf16[4,240,640]{2,1,0:T(8,128)(2,1)S(1)} %time_inverse.5.refs_0_, bf16[4,240,640]{2,1,0:T(8,128)(2,1)} %collective-permute-done.26.refs_1_, ...), custom_call_target="tpu_custom_call" | custom-call | flops 4224000000 | bytes 3840000 | tf_op jit(solution)/shard_map/slope_pass/pallas_call | solution.py:380
  235.5 12.6 %collective-permute-done.18 = bf16[4,4,72,256]{3,2,1,0:T(8,128)(2,1)S(1)} collective-permute-done((bf16[4,4,72,256]{3,2,1,0:T(8,128)(2,1)S(1)}, bf16[4,4,72,256]{3,2,1,0:T(8,128)(2,1)S(1)}, u32[]{:S(2)}, u32[]{:S(2)}) %collective-permute-start.18) | collective-permute-done | bytes 589856 | tf_op jit(solution)/shard_map/ppermute | solution.py:820
  248.4 3.0 collective-permute-start.21
  255.6 4.8 %collective-permute-done.28 = bf16[4,4,72,256]{3,2,1,0:T(8,128)(2,1)S(1)} collective-permute-done((bf16[4,4,72,256]{3,2,1,0:T(8,128)(2,1)S(1)}, bf16[4,4,72,256]{3,2,1,0:T(8,128)(2,1)S(1)}, u32[]{:S(2)}, u32[]{:S(2)}) %collective-permute-start.28) | collective-permute-done | bytes 589856 | tf_op jit(solution)/shard_map/ppermute | solution.py:820
  260.6 3.0 collective-permute-start.31
  269.9 9.1 %collective-permute-done.30.refs_6_ = bf16[1,4,72,256]{3,2,1,0:T(8,128)(2,1)S(1)} collective-permute-done((bf16[1,4,72,256]{3,2,1,0:T(8,128)(2,1)S(1)}, bf16[1,4,72,256]{3,2,1,0:T(8,128)(2,1)S(1)}, u32[]{:S(2)}, u32[]{:S(2)}) %collective-permute-start.30) | collective-permute-done | bytes 147488 | tf_op jit(solution)/shard_map/ppermute | solution.py:827
  280.9 7.5 %collective-permute-done.32.refs_1_.refs_3_ = bf16[8,72,256]{2,1,0:T(8,128)(2,1)S(1)} collective-permute-done((bf16[8,72,256]{2,1,0:T(8,128)(2,1)S(1)}, bf16[8,72,256]{2,1,0:T(8,128)(2,1)S(1)}, u32[]{:S(2)}, u32[]{:S(2)}) %collective-permute-start.32) | collective-permute-done | bytes 294944 | tf_op jit(solution)/shard_map/ppermute | solution.py:820
  288.5 20.1 %back_modes.1 = (bf16[8,72,256]{2,1,0:T(8,128)(2,1)S(1)}, bf16[8,72,256]{2,1,0:T(8,128)(2,1)S(1)}) custom-call(s32[3]{0:T(128)S(1)} %pad_add_fusion.ids_ref, bf16[8,72,256]{2,1,0:T(8,128)(2,1)S(1)} %get-tuple-element.72.refs_0_.refs_2_, bf16[8,72,256]{2,1,0:T(8,128)(2,1)S(1)} %collective-permute-done.32.refs_1_.refs_3_, bf16[8,9600,72]{2,1,0:T(8,128)(2,1)} %bitcast.24, ...), custom_call_target="tpu_custom_call" | custom-call | flops 2200000000 | bytes 2000000 | tf_op jit(solution)/shard_map/back_modes/pallas_call | solution.py:380
  309.2 6.6 %collective-permute-done.33.refs_1_ = bf16[8,72,256]{2,1,0:T(8,128)(2,1)S(1)} collective-permute-done((bf16[8,72,256]{2,1,0:T(8,128)(2,1)S(1)}, bf16[8,72,256]{2,1,0:T(8,128)(2,1)S(1)}, u32[]{:S(2)}, u32[]{:S(2)}) %collective-permute-start.33) | collective-permute-done | bytes 294944 | tf_op jit(solution)/shard_map/ppermute | solution.py:820
  322.9 8.3 %collective-permute-done.35 = bf16[1,4,72,256]{3,2,1,0:T(8,128)(2,1)S(1)} collective-permute-done((bf16[1,4,72,256]{3,2,1,0:T(8,128)(2,1)S(1)}, bf16[1,4,72,256]{3,2,1,0:T(8,128)(2,1)S(1)}, u32[]{:S(2)}, u32[]{:S(2)}) %collective-permute-start.35) | collective-permute-done | bytes 147488 | tf_op jit(solution)/shard_map/ppermute | solution.py:827
  338.0 8.9 %collective-permute-done.38 = bf16[1,4,72,256]{3,2,1,0:T(8,128)(2,1)S(1)} collective-permute-done((bf16[1,4,72,256]{3,2,1,0:T(8,128)(2,1)S(1)}, bf16[1,4,72,256]{3,2,1,0:T(8,128)(2,1)S(1)}, u32[]{:S(2)}, u32[]{:S(2)}) %collective-permute-start.38) | collective-permute-done | bytes 147488 | tf_op jit(solution)/shard_map/ppermute | solution.py:827
  347.6 14.6 %weight_modes.1.refs_3_ = bf16[8,9600,72]{2,1,0:T(8,128)(2,1)} custom-call(s32[3]{0:T(128)S(1)} %pad_add_fusion.ids_ref, bf16[8,72,256]{2,1,0:T(8,128)(2,1)S(1)} %copy-done.12, bf16[8,72,256]{2,1,0:T(8,128)(2,1)S(1)} %copy-done.14, bf16[8,72,256]{2,1,0:T(8,128)(2,1)S(1)} %get-tuple-element.72.refs_0_.refs_2_, ...), custom_call_target="tpu_custom_call" | custom-call | flops 1584000000 | bytes 1440000 | tf_op jit(solution)/shard_map/weight_modes/pallas_call | solution.py:380
  366.7 18.0 %input_pass.2.refs_6_ = bf16[8,240,32,128]{3,2,1,0:T(8,128)(2,1)} custom-call(s32[3]{0:T(128)S(1)} %pad_add_fusion.ids_ref, bf16[4,240,640]{2,1,0:T(8,128)(2,1)S(1)} %time_inverse.7.refs_0_, bf16[4,240,640]{2,1,0:T(8,128)(2,1)S(1)} %collective-permute-done.43.refs_1_, bf16[4,240,32,128]{3,2,1,0:T(8,128)(2,1)S(1)} %bitcast.14, bf16[20,20]{1,0:T(8,128)(2,1)S(1)} %copy-done.15, ...), custom_call_target="tpu_custom_call" | custom-call | flops 1936000000 | bytes 1760000 | tf_op jit(solution)/shard_map/input_pass/pallas_call | solution.py:380
  384.7 17.7 %input_pass.3 = bf16[8,240,32,128]{3,2,1,0:T(8,128)(2,1)} custom-call(s32[3]{0:T(128)S(1)} %pad_add_fusion.ids_ref, bf16[4,240,640]{2,1,0:T(8,128)(2,1)S(1)} %time_inverse.6.refs_0_, bf16[4,240,640]{2,1,0:T(8,128)(2,1)S(1)} %collective-permute-done.41.refs_1_, bf16[4,240,32,128]{3,2,1,0:T(8,128)(2,1)S(1)} %bitcast.16, ...), custom_call_target="tpu_custom_call", output_to_operand_aliasing={{}: (7, {})} | custom-call | flops 1936000000 | bytes 1760000 | tf_op jit(solution)/shard_map/input_pass/pallas_call | solution.py:380
  (149 shorter events, 65.0 us)
Async XLA Ops:
  13.7 13.5 %collective-permute-start.5 = (bf16[4,240,640]{2,1,0:T(8,128)(2,1)}, bf16[4,240,640]{2,1,0:T(8,128)(2,1)S(1)}, u32[]{:S(2)}, u32[]{:S(2)}) collective-permute-start(bf16[4,240,640]{2,1,0:T(8,128)(2,1)} %get-tuple-element.49), channel_id=1, source_target_pairs={{0,1},{1,0},{2,3},{3,2},{4,5},{5,4},{6,7},{7,6},{8,9},{9,8},{10,11... | collective-permute-start | bytes 3686408 | tf_op jit(solution)/shard_map/ppermute | solution.py:820
  28.6 17.1 %collective-permute-start.6 = (bf16[4,4,72,256]{3,2,1,0:T(8,128)(2,1)S(1)}, bf16[4,4,72,256]{3,2,1,0:T(8,128)(2,1)S(1)}, u32[]{:S(2)}, u32[]{:S(2)}) collective-permute-start(bf16[4,4,72,256]{3,2,1,0:T(8,128)(2,1)S(1)} %get-tuple-element.51), channel_id=1, source_target_pairs={{0,2},{2,0},{1,3},{3,1},{4,6},{6,4},{5,7},{7,5},{8,10},{10,8},{9,1... | collective-permute-start | bytes 1769480 | tf_op jit(solution)/shard_map/ppermute | solution.py:820
  33.0 24.8 %collective-permute-start.1 = (bf16[4,4,72,256]{3,2,1,0:T(8,128)(2,1)S(1)}, bf16[4,4,72,256]{3,2,1,0:T(8,128)(2,1)S(1)}, u32[]{:S(2)}, u32[]{:S(2)}) collective-permute-start(bf16[4,4,72,256]{3,2,1,0:T(8,128)(2,1)S(1)} %get-tuple-element.47), channel_id=1, source_target_pairs={{0,2},{2,0},{1,3},{3,1},{4,6},{6,4},{5,7},{7,5},{8,10},{10,8},{9,1... | collective-permute-start | bytes 1769480 | tf_op jit(solution)/shard_map/ppermute | solution.py:820
  46.0 15.9 %collective-permute-start.9 = (bf16[1,4,72,256]{3,2,1,0:T(8,128)(2,1)S(1)}, bf16[1,4,72,256]{3,2,1,0:T(8,128)(2,1)S(1)}, u32[]{:S(2)}, u32[]{:S(2)}) collective-permute-start(bf16[1,4,72,256]{3,2,1,0:T(8,128)(2,1)S(1)} %get-tuple-element.94), channel_id=1, source_target_pairs={{0,12},{4,0},{8,4},{12,8},{1,13},{5,1},{9,5},{13,9},{2,14},{6,2},{... | collective-permute-start | bytes 442376 | tf_op jit(solution)/shard_map/ppermute | solution.py:827
  50.2 12.9 %collective-permute-start.8 = (bf16[1,4,72,256]{3,2,1,0:T(8,128)(2,1)S(1)}, bf16[1,4,72,256]{3,2,1,0:T(8,128)(2,1)S(1)}, u32[]{:S(2)}, u32[]{:S(2)}) collective-permute-start(bf16[1,4,72,256]{3,2,1,0:T(8,128)(2,1)S(1)} %get-tuple-element.95), channel_id=1, source_target_pairs={{0,8},{4,12},{8,0},{12,4},{1,9},{5,13},{9,1},{13,5},{2,10},{6,14},... | collective-permute-start | bytes 442376 | tf_op jit(solution)/shard_map/ppermute | solution.py:827
  50.2 12.9 %collective-permute-start.7 = (bf16[1,4,72,256]{3,2,1,0:T(8,128)(2,1)S(1)}, bf16[1,4,72,256]{3,2,1,0:T(8,128)(2,1)S(1)}, u32[]{:S(2)}, u32[]{:S(2)}) collective-permute-start(bf16[1,4,72,256]{3,2,1,0:T(8,128)(2,1)S(1)} %get-tuple-element.96), channel_id=1, source_target_pairs={{0,4},{4,8},{8,12},{12,0},{1,5},{5,9},{9,13},{13,1},{2,6},{6,10},{... | collective-permute-start | bytes 442376 | tf_op jit(solution)/shard_map/ppermute | solution.py:827
  61.9 12.8 %collective-permute-start.3 = (bf16[1,4,72,256]{3,2,1,0:T(8,128)(2,1)S(1)}, bf16[1,4,72,256]{3,2,1,0:T(8,128)(2,1)S(1)}, u32[]{:S(2)}, u32[]{:S(2)}) collective-permute-start(bf16[1,4,72,256]{3,2,1,0:T(8,128)(2,1)S(1)} %get-tuple-element.99), channel_id=1, source_target_pairs={{0,8},{4,12},{8,0},{12,4},{1,9},{5,13},{9,1},{13,5},{2,10},{6,14},... | collective-permute-start | bytes 442376 | tf_op jit(solution)/shard_map/ppermute | solution.py:827
  61.9 12.8 %collective-permute-start.2 = (bf16[1,4,72,256]{3,2,1,0:T(8,128)(2,1)S(1)}, bf16[1,4,72,256]{3,2,1,0:T(8,128)(2,1)S(1)}, u32[]{:S(2)}, u32[]{:S(2)}) collective-permute-start(bf16[1,4,72,256]{3,2,1,0:T(8,128)(2,1)S(1)} %get-tuple-element.100), channel_id=1, source_target_pairs={{0,4},{4,8},{8,12},{12,0},{1,5},{5,9},{9,13},{13,1},{2,6},{6,10},{... | collective-permute-start | bytes 442376 | tf_op jit(solution)/shard_map/ppermute | solution.py:827
  108.8 12.8 %collective-permute-start.13 = (bf16[1,4,72,256]{3,2,1,0:T(8,128)(2,1)S(1)}, bf16[1,4,72,256]{3,2,1,0:T(8,128)(2,1)S(1)}, u32[]{:S(2)}, u32[]{:S(2)}) collective-permute-start(bf16[1,4,72,256]{3,2,1,0:T(8,128)(2,1)S(1)} %get-tuple-element.58), channel_id=1, source_target_pairs={{0,8},{4,12},{8,0},{12,4},{1,9},{5,13},{9,1},{13,5},{2,10},{6,14},... | collective-permute-start | bytes 442376 | tf_op jit(solution)/shard_map/ppermute | solution.py:827
  110.8 10.8 %collective-permute-start.14 = (bf16[1,4,72,256]{3,2,1,0:T(8,128)(2,1)S(1)}, bf16[1,4,72,256]{3,2,1,0:T(8,128)(2,1)S(1)}, u32[]{:S(2)}, u32[]{:S(2)}) collective-permute-start(bf16[1,4,72,256]{3,2,1,0:T(8,128)(2,1)S(1)} %get-tuple-element.59), channel_id=1, source_target_pairs={{0,4},{4,8},{8,12},{12,0},{1,5},{5,9},{9,13},{13,1},{2,6},{6,10},{... | collective-permute-start | bytes 442376 | tf_op jit(solution)/shard_map/ppermute | solution.py:827
  121.6 16.4 %collective-permute-start.15 = (bf16[4,4,72,256]{3,2,1,0:T(8,128)(2,1)S(1)}, bf16[4,4,72,256]{3,2,1,0:T(8,128)(2,1)S(1)}, u32[]{:S(2)}, u32[]{:S(2)}) collective-permute-start(bf16[4,4,72,256]{3,2,1,0:T(8,128)(2,1)S(1)} %constant_dynamic-update-slice_fusion.refs_0_.refs_3_), channel_id=1, source_target_pairs={{0,2},{2,0},{1,3},{3,1},{4,6},{6,4},{5,7},{7,5},{8,10},{10,8},{9,1... | collective-permute-start | bytes 1769480 | tf_op jit(solution)/shard_map/ppermute | solution.py:820
  124.5 12.9 %collective-permute-start.23 = (bf16[1,4,72,256]{3,2,1,0:T(8,128)(2,1)S(1)}, bf16[1,4,72,256]{3,2,1,0:T(8,128)(2,1)S(1)}, u32[]{:S(2)}, u32[]{:S(2)}) collective-permute-start(bf16[1,4,72,256]{3,2,1,0:T(8,128)(2,1)S(1)} %get-tuple-element.66), channel_id=1, source_target_pairs={{0,8},{4,12},{8,0},{12,4},{1,9},{5,13},{9,1},{13,5},{2,10},{6,14},... | collective-permute-start | bytes 442376 | tf_op jit(solution)/shard_map/ppermute | solution.py:827
  125.4 11.9 %collective-permute-start.24 = (bf16[1,4,72,256]{3,2,1,0:T(8,128)(2,1)S(1)}, bf16[1,4,72,256]{3,2,1,0:T(8,128)(2,1)S(1)}, u32[]{:S(2)}, u32[]{:S(2)}) collective-permute-start(bf16[1,4,72,256]{3,2,1,0:T(8,128)(2,1)S(1)} %get-tuple-element.67), channel_id=1, source_target_pairs={{0,4},{4,8},{8,12},{12,0},{1,5},{5,9},{9,13},{13,1},{2,6},{6,10},{... | collective-permute-start | bytes 442376 | tf_op jit(solution)/shard_map/ppermute | solution.py:827
  137.4 10.7 %collective-permute-start.25 = (bf16[4,4,72,256]{3,2,1,0:T(8,128)(2,1)S(1)}, bf16[4,4,72,256]{3,2,1,0:T(8,128)(2,1)S(1)}, u32[]{:S(2)}, u32[]{:S(2)}) collective-permute-start(bf16[4,4,72,256]{3,2,1,0:T(8,128)(2,1)S(1)} %constant_dynamic-update-slice_fusion.4.refs_0_), channel_id=1, source_target_pairs={{0,2},{2,0},{1,3},{3,1},{4,6},{6,4},{5,7},{7,5},{8,10},{10,8},{9,1... | collective-permute-start | bytes 1769480 | tf_op jit(solution)/shard_map/ppermute | solution.py:820
  140.5 9.2 %collective-permute-start.16 = (bf16[4,240,640]{2,1,0:T(8,128)(2,1)}, bf16[4,240,640]{2,1,0:T(8,128)(2,1)}, u32[]{:S(2)}, u32[]{:S(2)}) collective-permute-start(bf16[4,240,640]{2,1,0:T(8,128)(2,1)} %time_inverse.4.refs_0_), channel_id=1, source_target_pairs={{0,1},{1,0},{2,3},{3,2},{4,5},{5,4},{6,7},{7,6},{8,9},{9,8},{10,11... | collective-permute-start | bytes 3686408 | tf_op jit(solution)/shard_map/ppermute | solution.py:820
  149.5 40.8 %collective-permute-start.26 = (bf16[4,240,640]{2,1,0:T(8,128)(2,1)S(1)}, bf16[4,240,640]{2,1,0:T(8,128)(2,1)}, u32[]{:S(2)}, u32[]{:S(2)}) collective-permute-start(bf16[4,240,640]{2,1,0:T(8,128)(2,1)S(1)} %time_inverse.5.refs_0_), channel_id=1, source_target_pairs={{0,1},{1,0},{2,3},{3,2},{4,5},{5,4},{6,7},{7,6},{8,9},{9,8},{10,11... | collective-permute-start | bytes 3686408 | tf_op jit(solution)/shard_map/ppermute | solution.py:820
  189.7 40.9 %collective-permute-start.17 = (bf16[4,240,640]{2,1,0:T(8,128)(2,1)S(1)}, bf16[4,240,640]{2,1,0:T(8,128)(2,1)S(1)}, u32[]{:S(2)}, u32[]{:S(2)}) collective-permute-start(bf16[4,240,640]{2,1,0:T(8,128)(2,1)S(1)} %get-tuple-element.61), channel_id=1, source_target_pairs={{0,1},{1,0},{2,3},{3,2},{4,5},{5,4},{6,7},{7,6},{8,9},{9,8},{10,11... | collective-permute-start | bytes 3686408 | tf_op jit(solution)/shard_map/ppermute | solution.py:820
  232.0 16.2 %collective-permute-start.18 = (bf16[4,4,72,256]{3,2,1,0:T(8,128)(2,1)S(1)}, bf16[4,4,72,256]{3,2,1,0:T(8,128)(2,1)S(1)}, u32[]{:S(2)}, u32[]{:S(2)}) collective-permute-start(bf16[4,4,72,256]{3,2,1,0:T(8,128)(2,1)S(1)} %get-tuple-element.63), channel_id=1, source_target_pairs={{0,2},{2,0},{1,3},{3,1},{4,6},{6,4},{5,7},{7,5},{8,10},{10,8},{9,1... | collective-permute-start | bytes 1769480 | tf_op jit(solution)/shard_map/ppermute | solution.py:820
  234.9 25.5 %collective-permute-start.28 = (bf16[4,4,72,256]{3,2,1,0:T(8,128)(2,1)S(1)}, bf16[4,4,72,256]{3,2,1,0:T(8,128)(2,1)S(1)}, u32[]{:S(2)}, u32[]{:S(2)}) collective-permute-start(bf16[4,4,72,256]{3,2,1,0:T(8,128)(2,1)S(1)} %get-tuple-element.71), channel_id=1, source_target_pairs={{0,2},{2,0},{1,3},{3,1},{4,6},{6,4},{5,7},{7,5},{8,10},{10,8},{9,1... | collective-permute-start | bytes 1769480 | tf_op jit(solution)/shard_map/ppermute | solution.py:820
  248.4 17.5 %collective-permute-start.21 = (bf16[1,4,72,256]{3,2,1,0:T(8,128)(2,1)S(1)}, bf16[1,4,72,256]{3,2,1,0:T(8,128)(2,1)S(1)}, u32[]{:S(2)}, u32[]{:S(2)}) collective-permute-start(bf16[1,4,72,256]{3,2,1,0:T(8,128)(2,1)S(1)} %get-tuple-element.90), channel_id=1, source_target_pairs={{0,12},{4,0},{8,4},{12,8},{1,13},{5,1},{9,5},{13,9},{2,14},{6,2},{... | collective-permute-start | bytes 442376 | tf_op jit(solution)/shard_map/ppermute | solution.py:827
  251.4 16.4 %collective-permute-start.20 = (bf16[1,4,72,256]{3,2,1,0:T(8,128)(2,1)S(1)}, bf16[1,4,72,256]{3,2,1,0:T(8,128)(2,1)S(1)}, u32[]{:S(2)}, u32[]{:S(2)}) collective-permute-start(bf16[1,4,72,256]{3,2,1,0:T(8,128)(2,1)S(1)} %get-tuple-element.91), channel_id=1, source_target_pairs={{0,8},{4,12},{8,0},{12,4},{1,9},{5,13},{9,1},{13,5},{2,10},{6,14},... | collective-permute-start | bytes 442376 | tf_op jit(solution)/shard_map/ppermute | solution.py:827
  253.6 14.2 %collective-permute-start.19 = (bf16[1,4,72,256]{3,2,1,0:T(8,128)(2,1)S(1)}, bf16[1,4,72,256]{3,2,1,0:T(8,128)(2,1)S(1)}, u32[]{:S(2)}, u32[]{:S(2)}) collective-permute-start(bf16[1,4,72,256]{3,2,1,0:T(8,128)(2,1)S(1)} %get-tuple-element.92), channel_id=1, source_target_pairs={{0,4},{4,8},{8,12},{12,0},{1,5},{5,9},{9,13},{13,1},{2,6},{6,10},{... | collective-permute-start | bytes 442376 | tf_op jit(solution)/shard_map/ppermute | solution.py:827
  260.6 9.3 %collective-permute-start.31 = (bf16[1,4,72,256]{3,2,1,0:T(8,128)(2,1)S(1)}, bf16[1,4,72,256]{3,2,1,0:T(8,128)(2,1)S(1)}, u32[]{:S(2)}, u32[]{:S(2)}) collective-permute-start(bf16[1,4,72,256]{3,2,1,0:T(8,128)(2,1)S(1)} %get-tuple-element.86), channel_id=1, source_target_pairs={{0,12},{4,0},{8,4},{12,8},{1,13},{5,1},{9,5},{13,9},{2,14},{6,2},{... | collective-permute-start | bytes 442376 | tf_op jit(solution)/shard_map/ppermute | solution.py:827
  263.6 15.4 %collective-permute-start.30 = (bf16[1,4,72,256]{3,2,1,0:T(8,128)(2,1)S(1)}, bf16[1,4,72,256]{3,2,1,0:T(8,128)(2,1)S(1)}, u32[]{:S(2)}, u32[]{:S(2)}) collective-permute-start(bf16[1,4,72,256]{3,2,1,0:T(8,128)(2,1)S(1)} %get-tuple-element.87), channel_id=1, source_target_pairs={{0,8},{4,12},{8,0},{12,4},{1,9},{5,13},{9,1},{13,5},{2,10},{6,14},... | collective-permute-start | bytes 442376 | tf_op jit(solution)/shard_map/ppermute | solution.py:827
  265.9 13.1 %collective-permute-start.29 = (bf16[1,4,72,256]{3,2,1,0:T(8,128)(2,1)S(1)}, bf16[1,4,72,256]{3,2,1,0:T(8,128)(2,1)S(1)}, u32[]{:S(2)}, u32[]{:S(2)}) collective-permute-start(bf16[1,4,72,256]{3,2,1,0:T(8,128)(2,1)S(1)} %get-tuple-element.88), channel_id=1, source_target_pairs={{0,4},{4,8},{8,12},{12,0},{1,5},{5,9},{9,13},{13,1},{2,6},{6,10},{... | collective-permute-start | bytes 442376 | tf_op jit(solution)/shard_map/ppermute | solution.py:827
  317.1 14.1 %collective-permute-start.35 = (bf16[1,4,72,256]{3,2,1,0:T(8,128)(2,1)S(1)}, bf16[1,4,72,256]{3,2,1,0:T(8,128)(2,1)S(1)}, u32[]{:S(2)}, u32[]{:S(2)}) collective-permute-start(bf16[1,4,72,256]{3,2,1,0:T(8,128)(2,1)S(1)} %get-tuple-element.78), channel_id=1, source_target_pairs={{0,8},{4,12},{8,0},{12,4},{1,9},{5,13},{9,1},{13,5},{2,10},{6,14},... | collective-permute-start | bytes 442376 | tf_op jit(solution)/shard_map/ppermute | solution.py:827
  319.4 11.8 %collective-permute-start.36 = (bf16[1,4,72,256]{3,2,1,0:T(8,128)(2,1)S(1)}, bf16[1,4,72,256]{3,2,1,0:T(8,128)(2,1)S(1)}, u32[]{:S(2)}, u32[]{:S(2)}) collective-permute-start(bf16[1,4,72,256]{3,2,1,0:T(8,128)(2,1)S(1)} %get-tuple-element.79), channel_id=1, source_target_pairs={{0,4},{4,8},{8,12},{12,0},{1,5},{5,9},{9,13},{13,1},{2,6},{6,10},{... | collective-permute-start | bytes 442376 | tf_op jit(solution)/shard_map/ppermute | solution.py:827
  332.4 29.9 %collective-permute-start.42 = (bf16[4,4,72,256]{3,2,1,0:T(8,128)(2,1)S(1)}, bf16[4,4,72,256]{3,2,1,0:T(8,128)(2,1)S(1)}, u32[]{:S(2)}, u32[]{:S(2)}) collective-permute-start(bf16[4,4,72,256]{3,2,1,0:T(8,128)(2,1)S(1)} %constant_dynamic-update-slice_fusion.8.refs_3_.refs_0_), channel_id=1, source_target_pairs={{0,2},{2,0},{1,3},{3,1},{4,6},{6,4},{5,7},{7,5},{8,10},{10,8},{9,1... | collective-permute-start | bytes 1769480 | tf_op jit(solution)/shard_map/ppermute | solution.py:820
  333.0 14.0 %collective-permute-start.38 = (bf16[1,4,72,256]{3,2,1,0:T(8,128)(2,1)S(1)}, bf16[1,4,72,256]{3,2,1,0:T(8,128)(2,1)S(1)}, u32[]{:S(2)}, u32[]{:S(2)}) collective-permute-start(bf16[1,4,72,256]{3,2,1,0:T(8,128)(2,1)S(1)} %get-tuple-element.82), channel_id=1, source_target_pairs={{0,8},{4,12},{8,0},{12,4},{1,9},{5,13},{9,1},{13,5},{2,10},{6,14},... | collective-permute-start | bytes 442376 | tf_op jit(solution)/shard_map/ppermute | solution.py:827
  334.1 12.9 %collective-permute-start.39 = (bf16[1,4,72,256]{3,2,1,0:T(8,128)(2,1)S(1)}, bf16[1,4,72,256]{3,2,1,0:T(8,128)(2,1)S(1)}, u32[]{:S(2)}, u32[]{:S(2)}) collective-permute-start(bf16[1,4,72,256]{3,2,1,0:T(8,128)(2,1)S(1)} %get-tuple-element.83), channel_id=1, source_target_pairs={{0,4},{4,8},{8,12},{12,0},{1,5},{5,9},{9,13},{13,1},{2,6},{6,10},{... | collective-permute-start | bytes 442376 | tf_op jit(solution)/shard_map/ppermute | solution.py:827
  347.0 16.8 %collective-permute-start.40 = (bf16[4,4,72,256]{3,2,1,0:T(8,128)(2,1)S(1)}, bf16[4,4,72,256]{3,2,1,0:T(8,128)(2,1)S(1)}, u32[]{:S(2)}, u32[]{:S(2)}) collective-permute-start(bf16[4,4,72,256]{3,2,1,0:T(8,128)(2,1)S(1)} %constant_dynamic-update-slice_fusion.12.refs_0_), channel_id=1, source_target_pairs={{0,2},{2,0},{1,3},{3,1},{4,6},{6,4},{5,7},{7,5},{8,10},{10,8},{9,1... | collective-permute-start | bytes 1769480 | tf_op jit(solution)/shard_map/ppermute | solution.py:820
  365.3 19.4 %collective-permute-start.41 = (bf16[4,240,640]{2,1,0:T(8,128)(2,1)S(1)}, bf16[4,240,640]{2,1,0:T(8,128)(2,1)S(1)}, u32[]{:S(2)}, u32[]{:S(2)}) collective-permute-start(bf16[4,240,640]{2,1,0:T(8,128)(2,1)S(1)} %time_inverse.6.refs_0_), channel_id=1, source_target_pairs={{0,1},{1,0},{2,3},{3,2},{4,5},{5,4},{6,7},{7,6},{8,9},{9,8},{10,11... | collective-permute-start | bytes 3686408 | tf_op jit(solution)/shard_map/ppermute | solution.py:820
  (33 other events, 408.8 us)
